TPU v7x, 512 devices: a whole 4x4x16 slice. The times are simulated.
512 devices in a mesh: track: 8 (over y_hi, x), tm: 64 (over z, y_lo, core).
Axes of the slice: x: 4, y: 4 (y_hi: 2, y_lo: 2; y = y_hi * 2 + y_lo), z: 16, core: 2. Of those that a mesh axis runs over, the one named last changes fastest.
Arguments:
- time_query: bfloat16 [2, 4096, 8, 1024], P(None, 'tm', 'track'), may hold values from -6 to 6
- time_memory: bfloat16 [2, 4096, 8, 256], P(None, 'tm', 'track'), may hold values from -6 to 6
- time_grad_out: bfloat16 [2, 4096, 8, 1024], P(None, 'tm', 'track'), may hold values from -6 to 6
- track_query: bfloat16 [2, 4096, 8, 1024], P(None, 'tm', 'track'), may hold values from -6 to 6
- track_memory: bfloat16 [2, 4096, 8, 256], P(None, 'tm', 'track'), may hold values from -6 to 6
- track_grad_out: bfloat16 [2, 4096, 8, 1024], P(None, 'tm', 'track'), may hold values from -6 to 6
Outputs:
- time_query_grad: bfloat16 [2, 4096, 8, 1024], P(None, 'tm', 'track')
- time_memory_grad: bfloat16 [2, 4096, 8, 256], P(None, 'tm', 'track')
- track_query_grad: bfloat16 [2, 4096, 8, 1024], P(None, 'tm', 'track')
- track_memory_grad: bfloat16 [2, 4096, 8, 256], P(None, 'tm', 'track')
All inputs are finite; a program needn't handle non-finite values.
Results may differ from a plain program's by a relative error of at most 0.017.
Values may be sent and summed in bfloat16 or wider, within the bound.
No kernel may reach another device: no remote copies, remote signals or barrier semaphores. Data moves between devices by JAX's collectives and lax.ppermute only.
A program may use at most 64 MiB of HBM per device.

v0:
```python
import math

import jax
import jax.numpy as jnp
from jax import lax
from jax.sharding import PartitionSpec as P

FAR_BELOW = -1e30


def passed_along(block, axis, distance):
    devices = range(lax.axis_size(axis))
    route = [((i - distance) % len(devices), i) for i in devices]
    return lax.ppermute(block, axis, route)


def score_block(keys, queries, factor):
    return jnp.einsum("skd,srd->skr", keys, queries, preferred_element_type=jnp.float32) * factor


def group_rows(packed, head):
    songs, positions, single, doubled = packed.shape
    feature = doubled // 2
    rows = positions * (feature // head)
    queries = packed[..., :feature].reshape(songs, rows, head)
    grads_out = packed[..., feature:].reshape(songs, rows, head)
    return (queries, grads_out)


def causal_mask(start, width, positions):
    return ((start + lax.iota(jnp.int32, width))[:, None] <= positions[None, :])[None]


def softmax_stats(memory, queries, grads_out, positions, last_position, head, scale):
    songs, rows, single = queries.shape
    length = memory.shape[1]
    width = math.gcd(length, 512)

    def visit(index, state):
        start = index * width

        def visit_work(state):
            maximum, total, weighted = state
            block = lax.dynamic_slice_in_dim(memory, start, width, 1).reshape(
                songs, width, 2 * head
            )
            mask = causal_mask(start, width, positions)
            scores = jnp.where(mask, score_block(block[..., :head], queries, scale), FAR_BELOW)
            raised = jnp.maximum(maximum, jnp.max(scores, axis=1))
            weights = jnp.where(mask, jnp.exp(scores - raised[:, None, :]), 0.0)
            products = score_block(block[..., head:], grads_out, 1.0)
            fade = jnp.exp(maximum - raised)
            return (
                raised,
                total * fade + jnp.sum(weights, axis=1),
                weighted * fade + jnp.sum(weights * products, axis=1),
            )

        return lax.cond(start <= last_position, visit_work, lambda state: state, state)

    zeros = jnp.zeros((songs, rows), jnp.float32)
    maximum, total, weighted = lax.fori_loop(
        0, length // width, visit, (zeros + FAR_BELOW, zeros, zeros)
    )
    return (maximum + jnp.log(total), weighted / total)


def block_update(memory, prepared, start, width, head, scale, accum, query_grad):
    queries, grads_out, positions, last_position, log_total, delta = prepared
    songs = queries.shape[0]
    block = lax.dynamic_slice_in_dim(memory, start, width, 1).reshape(songs, width, 2 * head)
    keys = block[..., :head]
    values = block[..., head:]
    mask = causal_mask(start, width, positions)
    scores = jnp.where(mask, score_block(keys, queries, scale), FAR_BELOW)
    weights = jnp.where(mask, jnp.exp(scores - log_total[:, None, :]), 0.0)
    products = score_block(values, grads_out, 1.0)
    slopes = weights * (products - delta[:, None, :])
    weights_half = weights.astype(jnp.bfloat16)
    slopes_half = slopes.astype(jnp.bfloat16)
    key_grad = (
        jnp.einsum("skr,srd->skd", slopes_half, queries, preferred_element_type=jnp.float32) * scale
    )
    value_grad = jnp.einsum(
        "skr,srd->skd", weights_half, grads_out, preferred_element_type=jnp.float32
    )
    accum = accum + jnp.concatenate([key_grad, value_grad], axis=2)
    query_grad = query_grad + jnp.einsum(
        "skr,skd->srd", slopes_half, keys, preferred_element_type=jnp.float32
    )
    return (accum, query_grad)


def track_core(queries, grads_out, memory, head, scale):
    keys = memory[..., :head]
    values = memory[..., head:]
    scores = (
        jnp.einsum("spqhd,sptd->spqht", queries, keys, preferred_element_type=jnp.float32) * scale
    )
    top = jnp.max(scores, axis=-1, keepdims=True)
    log_total = top + jnp.log(jnp.sum(jnp.exp(scores - top), axis=-1, keepdims=True))
    weights = jnp.exp(scores - log_total)
    products = jnp.einsum(
        "spqhd,sptd->spqht", grads_out, values, preferred_element_type=jnp.float32
    )
    delta = jnp.sum(weights * products, axis=-1, keepdims=True)
    slopes = weights * (products - delta)
    weights_half = weights.astype(jnp.bfloat16)
    slopes_half = slopes.astype(jnp.bfloat16)
    query_grad = (
        jnp.einsum("spqht,sptd->spqhd", slopes_half, keys, preferred_element_type=jnp.float32)
        * scale
    )
    key_grad = (
        jnp.einsum("spqht,spqhd->sptd", slopes_half, queries, preferred_element_type=jnp.float32)
        * scale
    )
    value_grad = jnp.einsum(
        "spqht,spqhd->sptd", weights_half, grads_out, preferred_element_type=jnp.float32
    )
    return (query_grad, jnp.concatenate([key_grad, value_grad], axis=-1))


def body(time_query, time_memory, time_grad_out, track_query, track_memory, track_grad_out):
    songs, pos_dev, single, feature = time_query.shape
    head = time_memory.shape[3] // 2
    heads = feature // head
    scale = head ** (-0.5)
    count = lax.axis_size("tm")
    rank = lax.axis_index("tm")
    half = songs // 2
    rows = pos_dev * heads
    everything = lax.all_gather(time_memory, "tm", axis=1, tiled=True)
    packed = jnp.concatenate([time_query, time_grad_out], axis=3)
    lower = packed[:half]
    upper = packed[half:]
    blocks = (rank, rank)
    memories = (everything[:half], everything[half:])
    prepared = []
    for index, packed_group in enumerate((lower, upper)):
        queries, grads_out = group_rows(packed_group, head)
        positions = blocks[index] * pos_dev + lax.iota(jnp.int32, rows) // heads
        last_position = blocks[index] * pos_dev + pos_dev - 1
        log_total, delta = softmax_stats(
            memories[index], queries, grads_out, positions, last_position, head, scale
        )
        prepared.append((queries, grads_out, positions, last_position, log_total, delta))

    def contribute(step, accums, query_grads):
        results = []
        for index in range(2):
            block = (rank - 1 - step) % count
            start = block * pos_dev

            def contribute_work(state, index=index, start=start):
                return block_update(
                    memories[index],
                    prepared[index],
                    start,
                    pos_dev,
                    head,
                    scale,
                    state[0],
                    state[1],
                )

            results.append(
                lax.cond(
                    start <= prepared[index][3],
                    contribute_work,
                    lambda state: state,
                    (accums[index], query_grads[index]),
                )
            )
        return ((results[0][0], results[1][0]), (results[0][1], results[1][1]))

    def cycle_step(step, state):
        accums, query_grads = contribute(step, state[:2], state[2:])
        joined = passed_along(jnp.concatenate(accums, axis=0), "tm", 1)
        accums = (joined[:half], joined[half:])
        return accums + query_grads

    zero_accum = jnp.zeros((half, pos_dev, 2 * head), jnp.float32)
    zero_grad = jnp.zeros((half, rows, head), jnp.float32)
    state = lax.fori_loop(0, count - 1, cycle_step, (zero_accum, zero_accum, zero_grad, zero_grad))
    accums, query_grads = contribute(count - 1, state[:2], state[2:])
    time_memory_grad = (
        jnp.concatenate(accums, axis=0).reshape(songs, pos_dev, 1, 2 * head).astype(jnp.bfloat16)
    )
    lower_grad = (query_grads[0] * scale).reshape(half, pos_dev, 1, feature).astype(jnp.bfloat16)
    upper_grad = (query_grads[1] * scale).reshape(half, pos_dev, 1, feature).astype(jnp.bfloat16)
    time_query_grad = jnp.concatenate([lower_grad, upper_grad], axis=0)
    track_heads = track_query.shape[3] // head
    track_everything = lax.all_gather(track_memory, "track", axis=2, tiled=True)
    shaped = (songs, pos_dev, 1, track_heads, head)
    track_grad, partial_value = track_core(
        track_query.reshape(shaped), track_grad_out.reshape(shaped), track_everything, head, scale
    )
    track_query_grad = track_grad.astype(jnp.bfloat16).reshape(
        songs, pos_dev, 1, track_heads * head
    )
    track_memory_grad = lax.psum_scatter(
        partial_value.astype(jnp.bfloat16), "track", scatter_dimension=2, tiled=True
    )
    return (time_query_grad, time_memory_grad, track_query_grad, track_memory_grad)


def solution(mesh):
    placed = (
        P(None, "tm", "track", None),
        P(None, "tm", "track", None),
        P(None, "tm", "track", None),
        P(None, "tm", "track", None),
        P(None, "tm", "track", None),
        P(None, "tm", "track", None),
    )
    return jax.shard_map(
        body,
        mesh=mesh,
        in_specs=placed,
        out_specs=(
            P(None, "tm", "track", None),
            P(None, "tm", "track", None),
            P(None, "tm", "track", None),
            P(None, "tm", "track", None),
        ),
        check_vma=False,
    )
```

profile of v0, /device:TPU:384, one launch (start us, length us, event | category | flops | bytes accessed | tf_op | source)
XLA Modules:
  0.0 841.9 jit_solution(14456056682718855901)
XLA Ops:
  10.8 35.9 %all_gather.7 = bf16[2,64,8,256]{3,1,0,2:T(8,128)(2,1)S(1)} all-gather(bf16[2,64,1,256]{3,1,0,2:T(8,128)(2,1)} %bitcast.266), channel_id=1, replica_groups=mesh['track'=8,'tm'=64] {'track'}, dimensions={2}, use_global_device_ids=true | all-gather | bytes 589824 | tf_op jit(solution)/shard_map/all_gather | solution.py:194
  51.7 80.8 %all-gather.2.cloned.1.call-done = bf16[2,4096,1,256]{3,1,2,0:T(8,128)(2,1)} async-done(((bf16[2,64,1,256]{3,1,2,0:T(8,128)(2,1)}), bf16[2,4096,1,256]{3,1,2,0:T(8,128)(2,1)}) %all-gather.2.cloned.1.call-update) | async-done | bytes 4194320 | tf_op jit(solution)/shard_map/all_gather | solution.py:133
  136.4 14.4 %while.60 = (s32[]{:T(128)}, f32[1,512]{1,0:T(1,128)S(1)}, f32[1,512]{1,0:T(1,128)S(1)}, f32[1,512]{1,0:T(1,128)S(1)}, s32[]{:T(128)}, /*index=5*/bf16[1,4096,1,...) while((s32[]{:T(128)}, f32[1,512]{1,0:T(1,128)S(1)}, ...), condition=%wide.region_6.7_spmd.clone, body=%wide.region_0.6_spmd.clone.sunk | while | flops 137632256 | bytes 4260185 | solution.py:62
  150.9 7.8 while.61
  158.8 670.0 %while.62 = (s32[]{:T(128)}, f32[1,64,256]{2,1,0:T(8,128)S(1)}, f32[1,64,256]{2,1,0:T(8,128)S(1)}, f32[1,512,128]{2,1,0:T(8,128)S(1)}, f32[1,512,128]{2,1,0:T(8,...) while((s32[]{:T(128)}, f32[1,64,256]{2,1,0:T(8,128)S(1)}, ...), condition=%wide.region_19.20_spmd.clone, body=%wide.region_14.19_spmd.clone.sunk | while | flops 84726424 | bytes 5095608 | solution.py:185
  174.9 6.5 collective-permute-done
  186.2 6.5 collective-permute-done
  197.5 6.5 collective-permute-done
  208.8 6.5 collective-permute-done
  220.1 6.5 collective-permute-done
  231.4 6.5 collective-permute-done
  242.6 6.5 collective-permute-done
  253.9 6.5 collective-permute-done
  265.2 6.5 collective-permute-done
  276.5 6.5 collective-permute-done
  287.8 6.5 collective-permute-done
  299.1 6.5 collective-permute-done
  310.4 6.5 collective-permute-done
  321.7 6.5 collective-permute-done
  333.0 6.5 collective-permute-done
  344.3 6.5 collective-permute-done
  355.6 6.5 collective-permute-done
  366.9 6.5 collective-permute-done
  378.2 6.5 collective-permute-done
  389.4 6.5 collective-permute-done
  400.7 6.5 collective-permute-done
  412.0 6.5 collective-permute-done
  423.3 6.5 collective-permute-done
  434.6 6.5 collective-permute-done
  445.9 6.5 collective-permute-done
  457.2 6.5 collective-permute-done
  468.5 6.5 collective-permute-done
  479.8 6.5 collective-permute-done
  491.1 6.5 collective-permute-done
  502.4 6.5 collective-permute-done
  513.7 6.5 collective-permute-done
  525.0 6.5 collective-permute-done
  536.3 6.5 collective-permute-done
  547.5 6.5 collective-permute-done
  558.8 6.5 collective-permute-done
  570.1 6.5 collective-permute-done
  581.4 6.5 collective-permute-done
  592.7 6.5 collective-permute-done
  604.0 6.5 collective-permute-done
  615.3 6.5 collective-permute-done
  626.6 6.5 collective-permute-done
  637.9 6.5 collective-permute-done
  649.2 6.5 collective-permute-done
  660.5 6.5 collective-permute-done
  671.8 6.5 collective-permute-done
  683.1 6.5 collective-permute-done
  694.4 6.5 collective-permute-done
  702.9 6.5 collective-permute-done
  711.4 6.5 collective-permute-done
  719.9 6.5 collective-permute-done
  728.5 6.5 collective-permute-done
  745.5 6.5 collective-permute-done
  754.0 6.5 collective-permute-done
  762.6 6.5 collective-permute-done
  779.6 6.5 collective-permute-done
  788.2 6.5 collective-permute-done
  796.7 6.5 collective-permute-done
  813.7 6.5 collective-permute-done
  822.3 6.5 collective-permute-done
  (1376 shorter events, 475.0 us)
Async XLA Ops:
  8.0 124.6 %all-gather.2.cloned.1.call-start = ((), (), s32[]{:S(2)}) async-start(), calls=%async_computation.1 | async-start | bytes 4259840 | tf_op jit(solution)/shard_map/all_gather | solution.py:133
  8.7 825.8 %reduce-scatter.2.cloned.1.call-start = ((), (), s32[]{:S(2)}) async-start(), calls=%async_computation.2 | async-start | bytes 589824 | tf_op jit(solution)/shard_map/reduce_scatter | solution.py:202
  161.7 8.4 collective-permute-start
  173.0 8.4 collective-permute-start
  184.3 8.4 collective-permute-start
  195.5 8.4 collective-permute-start
  206.8 8.4 collective-permute-start
  218.1 8.4 collective-permute-start
  229.4 8.4 collective-permute-start
  240.7 8.4 collective-permute-start
  252.0 8.4 collective-permute-start
  263.3 8.4 collective-permute-start
  274.6 8.4 collective-permute-start
  285.9 8.4 collective-permute-start
  297.2 8.4 collective-permute-start
  308.5 8.4 collective-permute-start
  319.8 8.4 collective-permute-start
  331.1 8.4 collective-permute-start
  342.4 8.4 collective-permute-start
  353.6 8.4 collective-permute-start
  364.9 8.4 collective-permute-start
  376.2 8.4 collective-permute-start
  387.5 8.4 collective-permute-start
  398.8 8.4 collective-permute-start
  410.1 8.4 collective-permute-start
  421.4 8.4 collective-permute-start
  432.7 8.4 collective-permute-start
  444.0 8.4 collective-permute-start
  455.3 8.4 collective-permute-start
  466.6 8.4 collective-permute-start
  477.9 8.4 collective-permute-start
  489.2 8.4 collective-permute-start
  500.4 8.4 collective-permute-start
  511.7 8.4 collective-permute-start
  523.0 8.4 collective-permute-start
  534.3 8.4 collective-permute-start
  545.6 8.4 collective-permute-start
  556.9 8.4 collective-permute-start
  568.2 8.4 collective-permute-start
  579.5 8.4 collective-permute-start
  590.8 8.4 collective-permute-start
  602.1 8.4 collective-permute-start
  613.4 8.4 collective-permute-start
  624.7 8.4 collective-permute-start
  636.0 8.4 collective-permute-start
  647.3 8.4 collective-permute-start
  658.5 8.4 collective-permute-start
  669.8 8.4 collective-permute-start
  681.1 8.4 collective-permute-start
  692.4 8.4 collective-permute-start
  701.0 8.4 collective-permute-start
  709.5 8.4 collective-permute-start
  718.0 8.4 collective-permute-start
  726.5 8.4 collective-permute-start
  735.1 8.4 collective-permute-start
  743.6 8.4 collective-permute-start
  752.1 8.4 collective-permute-start
  760.6 8.4 collective-permute-start
  769.2 8.4 collective-permute-start
  777.7 8.4 collective-permute-start
  786.2 8.4 collective-permute-start
  794.8 8.4 collective-permute-start
  811.8 8.4 collective-permute-start
  820.3 8.4 collective-permute-start
  (3 other events, 12.8 us)
Sparse Core Ops, SparseCore 0:
  11.0 121.5 all-gather.1
Sparse Core Ops, SparseCore 1:
  49.7 85.3 reduce-scatter.1
where the time goes:
time: 849 us; the launch traced here: 842 us
  waiting for transfers between devices  489 us (58%)
  starting transfers between devices  121 us (14%)
  matrix products  102 us (12%)
  local copies, waits for them, and re-layouts  55.3 us (7%)
  blocking collectives  35.9 us (4%)
  between operations  15.8 us (2%)
  loops' own time  12.8 us (2%)
  other arithmetic  9.84 us (1%)
    ppermute x63, waiting for transfers between devices, passed_along(): return lax.ppermute(block, axis, route)  407 us
    ppermute x63, starting transfers between devices, passed_along(): return lax.ppermute(block, axis, route)  121 us
    all_gather x1, waiting for transfers between devices, body(): everything = lax.all_gather(time_memory, 'tm', axis=1, tiled=True)  80.8 us
    dot_general x224, matrix products, score_block(): jnp.einsum('skd,srd->skr', keys, queries, preferred_element_type=jnp.floa...  47.2 us
    reshape x98, local copies, waits for them, and re-layouts, block_update(): lax.dynamic_slice_in_dim(memory, start, width, 1)  39.5 us
    all_gather x1, blocking collectives, body(): track_everything = lax.all_gather(track_memory, 'track', axis=2, tiled=True)  35.9 us
    dot_general x98, matrix products, block_update(): jnp.einsum('skr,skd->srd', slopes_half, keys, preferred_element_type=jnp....  22.4 us
  transfers between devices with their start and end apart: 65, of which 64 were waited for; matrix products, arithmetic and copies ran while one was open for 20% of the time, Pallas kernels for 0%

commit v1 on v0

v1 whole, which is shorter than its diff:
```python
import functools
import math

import jax
import jax.numpy as jnp
from jax import lax
from jax.experimental import pallas as pl
from jax.experimental.pallas import tpu as pltpu
from jax.sharding import Mesh, PartitionSpec as P

FAR_BELOW = -1e30
LOG2E = math.log2(math.e)
NT = (((1,), (1,)), ((), ()))
NN = (((1,), (0,)), ((), ()))
TN = (((0,), (0,)), ((), ()))
VMEM = pl.BlockSpec(memory_space=pltpu.VMEM)
SMEM = pl.BlockSpec(memory_space=pltpu.SMEM)
PARAMS = pltpu.CompilerParams(vmem_limit_bytes=48 * 1024 * 1024)


def dot(a, b, dims):
    return lax.dot_general(a, b, dims, preferred_element_type=jnp.float32)


def swapped(block, axis):
    return lax.ppermute(block, axis, [(0, 1), (1, 0)])


def fill_mask(info, mask, block, groups):
    low, side, core = info[1], info[2], info[3]
    half = block // 2

    def place(index):
        return lax.rem(index + core * half, block)

    key = lax.broadcasted_iota(jnp.int32, (block, block), 0)
    row = lax.broadcasted_iota(jnp.int32, (block, block), 1)
    causal = jnp.where(place(key) <= place(row), 0.0, FAR_BELOW)
    for g in range(groups):
        before = jnp.where(g < low, 0.0, FAR_BELOW)
        at = g == low
        own = jnp.where(at, causal, before)
        other = jnp.where(jnp.logical_and(at, side == 0), 0.0, before)
        mask[g * block : (g + 1) * block, :block] = own
        mask[g * block : (g + 1) * block, block:] = jnp.broadcast_to(other, (block, block))


def group_of(memory, index, head, part):
    pieces = [memory[g, index, :, part * head : (part + 1) * head] for g in range(memory.shape[0])]
    return jnp.concatenate(pieces, axis=0)


def head_rows(own, other, column, head):
    cut = slice(column * head, (column + 1) * head)
    return jnp.concatenate([own[:, cut], other[:, cut]], axis=0)


def stats_kernel(heads, head, factor, info, own, other, memory, out, mask, most, total, weighted):
    groups, _, block, _ = memory.shape
    fill_mask(info, mask, block, groups)
    most[...] = jnp.full(most.shape, FAR_BELOW, jnp.float32)
    total[...] = jnp.zeros(total.shape, jnp.float32)
    weighted[...] = jnp.zeros(weighted.shape, jnp.float32)

    def visit(index, masked):
        keys = group_of(memory, index, head, 0)
        values = group_of(memory, index, head, 1)
        for h in range(heads):
            scores = dot(keys, head_rows(own, other, h, head), NT)
            products = dot(values, head_rows(own, other, heads + h, head), NT)
            if masked:
                scores = scores + mask[...]
            rows = scores.shape[1]
            scores = scores.reshape(-1, 8, rows)
            products = products.reshape(-1, 8, rows)
            raised = jnp.maximum(most[h], jnp.max(scores, axis=0))
            fade = jnp.exp2((most[h] - raised) * factor)
            weights = jnp.exp2((scores - raised[None]) * factor)
            most[h] = raised
            total[h] = total[h] * fade + jnp.sum(weights, axis=0)
            weighted[h] = weighted[h] * fade + jnp.sum(weights * products, axis=0)

    visit(0, True)

    @pl.loop(1, info[0] + 1)
    def _(index):
        visit(index, False)

    for h in range(heads):
        top = jnp.max(most[h], axis=0, keepdims=True)
        fade = jnp.exp2((most[h] - top) * factor)
        out[0, h : h + 1] = top
        out[1, h : h + 1] = jnp.sum(total[h] * fade, axis=0, keepdims=True)
        out[2, h : h + 1] = jnp.sum(weighted[h] * fade, axis=0, keepdims=True)


def grads_kernel(
    heads, head, scale, info, own, other, memory, mine, theirs,
    own_grad, other_grad, memory_grad,
    mask, queries, grads, weights_half, slopes_half, query_grad, shift, delta,
):
    groups, _, block, _ = memory.shape
    rows = 2 * block
    factor = scale * LOG2E
    fill_mask(info, mask, block, groups)

    def turned(stat):
        return jnp.concatenate([theirs[stat, :, block:], theirs[stat, :, :block]], axis=1)

    most = [mine[0], turned(0)]
    top = jnp.maximum(most[0], most[1])
    fades = [jnp.exp2((m - top) * factor) for m in most]
    total = mine[1] * fades[0] + turned(1) * fades[1]
    weighted = mine[2] * fades[0] + turned(2) * fades[1]
    shift[...] = top * factor + jnp.log(total) * LOG2E
    delta[...] = weighted / total
    for h in range(heads):
        queries[h * rows : (h + 1) * rows] = head_rows(own, other, h, head)
        grads[h * rows : (h + 1) * rows] = head_rows(own, other, heads + h, head)
    query_grad[...] = jnp.zeros(query_grad.shape, jnp.float32)

    def visit(index, masked):
        keys = group_of(memory, index, head, 0)
        values = group_of(memory, index, head, 1)
        for h in range(heads):
            cut = slice(h * rows, (h + 1) * rows)
            scores = dot(keys, queries[cut], NT)
            products = dot(values, grads[cut], NT)
            if masked:
                scores = scores + mask[...]
            weights = jnp.exp2(scores * factor - shift[h : h + 1])
            slopes = weights * (products - delta[h : h + 1])
            weights_half[:, cut] = weights.astype(jnp.bfloat16)
            slopes_half[:, cut] = slopes.astype(jnp.bfloat16)
        value_grad = dot(weights_half[...], grads[...], NN).astype(jnp.bfloat16)
        key_grad = (dot(slopes_half[...], queries[...], NN) * scale).astype(jnp.bfloat16)
        for g in range(groups):
            cut = slice(g * block, (g + 1) * block)
            memory_grad[g, index, :, :head] = key_grad[cut]
            memory_grad[g, index, :, head:] = value_grad[cut]
        query_grad[...] += dot(keys, slopes_half[...], TN)

    visit(0, True)

    @pl.loop(1, info[0] + 1)
    def _(index):
        visit(index, False)

    for h in range(heads):
        piece = query_grad[:, h * rows : (h + 1) * rows].T * scale
        own_grad[:, h * head : (h + 1) * head] = piece[:block]
        other_grad[:, h * head : (h + 1) * head] = piece[block:].astype(jnp.bfloat16)


def track_kernel(heads, head, scale, span, queries, grads, memory, query_grad, memory_grad):
    tracks, positions, _ = memory.shape
    factor = scale * LOG2E
    key_place = lax.rem(lax.broadcasted_iota(jnp.int32, (tracks * span, heads * span), 0), span)
    row_place = lax.rem(lax.broadcasted_iota(jnp.int32, (tracks * span, heads * span), 1), span)
    mask = jnp.where(key_place == row_place, 0.0, FAR_BELOW)
    for begin in range(0, positions, span):
        at = slice(begin, begin + span)
        rows = jnp.concatenate([queries[at, h * head : (h + 1) * head] for h in range(heads)], axis=0)
        out_rows = jnp.concatenate([grads[at, h * head : (h + 1) * head] for h in range(heads)], axis=0)
        keys = jnp.concatenate([memory[t, at, :head] for t in range(tracks)], axis=0)
        values = jnp.concatenate([memory[t, at, head:] for t in range(tracks)], axis=0)
        scores = dot(keys, rows, NT) + mask
        products = dot(values, out_rows, NT)
        top = jnp.max(scores, axis=0, keepdims=True)
        raw = jnp.exp2((scores - top) * factor)
        inverse = 1.0 / jnp.sum(raw, axis=0, keepdims=True)
        weights = raw * inverse
        delta = jnp.sum(weights * products, axis=0, keepdims=True)
        slopes = weights * (products - delta)
        weights_half = weights.astype(jnp.bfloat16)
        slopes_half = slopes.astype(jnp.bfloat16)
        value_grad = dot(weights_half, out_rows, NN).astype(jnp.bfloat16)
        key_grad = (dot(slopes_half, rows, NN) * scale).astype(jnp.bfloat16)
        row_grad = (dot(keys, slopes_half, TN).T * scale).astype(jnp.bfloat16)
        for t in range(tracks):
            cut = slice(t * span, (t + 1) * span)
            memory_grad[t, at, :head] = key_grad[cut]
            memory_grad[t, at, head:] = value_grad[cut]
        for h in range(heads):
            query_grad[at, h * head : (h + 1) * head] = row_grad[h * span : (h + 1) * span]


def body(time_query, time_memory, time_grad_out, track_query, track_memory, track_grad_out):
    songs, pos_dev, _, feature = time_query.shape
    head = time_memory.shape[3] // 2
    heads = feature // head
    scale = head ** (-0.5)
    block = 2 * pos_dev
    rows = 2 * block
    core = lax.axis_index("core")
    side = lax.axis_index("side")
    low = lax.axis_index("low")
    high = lax.axis_index("high")
    n_low = lax.axis_size("low")
    n_high = lax.axis_size("high")
    tracks = lax.axis_size("track")
    info = jnp.stack([high, low, side, core]).astype(jnp.int32)

    def of_song(array, index):
        return lax.dynamic_index_in_dim(array, index, 0, keepdims=False)

    memory = time_memory[:, :, 0]
    with jax.named_scope("memory_songs"):
        memory = jnp.concatenate(
            [of_song(memory, core), swapped(of_song(memory, 1 - core), "core")], axis=0
        )
    with jax.named_scope("memory_high"):
        held = [memory]
        for s in range(1, n_high):
            held.append(lax.ppermute(memory, "high", [(i, i + s) for i in range(n_high - s)]))
        held = jnp.stack(held)
    with jax.named_scope("memory_low"):
        held = lax.all_to_all(
            jnp.broadcast_to(held[None], (n_low, *held.shape)), "low", 0, 0, tiled=True
        )
    with jax.named_scope("query_songs"):
        packed = jnp.concatenate([time_query[:, :, 0], time_grad_out[:, :, 0]], axis=2)
        own = jnp.concatenate(
            [of_song(packed, core), swapped(of_song(packed, 1 - core), "core")], axis=0
        )
    with jax.named_scope("query_sides"):
        other = swapped(own, "side")

    with jax.named_scope("track_gather"):
        track_blocks = track_memory.reshape(1, block, 2 * head)
        everything = lax.all_to_all(
            jnp.broadcast_to(track_blocks, (tracks, block, 2 * head)), "track", 0, 0, tiled=True
        )
    track_query_grad, track_partial = pl.pallas_call(
        functools.partial(track_kernel, heads, head, scale, 32),
        out_shape=(
            jax.ShapeDtypeStruct((block, feature), jnp.bfloat16),
            jax.ShapeDtypeStruct((tracks, block, 2 * head), jnp.bfloat16),
        ),
        in_specs=[VMEM] * 3,
        out_specs=(VMEM, VMEM),
        compiler_params=PARAMS,
        name="track_core",
    )(track_query.reshape(block, feature), track_grad_out.reshape(block, feature), everything)

    mine = pl.pallas_call(
        functools.partial(stats_kernel, heads, head, scale * LOG2E),
        out_shape=jax.ShapeDtypeStruct((3, heads, rows), jnp.float32),
        in_specs=[SMEM] + [VMEM] * 3,
        out_specs=VMEM,
        scratch_shapes=[pltpu.VMEM((n_low * block, rows), jnp.float32)]
        + [pltpu.VMEM((heads, 8, rows), jnp.float32)] * 3,
        compiler_params=PARAMS,
        name="time_stats",
    )(info, own, other, held)
    with jax.named_scope("stats_sides"):
        theirs = swapped(mine, "side")
    own_grad, other_grad, memory_grad = pl.pallas_call(
        functools.partial(grads_kernel, heads, head, scale),
        out_shape=(
            jax.ShapeDtypeStruct((block, feature), jnp.float32),
            jax.ShapeDtypeStruct((block, feature), jnp.bfloat16),
            jax.ShapeDtypeStruct((n_low, n_high, block, 2 * head), jnp.bfloat16),
        ),
        in_specs=[SMEM] + [VMEM] * 5,
        out_specs=(VMEM, VMEM, VMEM),
        scratch_shapes=[
            pltpu.VMEM((n_low * block, rows), jnp.float32),
            pltpu.VMEM((heads * rows, head), jnp.bfloat16),
            pltpu.VMEM((heads * rows, head), jnp.bfloat16),
            pltpu.VMEM((n_low * block, heads * rows), jnp.bfloat16),
            pltpu.VMEM((n_low * block, heads * rows), jnp.bfloat16),
            pltpu.VMEM((head, heads * rows), jnp.float32),
            pltpu.VMEM((heads, rows), jnp.float32),
            pltpu.VMEM((heads, rows), jnp.float32),
        ],
        compiler_params=PARAMS,
        name="time_grads",
    )(info, own, other, held, mine, theirs)

    with jax.named_scope("memory_grad_low"):
        parts = lax.all_to_all(memory_grad, "low", 0, 0, tiled=True)
        sums = jnp.sum(parts.astype(jnp.float32), axis=0)
    with jax.named_scope("memory_grad_high"):
        gathered = sums[0]
        for s in range(1, n_high):
            back = lax.ppermute(
                sums[s].astype(jnp.bfloat16), "high", [(i + s, i) for i in range(n_high - s)]
            )
            gathered = gathered + back.astype(jnp.float32)
        gathered = gathered.astype(jnp.bfloat16)

    def to_songs(array):
        ours = array[:pos_dev]
        back = swapped(array[pos_dev:], "core")
        first = jnp.where(core == 0, ours, back)
        second = jnp.where(core == 0, back, ours)
        return jnp.stack([first, second])[:, :, None, :]

    with jax.named_scope("memory_grad_songs"):
        time_memory_grad = to_songs(gathered)
    with jax.named_scope("query_grad_sides"):
        query_grad = own_grad + swapped(other_grad, "side").astype(jnp.float32)
    with jax.named_scope("query_grad_songs"):
        time_query_grad = to_songs(query_grad.astype(jnp.bfloat16))
    with jax.named_scope("track_scatter"):
        track_parts = lax.all_to_all(track_partial, "track", 0, 0, tiled=True)
        track_memory_grad = jnp.sum(track_parts.astype(jnp.float32), axis=0).astype(jnp.bfloat16)
    return (
        time_query_grad,
        time_memory_grad,
        track_query_grad.reshape(track_query.shape),
        track_memory_grad.reshape(track_memory.shape),
    )


def solution(mesh):
    tracks, times = mesh.devices.shape
    chips = times // 4
    high = next(n for n in (4, 2, 1) if chips % n == 0)
    axes = ("track", "high", "low", "side", "core")
    finer = Mesh(mesh.devices.reshape(tracks, high, chips // high, 2, 2), axes)
    placed = P(None, axes[1:], "track", None)
    return jax.shard_map(
        body,
        mesh=finer,
        in_specs=(placed,) * 6,
        out_specs=(placed,) * 4,
        check_vma=False,
    )
```

time: 849 us -> 153 us (0.18)
  the two profiles are of different devices: /device:TPU:384 before, /device:TPU:99 now
where the time goes in v1:
time: 153 us; the launch traced here: 152 us
  starting transfers between devices  82 us (54%)
  waiting for transfers between devices  54.6 us (36%)
  Pallas kernels  9.32 us (6%)
  local copies, waits for them, and re-layouts  2.89 us (2%)
  other arithmetic  2.58 us (2%)
    ppermute x7, starting transfers between devices, swapped(): return lax.ppermute(block, axis, [(0, 1), (1, 0)])  28.9 us
    ppermute x3, waiting for transfers between devices, body(): lax.ppermute(sums[s].astype(jnp.bfloat16), 'high', [(i + s, i) for i in r...  20 us
    ppermute x3, starting transfers between devices, body(): lax.ppermute(memory, 'high', [(i, i + s) for i in range(n_high - s)])  18 us
    all_to_all x1, waiting for transfers between devices, body(): lax.all_to_all(jnp.broadcast_to(held[None], (n_low, *held.shape)), 'low',...  13.9 us
    all_to_all x1, starting transfers between devices, body(): lax.all_to_all(jnp.broadcast_to(held[None], (n_low, *held.shape)), 'low',...  11.9 us
    ppermute x7, waiting for transfers between devices, swapped(): return lax.ppermute(block, axis, [(0, 1), (1, 0)])  8.93 us
    all_to_all x1, waiting for transfers between devices, body(): parts = lax.all_to_all(memory_grad, 'low', 0, 0, tiled=True)  8.71 us
    all_to_all x1, starting transfers between devices, body(): lax.all_to_all(jnp.broadcast_to(track_blocks, (tracks, block, 2 * head)),...  6.9 us
  transfers between devices with their start and end apart: 17, of which 11 were waited for; matrix products, arithmetic and copies ran while one was open for 1% of the time, Pallas kernels for 6%

profile of v1, /device:TPU:99, one launch (start us, length us, event | category | flops | bytes accessed | tf_op | source)
XLA Modules:
  0.0 152.3 jit_solution(7818835715358633915)
XLA Ops:
  0.6 0.0 copy-start.4
  0.6 1.7 %broadcast_in_dim.23 = bf16[8,128,256]{2,1,0:T(8,128)(2,1)} broadcast(bf16[128,256]{1,0:T(8,128)(2,1)} %bitcast.60), dimensions={1,2} | broadcast | bytes 589824 | tf_op jit(solution)/shard_map/track_gather/broadcast_in_dim | solution.py:232
  2.4 6.9 %all-to-all-start.2 = ((bf16[8,128,256]{2,1,0:T(8,128)(2,1)}), bf16[8,128,256]{2,1,0:T(8,128)(2,1)S(1)}, u32[]{:S(2)}, u32[]{:S(2)}) async-start(bf16[8,128,256]{2,1,0:T(8,128)(2,1)} %broadcast_in_dim.23), calls=%async_computation.2 | async-start | bytes 1048576 | tf_op jit(solution)/shard_map/track_gather/all_to_all | solution.py:231
  9.3 0.0 copy-done.4
  9.3 3.1 %collective-permute-start.2 = (bf16[64,256]{1,0:T(8,128)(2,1)S(1)}, bf16[64,256]{1,0:T(8,128)(2,1)S(1)}, u32[]{:S(2)}, u32[]{:S(2)}) collective-permute-start(bf16[64,256]{1,0:T(8,128)(2,1)S(1)} %get-tuple-element.30), channel_id=1, source_target_pairs={{0,1},{1,0},{2,3},{3,2},{4,5},{5,4},{6,7},{7,6},{8,9},{9,8},{10,11... | collective-permute-start | bytes 98312 | tf_op jit(solution)/shard_map/memory_songs/ppermute | solution.py:26
  12.4 0.8 collective-permute-done.2
  13.3 8.8 %collective-permute-start.3 = (bf16[128,256]{1,0:T(8,128)(2,1)S(1)}, bf16[128,256]{1,0:T(8,128)(2,1)S(1)}, u32[]{:S(2)}, u32[]{:S(2)}) collective-permute-start(bf16[128,256]{1,0:T(8,128)(2,1)S(1)} %get-tuple-element.28), channel_id=1, source_target_pairs={{0,16},{16,32},{32,48},{1,17},{17,33},{33,49},{2,18},{18,34},{34,5... | collective-permute-start | bytes 196616 | tf_op jit(solution)/shard_map/memory_high/ppermute | solution.py:215
  22.1 7.9 %collective-permute-start.4 = (bf16[128,256]{1,0:T(8,128)(2,1)S(1)}, bf16[128,256]{1,0:T(8,128)(2,1)S(1)}, u32[]{:S(2)}, u32[]{:S(2)}) collective-permute-start(bf16[128,256]{1,0:T(8,128)(2,1)S(1)} %get-tuple-element.28), channel_id=1, source_target_pairs={{0,32},{16,48},{1,33},{17,49},{2,34},{18,50},{3,35},{19,51},{4,36}... | collective-permute-start | bytes 196616 | tf_op jit(solution)/shard_map/memory_high/ppermute | solution.py:215
  30.0 1.3 collective-permute-start.5
  31.3 0.0 collective-permute-done.3
  31.4 1.6 %collective-permute-done.4 = bf16[128,256]{1,0:T(8,128)(2,1)S(1)} collective-permute-done((bf16[128,256]{1,0:T(8,128)(2,1)S(1)}, bf16[128,256]{1,0:T(8,128)(2,1)S(1)}, u32[]{:S(2)}, u32[]{:S(2)}) %collective-permute-start.4) | collective-permute-done | bytes 65568 | tf_op jit(solution)/shard_map/memory_high/ppermute | solution.py:215
  33.0 1.5 collective-permute-done.5
  34.5 0.0 all-to-all-done.2.memory
  34.5 1.1 broadcast_in_dim.19
  35.6 0.0 copy-start.2
  35.6 0.0 copy-start.3
  35.6 11.9 %all-to-all-start = ((bf16[4,4,128,256]{3,2,1,0:T(8,128)(2,1)}), bf16[4,4,128,256]{3,2,1,0:T(8,128)(2,1)S(1)}, u32[]{:S(2)}, u32[]{:S(2)}) async-start(bf16[4,4,128,256]{3,2,1,0:T(8,128)(2,1)} %broadcast_in_dim.19), calls=%async_computation | async-start | bytes 2097152 | tf_op jit(solution)/shard_map/memory_low/all_to_all | solution.py:218
  47.6 0.0 copy-done.2
  47.6 0.0 copy-done.3
  47.6 0.0 copy-start
  47.6 0.0 copy-start.1
  47.7 3.0 %collective-permute-start = (bf16[64,2048]{1,0:T(8,128)(2,1)S(1)}, bf16[64,2048]{1,0:T(8,128)(2,1)S(1)}, u32[]{:S(2)}, u32[]{:S(2)}) collective-permute-start(bf16[64,2048]{1,0:T(8,128)(2,1)S(1)} %get-tuple-element.19), channel_id=1, source_target_pairs={{0,1},{1,0},{2,3},{3,2},{4,5},{5,4},{6,7},{7,6},{8,9},{9,8},{10,11... | collective-permute-start | bytes 786440 | tf_op jit(solution)/shard_map/query_songs/ppermute | solution.py:26
  50.6 1.1 collective-permute-done
  51.8 2.3 %collective-permute-start.1 = (bf16[128,2048]{1,0:T(8,128)(2,1)S(1)}, bf16[128,2048]{1,0:T(8,128)(2,1)S(1)}, u32[]{:S(2)}, u32[]{:S(2)}) collective-permute-start(bf16[128,2048]{1,0:T(8,128)(2,1)S(1)} %pad_maximum_fusion.own), channel_id=1, source_target_pairs={{0,2},{2,0},{1,3},{3,1},{4,6},{6,4},{5,7},{7,5},{8,10},{10,8},{9,1... | collective-permute-start | bytes 1572872 | tf_op jit(solution)/shard_map/query_sides/ppermute | solution.py:26
  54.1 0.0 copy-done
  54.1 0.0 copy-done.1
  54.2 2.6 %track_core.1 = (bf16[128,1024]{1,0:T(8,128)(2,1)}, bf16[8,128,256]{2,1,0:T(8,128)(2,1)}) custom-call(bf16[128,1024]{1,0:T(8,128)(2,1)S(1)} %bitcast.56, bf16[128,1024]{1,0:T(8,128)(2,1)S(1)} %bitcast.57, bf16[8,128,256]{2,1,0:T(8,128)(2,1)S(1)} %all-to-all-done.2.memory), custom_call_target="tpu_custom_call" | custom-call | tf_op jit(solution)/shard_map/track_core/pallas_call | solution.py:234
  56.8 13.9 %all-to-all-done.memory = bf16[4,4,128,256]{3,2,1,0:T(8,128)(2,1)S(1)} async-done(((bf16[4,4,128,256]{3,2,1,0:T(8,128)(2,1)}), bf16[4,4,128,256]{3,2,1,0:T(8,128)(2,1)S(1)}, u32[]{:S(2)}, u32[]{:S(2)}) %all-to-all-start) | async-done | bytes 1048608 | tf_op jit(solution)/shard_map/memory_low/all_to_all | solution.py:218
  70.7 6.6 %all-to-all-start.3 = ((bf16[8,128,256]{2,1,0:T(8,128)(2,1)}), bf16[8,128,256]{2,1,0:T(8,128)(2,1)S(1)}, u32[]{:S(2)}, u32[]{:S(2)}) async-start(bf16[8,128,256]{2,1,0:T(8,128)(2,1)} %get-tuple-element.13), calls=%async_computation.3 | async-start | bytes 1048576 | tf_op jit(solution)/shard_map/track_scatter/all_to_all | solution.py:307
  77.3 0.1 pad_add_fusion.info
  77.4 0.0 collective-permute-done.1.other
  77.4 2.4 %time_stats.1.mine = f32[3,8,256]{2,1,0:T(8,128)S(1)} custom-call(s32[4]{0:T(128)S(1)} %pad_add_fusion.info, bf16[128,2048]{1,0:T(8,128)(2,1)S(1)} %pad_maximum_fusion.own, bf16[128,2048]{1,0:T(8,128)(2,1)S(1)} %collective-permute-done.1.other, bf16[4,4,128,256]{3,2,1,0:T(8,128)(2,1)S(1)} %all-to-all-done.memory), custom_call_target="tpu_custom_call" | custom-call | tf_op jit(solution)/shard_map/time_stats/pallas_call | solution.py:246
  79.8 2.3 %collective-permute-start.6 = (f32[3,8,256]{2,1,0:T(8,128)S(1)}, f32[3,8,256]{2,1,0:T(8,128)S(1)}, u32[]{:S(2)}, u32[]{:S(2)}) collective-permute-start(f32[3,8,256]{2,1,0:T(8,128)S(1)} %time_stats.1.mine), channel_id=1, source_target_pairs={{0,2},{2,0},{1,3},{3,1},{4,6},{6,4},{5,7},{7,5},{8,10},{10,8},{9,1... | collective-permute-start | bytes 73736 | tf_op jit(solution)/shard_map/stats_sides/ppermute | solution.py:26
  82.1 3.1 %collective-permute-done.6.theirs = f32[3,8,256]{2,1,0:T(8,128)S(1)} collective-permute-done((f32[3,8,256]{2,1,0:T(8,128)S(1)}, f32[3,8,256]{2,1,0:T(8,128)S(1)}, u32[]{:S(2)}, u32[]{:S(2)}) %collective-permute-start.6) | collective-permute-done | bytes 24608 | tf_op jit(solution)/shard_map/stats_sides/ppermute | solution.py:26
  85.2 4.3 %time_grads.1 = (f32[128,1024]{1,0:T(8,128)S(1)}, bf16[128,1024]{1,0:T(8,128)(2,1)S(1)}, bf16[4,4,128,256]{3,2,1,0:T(8,128)(2,1)}) custom-call(s32[4]{0:T(128)S(1)} %pad_add_fusion.info, bf16[128,2048]{1,0:T(8,128)(2,1)S(1)} %pad_maximum_fusion.own, bf16[128,2048]{1,0:T(8,128)(2,1)S(1)} %collective-permute-done.1.other, ...), custom_call_target="tpu_custom_call" | custom-call | tf_op jit(solution)/shard_map/time_grads/pallas_call | solution.py:258
  89.6 0.0 all-to-all-done.3
  89.6 5.7 %all-to-all-start.1 = ((bf16[4,4,128,256]{3,2,1,0:T(8,128)(2,1)}), bf16[4,4,128,256]{3,2,1,0:T(8,128)(2,1)S(1)}, u32[]{:S(2)}, u32[]{:S(2)}) async-start(bf16[4,4,128,256]{3,2,1,0:T(8,128)(2,1)} %get-tuple-element.11), calls=%async_computation.1 | async-start | bytes 2097152 | tf_op jit(solution)/shard_map/memory_grad_low/all_to_all | solution.py:282
  95.3 3.0 %collective-permute-start.7 = (bf16[128,1024]{1,0:T(8,128)(2,1)S(1)}, bf16[128,1024]{1,0:T(8,128)(2,1)S(1)}, u32[]{:S(2)}, u32[]{:S(2)}) collective-permute-start(bf16[128,1024]{1,0:T(8,128)(2,1)S(1)} %get-tuple-element.10), channel_id=1, source_target_pairs={{0,2},{2,0},{1,3},{3,1},{4,6},{6,4},{5,7},{7,5},{8,10},{10,8},{9,1... | collective-permute-start | bytes 786440 | tf_op jit(solution)/shard_map/query_grad_sides/ppermute | solution.py:26
  98.3 0.7 reduce_sum.22
  99.0 3.7 %collective-permute-done.7 = bf16[128,1024]{1,0:T(8,128)(2,1)S(1)} collective-permute-done((bf16[128,1024]{1,0:T(8,128)(2,1)S(1)}, bf16[128,1024]{1,0:T(8,128)(2,1)S(1)}, u32[]{:S(2)}, u32[]{:S(2)}) %collective-permute-start.7) | collective-permute-done | bytes 262176 | tf_op jit(solution)/shard_map/query_grad_sides/ppermute | solution.py:26
  102.7 0.1 add_convert_fusion
  102.8 5.3 %collective-permute-start.8 = (bf16[64,1024]{1,0:T(8,128)(2,1)S(1)}, bf16[64,1024]{1,0:T(8,128)(2,1)S(1)}, u32[]{:S(2)}, u32[]{:S(2)}) collective-permute-start(bf16[64,1024]{1,0:T(8,128)(2,1)S(1)} %slice.36), channel_id=1, source_target_pairs={{0,1},{1,0},{2,3},{3,2},{4,5},{5,4},{6,7},{7,6},{8,9},{9,8},{10,11... | collective-permute-start | bytes 393224 | tf_op jit(solution)/shard_map/query_grad_songs/ppermute | solution.py:26
  108.0 8.7 %all-to-all-done.1 = bf16[4,4,128,256]{3,2,1,0:T(8,128)(2,1)S(1)} async-done(((bf16[4,4,128,256]{3,2,1,0:T(8,128)(2,1)}), bf16[4,4,128,256]{3,2,1,0:T(8,128)(2,1)S(1)}, u32[]{:S(2)}, u32[]{:S(2)}) %all-to-all-start.1) | async-done | bytes 1048608 | tf_op jit(solution)/shard_map/memory_grad_low/all_to_all | solution.py:282
  116.7 0.2 convert_reduce_fusion
  117.0 1.3 collective-permute-start.10
  118.3 1.3 collective-permute-start.11
  119.6 1.3 collective-permute-start.9
  120.9 0.0 collective-permute-done.8
  120.9 13.2 %collective-permute-done.10 = bf16[128,256]{1,0:T(8,128)(2,1)S(1)} collective-permute-done((bf16[128,256]{1,0:T(8,128)(2,1)S(1)}, bf16[128,256]{1,0:T(8,128)(2,1)S(1)}, u32[]{:S(2)}, u32[]{:S(2)}) %collective-permute-start.10) | collective-permute-done | bytes 65568 | tf_op jit(solution)/shard_map/memory_grad_high/ppermute | solution.py:287
  134.1 6.7 %collective-permute-done.11 = bf16[128,256]{1,0:T(8,128)(2,1)S(1)} collective-permute-done((bf16[128,256]{1,0:T(8,128)(2,1)S(1)}, bf16[128,256]{1,0:T(8,128)(2,1)S(1)}, u32[]{:S(2)}, u32[]{:S(2)}) %collective-permute-start.11) | collective-permute-done | bytes 65568 | tf_op jit(solution)/shard_map/memory_grad_high/ppermute | solution.py:287
  140.8 0.0 collective-permute-done.9
  140.9 9.9 %collective-permute-start.12 = (bf16[64,256]{1,0:T(8,128)(2,1)S(1)}, bf16[64,256]{1,0:T(8,128)(2,1)S(1)}, u32[]{:S(2)}, u32[]{:S(2)}) collective-permute-start(bf16[64,256]{1,0:T(8,128)(2,1)S(1)} %slice.42), channel_id=1, source_target_pairs={{0,1},{1,0},{2,3},{3,2},{4,5},{5,4},{6,7},{7,6},{8,9},{9,8},{10,11... | collective-permute-start | bytes 98312 | tf_op jit(solution)/shard_map/memory_grad_songs/ppermute | solution.py:26
  150.8 0.7 maximum_bitcast_fusion
  151.6 0.1 collective-permute-done.12
  151.7 0.6 maximum_bitcast_fusion.1
  (12 shorter events, 0.3 us)
Async XLA Ops:
  0.6 8.6 %copy-start.4 = (bf16[2,64,1,256]{3,1,2,0:T(8,128)(2,1)S(1)}, bf16[2,64,1,256]{3,1,2,0:T(8,128)(2,1)}, u32[]{:S(2)}) copy-start(bf16[2,64,1,256]{3,1,2,0:T(8,128)(2,1)} %param.7) | copy-start | bytes 196612
  2.4 32.2 %all-to-all-start.2 = ((bf16[8,128,256]{2,1,0:T(8,128)(2,1)}), bf16[8,128,256]{2,1,0:T(8,128)(2,1)S(1)}, u32[]{:S(2)}, u32[]{:S(2)}) async-start(bf16[8,128,256]{2,1,0:T(8,128)(2,1)} %broadcast_in_dim.23), calls=%async_computation.2 | async-start | bytes 1048576 | tf_op jit(solution)/shard_map/track_gather/all_to_all | solution.py:231
  9.3 4.0 %collective-permute-start.2 = (bf16[64,256]{1,0:T(8,128)(2,1)S(1)}, bf16[64,256]{1,0:T(8,128)(2,1)S(1)}, u32[]{:S(2)}, u32[]{:S(2)}) collective-permute-start(bf16[64,256]{1,0:T(8,128)(2,1)S(1)} %get-tuple-element.30), channel_id=1, source_target_pairs={{0,1},{1,0},{2,3},{3,2},{4,5},{5,4},{6,7},{7,6},{8,9},{9,8},{10,11... | collective-permute-start | bytes 98312 | tf_op jit(solution)/shard_map/memory_songs/ppermute | solution.py:26
  13.3 18.1 %collective-permute-start.3 = (bf16[128,256]{1,0:T(8,128)(2,1)S(1)}, bf16[128,256]{1,0:T(8,128)(2,1)S(1)}, u32[]{:S(2)}, u32[]{:S(2)}) collective-permute-start(bf16[128,256]{1,0:T(8,128)(2,1)S(1)} %get-tuple-element.28), channel_id=1, source_target_pairs={{0,16},{16,32},{32,48},{1,17},{17,33},{33,49},{2,18},{18,34},{34,5... | collective-permute-start | bytes 196616 | tf_op jit(solution)/shard_map/memory_high/ppermute | solution.py:215
  22.1 10.9 %collective-permute-start.4 = (bf16[128,256]{1,0:T(8,128)(2,1)S(1)}, bf16[128,256]{1,0:T(8,128)(2,1)S(1)}, u32[]{:S(2)}, u32[]{:S(2)}) collective-permute-start(bf16[128,256]{1,0:T(8,128)(2,1)S(1)} %get-tuple-element.28), channel_id=1, source_target_pairs={{0,32},{16,48},{1,33},{17,49},{2,34},{18,50},{3,35},{19,51},{4,36}... | collective-permute-start | bytes 196616 | tf_op jit(solution)/shard_map/memory_high/ppermute | solution.py:215
  30.0 4.4 %collective-permute-start.5 = (bf16[128,256]{1,0:T(8,128)(2,1)S(1)}, bf16[128,256]{1,0:T(8,128)(2,1)S(1)}, u32[]{:S(2)}, u32[]{:S(2)}) collective-permute-start(bf16[128,256]{1,0:T(8,128)(2,1)S(1)} %get-tuple-element.28), channel_id=1, source_target_pairs={{0,48},{1,49},{2,50},{3,51},{4,52},{5,53},{6,54},{7,55},{8,56},{9,... | collective-permute-start | bytes 196616 | tf_op jit(solution)/shard_map/memory_high/ppermute | solution.py:215
  35.6 12.0 %copy-start.2 = (bf16[2,64,1,1024]{3,1,2,0:T(8,128)(2,1)S(1)}, bf16[2,64,1,1024]{3,1,2,0:T(8,128)(2,1)}, u32[]{:S(2)}) copy-start(bf16[2,64,1,1024]{3,1,2,0:T(8,128)(2,1)} %param.6) | copy-start | bytes 786436
  35.6 12.0 %copy-start.3 = (bf16[2,64,1,1024]{3,1,2,0:T(8,128)(2,1)S(1)}, bf16[2,64,1,1024]{3,1,2,0:T(8,128)(2,1)}, u32[]{:S(2)}) copy-start(bf16[2,64,1,1024]{3,1,2,0:T(8,128)(2,1)} %param.8) | copy-start | bytes 786436
  35.6 35.0 %all-to-all-start = ((bf16[4,4,128,256]{3,2,1,0:T(8,128)(2,1)}), bf16[4,4,128,256]{3,2,1,0:T(8,128)(2,1)S(1)}, u32[]{:S(2)}, u32[]{:S(2)}) async-start(bf16[4,4,128,256]{3,2,1,0:T(8,128)(2,1)} %broadcast_in_dim.19), calls=%async_computation | async-start | bytes 2097152 | tf_op jit(solution)/shard_map/memory_low/all_to_all | solution.py:218
  47.6 6.5 %copy-start = (bf16[2,64,1,1024]{3,1,2,0:T(8,128)(2,1)S(1)}, bf16[2,64,1,1024]{3,1,2,0:T(8,128)(2,1)}, u32[]{:S(2)}) copy-start(bf16[2,64,1,1024]{3,1,2,0:T(8,128)(2,1)} %param.9) | copy-start | bytes 786436
  47.6 6.5 %copy-start.1 = (bf16[2,64,1,1024]{3,1,2,0:T(8,128)(2,1)S(1)}, bf16[2,64,1,1024]{3,1,2,0:T(8,128)(2,1)}, u32[]{:S(2)}) copy-start(bf16[2,64,1,1024]{3,1,2,0:T(8,128)(2,1)} %param.11) | copy-start | bytes 786436
  47.7 4.1 %collective-permute-start = (bf16[64,2048]{1,0:T(8,128)(2,1)S(1)}, bf16[64,2048]{1,0:T(8,128)(2,1)S(1)}, u32[]{:S(2)}, u32[]{:S(2)}) collective-permute-start(bf16[64,2048]{1,0:T(8,128)(2,1)S(1)} %get-tuple-element.19), channel_id=1, source_target_pairs={{0,1},{1,0},{2,3},{3,2},{4,5},{5,4},{6,7},{7,6},{8,9},{9,8},{10,11... | collective-permute-start | bytes 786440 | tf_op jit(solution)/shard_map/query_songs/ppermute | solution.py:26
  51.8 25.6 %collective-permute-start.1 = (bf16[128,2048]{1,0:T(8,128)(2,1)S(1)}, bf16[128,2048]{1,0:T(8,128)(2,1)S(1)}, u32[]{:S(2)}, u32[]{:S(2)}) collective-permute-start(bf16[128,2048]{1,0:T(8,128)(2,1)S(1)} %pad_maximum_fusion.own), channel_id=1, source_target_pairs={{0,2},{2,0},{1,3},{3,1},{4,6},{6,4},{5,7},{7,5},{8,10},{10,8},{9,1... | collective-permute-start | bytes 1572872 | tf_op jit(solution)/shard_map/query_sides/ppermute | solution.py:26
  70.7 18.9 %all-to-all-start.3 = ((bf16[8,128,256]{2,1,0:T(8,128)(2,1)}), bf16[8,128,256]{2,1,0:T(8,128)(2,1)S(1)}, u32[]{:S(2)}, u32[]{:S(2)}) async-start(bf16[8,128,256]{2,1,0:T(8,128)(2,1)} %get-tuple-element.13), calls=%async_computation.3 | async-start | bytes 1048576 | tf_op jit(solution)/shard_map/track_scatter/all_to_all | solution.py:307
  79.8 5.4 %collective-permute-start.6 = (f32[3,8,256]{2,1,0:T(8,128)S(1)}, f32[3,8,256]{2,1,0:T(8,128)S(1)}, u32[]{:S(2)}, u32[]{:S(2)}) collective-permute-start(f32[3,8,256]{2,1,0:T(8,128)S(1)} %time_stats.1.mine), channel_id=1, source_target_pairs={{0,2},{2,0},{1,3},{3,1},{4,6},{6,4},{5,7},{7,5},{8,10},{10,8},{9,1... | collective-permute-start | bytes 73736 | tf_op jit(solution)/shard_map/stats_sides/ppermute | solution.py:26
  89.6 27.2 %all-to-all-start.1 = ((bf16[4,4,128,256]{3,2,1,0:T(8,128)(2,1)}), bf16[4,4,128,256]{3,2,1,0:T(8,128)(2,1)S(1)}, u32[]{:S(2)}, u32[]{:S(2)}) async-start(bf16[4,4,128,256]{3,2,1,0:T(8,128)(2,1)} %get-tuple-element.11), calls=%async_computation.1 | async-start | bytes 2097152 | tf_op jit(solution)/shard_map/memory_grad_low/all_to_all | solution.py:282
  95.3 7.4 %collective-permute-start.7 = (bf16[128,1024]{1,0:T(8,128)(2,1)S(1)}, bf16[128,1024]{1,0:T(8,128)(2,1)S(1)}, u32[]{:S(2)}, u32[]{:S(2)}) collective-permute-start(bf16[128,1024]{1,0:T(8,128)(2,1)S(1)} %get-tuple-element.10), channel_id=1, source_target_pairs={{0,2},{2,0},{1,3},{3,1},{4,6},{6,4},{5,7},{7,5},{8,10},{10,8},{9,1... | collective-permute-start | bytes 786440 | tf_op jit(solution)/shard_map/query_grad_sides/ppermute | solution.py:26
  102.8 18.1 %collective-permute-start.8 = (bf16[64,1024]{1,0:T(8,128)(2,1)S(1)}, bf16[64,1024]{1,0:T(8,128)(2,1)S(1)}, u32[]{:S(2)}, u32[]{:S(2)}) collective-permute-start(bf16[64,1024]{1,0:T(8,128)(2,1)S(1)} %slice.36), channel_id=1, source_target_pairs={{0,1},{1,0},{2,3},{3,2},{4,5},{5,4},{6,7},{7,6},{8,9},{9,8},{10,11... | collective-permute-start | bytes 393224 | tf_op jit(solution)/shard_map/query_grad_songs/ppermute | solution.py:26
  117.0 17.2 %collective-permute-start.10 = (bf16[128,256]{1,0:T(8,128)(2,1)S(1)}, bf16[128,256]{1,0:T(8,128)(2,1)S(1)}, u32[]{:S(2)}, u32[]{:S(2)}) collective-permute-start(bf16[128,256]{1,0:T(8,128)(2,1)S(1)} %get-tuple-element.24), channel_id=1, source_target_pairs={{32,0},{48,16},{33,1},{49,17},{34,2},{50,18},{35,3},{51,19},{36,4}... | collective-permute-start | bytes 196616 | tf_op jit(solution)/shard_map/memory_grad_high/ppermute | solution.py:287
  118.3 22.6 %collective-permute-start.11 = (bf16[128,256]{1,0:T(8,128)(2,1)S(1)}, bf16[128,256]{1,0:T(8,128)(2,1)S(1)}, u32[]{:S(2)}, u32[]{:S(2)}) collective-permute-start(bf16[128,256]{1,0:T(8,128)(2,1)S(1)} %get-tuple-element.23), channel_id=1, source_target_pairs={{48,0},{49,1},{50,2},{51,3},{52,4},{53,5},{54,6},{55,7},{56,8},{57... | collective-permute-start | bytes 196616 | tf_op jit(solution)/shard_map/memory_grad_high/ppermute | solution.py:287
  119.6 21.3 %collective-permute-start.9 = (bf16[128,256]{1,0:T(8,128)(2,1)S(1)}, bf16[128,256]{1,0:T(8,128)(2,1)S(1)}, u32[]{:S(2)}, u32[]{:S(2)}) collective-permute-start(bf16[128,256]{1,0:T(8,128)(2,1)S(1)} %get-tuple-element.22), channel_id=1, source_target_pairs={{16,0},{32,16},{48,32},{17,1},{33,17},{49,33},{18,2},{34,18},{50,3... | collective-permute-start | bytes 196616 | tf_op jit(solution)/shard_map/memory_grad_high/ppermute | solution.py:287
  140.9 10.8 %collective-permute-start.12 = (bf16[64,256]{1,0:T(8,128)(2,1)S(1)}, bf16[64,256]{1,0:T(8,128)(2,1)S(1)}, u32[]{:S(2)}, u32[]{:S(2)}) collective-permute-start(bf16[64,256]{1,0:T(8,128)(2,1)S(1)} %slice.42), channel_id=1, source_target_pairs={{0,1},{1,0},{2,3},{3,2},{4,5},{5,4},{6,7},{7,6},{8,9},{9,8},{10,11... | collective-permute-start | bytes 98312 | tf_op jit(solution)/shard_map/memory_grad_songs/ppermute | solution.py:26

commit v2 on v1

--- a/solution.py
+++ b/solution.py
@@ -22,6 +22,10 @@
     return lax.dot_general(a, b, dims, preferred_element_type=jnp.float32)
 
 
+def after(block, earlier):
+    return lax.optimization_barrier((block, earlier))[0]
+
+
 def swapped(block, axis):
     return lax.ppermute(block, axis, [(0, 1), (1, 0)])
 
@@ -35,7 +39,7 @@
 
     key = lax.broadcasted_iota(jnp.int32, (block, block), 0)
     row = lax.broadcasted_iota(jnp.int32, (block, block), 1)
-    causal = jnp.where(place(key) <= place(row), 0.0, FAR_BELOW)
+    causal = jnp.where(key <= place(row), 0.0, FAR_BELOW)
     for g in range(groups):
         before = jnp.where(g < low, 0.0, FAR_BELOW)
         at = g == low
@@ -56,7 +60,7 @@
 
 
 def stats_kernel(heads, head, factor, info, own, other, memory, out, mask, most, total, weighted):
-    groups, _, block, _ = memory.shape
+    groups, block = memory.shape[0] // 2, 2 * memory.shape[2]
     fill_mask(info, mask, block, groups)
     most[...] = jnp.full(most.shape, FAR_BELOW, jnp.float32)
     total[...] = jnp.zeros(total.shape, jnp.float32)
@@ -99,8 +103,8 @@
     own_grad, other_grad, memory_grad,
     mask, queries, grads, weights_half, slopes_half, query_grad, shift, delta,
 ):
-    groups, _, block, _ = memory.shape
-    rows = 2 * block
+    groups, block = memory.shape[0] // 2, 2 * memory.shape[2]
+    half, rows = block // 2, 2 * block
     factor = scale * LOG2E
     fill_mask(info, mask, block, groups)
 
@@ -134,8 +138,8 @@
             slopes_half[:, cut] = slopes.astype(jnp.bfloat16)
         value_grad = dot(weights_half[...], grads[...], NN).astype(jnp.bfloat16)
         key_grad = (dot(slopes_half[...], queries[...], NN) * scale).astype(jnp.bfloat16)
-        for g in range(groups):
-            cut = slice(g * block, (g + 1) * block)
+        for g in range(2 * groups):
+            cut = slice(g * half, (g + 1) * half)
             memory_grad[g, index, :, :head] = key_grad[cut]
             memory_grad[g, index, :, head:] = value_grad[cut]
         query_grad[...] += dot(keys, slopes_half[...], TN)
@@ -204,44 +208,43 @@
     def of_song(array, index):
         return lax.dynamic_index_in_dim(array, index, 0, keepdims=False)
 
+    def places(step):
+        pairs = []
+        for i in range(n_high - step):
+            for j in range(n_low):
+                to = n_low - 1 - j if 2 * step == n_high else j
+                pairs.append((i * n_low + j, (i + step) * n_low + to))
+        return pairs
+
     memory = time_memory[:, :, 0]
-    with jax.named_scope("memory_songs"):
-        memory = jnp.concatenate(
-            [of_song(memory, core), swapped(of_song(memory, 1 - core), "core")], axis=0
-        )
     with jax.named_scope("memory_high"):
         held = [memory]
         for s in range(1, n_high):
-            held.append(lax.ppermute(memory, "high", [(i, i + s) for i in range(n_high - s)]))
-        held = jnp.stack(held)
-    with jax.named_scope("memory_low"):
-        held = lax.all_to_all(
-            jnp.broadcast_to(held[None], (n_low, *held.shape)), "low", 0, 0, tiled=True
-        )
+            held.append(lax.ppermute(memory, ("high", "low"), places(s)))
+    near = held[1]
+    held = jnp.stack(held, axis=1)
     with jax.named_scope("query_songs"):
         packed = jnp.concatenate([time_query[:, :, 0], time_grad_out[:, :, 0]], axis=2)
+        packed = after(packed, near)
         own = jnp.concatenate(
             [of_song(packed, core), swapped(of_song(packed, 1 - core), "core")], axis=0
         )
     with jax.named_scope("query_sides"):
         other = swapped(own, "side")
+    with jax.named_scope("memory_low"):
+        held = lax.all_to_all(
+            jnp.broadcast_to(held[None], (n_low, *held.shape)).reshape(-1, *held.shape[1:]),
+            ("low", "core"), 0, 0, tiled=True,
+        )
+    bits = [1 << i for i in reversed(range((tracks - 1).bit_length()))]
+
+    def across(array, bit):
+        return lax.ppermute(array, "track", [(i, i ^ bit) for i in range(tracks)])
 
     with jax.named_scope("track_gather"):
-        track_blocks = track_memory.reshape(1, block, 2 * head)
-        everything = lax.all_to_all(
-            jnp.broadcast_to(track_blocks, (tracks, block, 2 * head)), "track", 0, 0, tiled=True
-        )
-    track_query_grad, track_partial = pl.pallas_call(
-        functools.partial(track_kernel, heads, head, scale, 32),
-        out_shape=(
-            jax.ShapeDtypeStruct((block, feature), jnp.bfloat16),
-            jax.ShapeDtypeStruct((tracks, block, 2 * head), jnp.bfloat16),
-        ),
-        in_specs=[VMEM] * 3,
-        out_specs=(VMEM, VMEM),
-        compiler_params=PARAMS,
-        name="track_core",
-    )(track_query.reshape(block, feature), track_grad_out.reshape(block, feature), everything)
+        everything = after(track_memory.reshape(1, block, 2 * head), near)
+        for bit in bits:
+            everything = jnp.concatenate([everything, across(everything, bit)], axis=0)
 
     mine = pl.pallas_call(
         functools.partial(stats_kernel, heads, head, scale * LOG2E),
@@ -255,12 +258,24 @@
     )(info, own, other, held)
     with jax.named_scope("stats_sides"):
         theirs = swapped(mine, "side")
+    track_query_grad, track_partial = pl.pallas_call(
+        functools.partial(track_kernel, heads, head, scale, 32),
+        out_shape=(
+            jax.ShapeDtypeStruct((block, feature), jnp.bfloat16),
+            jax.ShapeDtypeStruct((tracks, block, 2 * head), jnp.bfloat16),
+        ),
+        in_specs=[VMEM] * 3,
+        out_specs=(VMEM, VMEM),
+        compiler_params=PARAMS,
+        name="track_core",
+    )(track_query.reshape(block, feature), track_grad_out.reshape(block, feature), after(everything, mine))
+    theirs = after(theirs, track_partial)
     own_grad, other_grad, memory_grad = pl.pallas_call(
         functools.partial(grads_kernel, heads, head, scale),
         out_shape=(
             jax.ShapeDtypeStruct((block, feature), jnp.float32),
             jax.ShapeDtypeStruct((block, feature), jnp.bfloat16),
-            jax.ShapeDtypeStruct((n_low, n_high, block, 2 * head), jnp.bfloat16),
+            jax.ShapeDtypeStruct((2 * n_low, n_high, pos_dev, 2 * head), jnp.bfloat16),
         ),
         in_specs=[SMEM] + [VMEM] * 5,
         out_specs=(VMEM, VMEM, VMEM),
@@ -279,16 +294,19 @@
     )(info, own, other, held, mine, theirs)
 
     with jax.named_scope("memory_grad_low"):
-        parts = lax.all_to_all(memory_grad, "low", 0, 0, tiled=True)
+        parts = lax.all_to_all(memory_grad, ("low", "core"), 0, 0, tiled=True)
+        parts = parts.reshape(n_low, 2, n_high, pos_dev, 2 * head)
         sums = jnp.sum(parts.astype(jnp.float32), axis=0)
     with jax.named_scope("memory_grad_high"):
-        gathered = sums[0]
+        gathered = sums[:, 0]
         for s in range(1, n_high):
             back = lax.ppermute(
-                sums[s].astype(jnp.bfloat16), "high", [(i + s, i) for i in range(n_high - s)]
+                sums[:, s].astype(jnp.bfloat16),
+                ("high", "low"),
+                [(to, origin) for origin, to in places(s)],
             )
             gathered = gathered + back.astype(jnp.float32)
-        gathered = gathered.astype(jnp.bfloat16)
+        time_memory_grad = gathered.astype(jnp.bfloat16).reshape(time_memory.shape)
 
     def to_songs(array):
         ours = array[:pos_dev]
@@ -297,15 +315,17 @@
         second = jnp.where(core == 0, back, ours)
         return jnp.stack([first, second])[:, :, None, :]
 
-    with jax.named_scope("memory_grad_songs"):
-        time_memory_grad = to_songs(gathered)
     with jax.named_scope("query_grad_sides"):
         query_grad = own_grad + swapped(other_grad, "side").astype(jnp.float32)
     with jax.named_scope("query_grad_songs"):
         time_query_grad = to_songs(query_grad.astype(jnp.bfloat16))
     with jax.named_scope("track_scatter"):
-        track_parts = lax.all_to_all(track_partial, "track", 0, 0, tiled=True)
-        track_memory_grad = jnp.sum(track_parts.astype(jnp.float32), axis=0).astype(jnp.bfloat16)
+        partial = track_partial
+        for bit in reversed(bits):
+            kept, sent = jnp.split(partial, 2)
+            back = across(sent.astype(jnp.bfloat16), bit)
+            partial = kept.astype(jnp.float32) + back.astype(jnp.float32)
+        track_memory_grad = partial.astype(jnp.bfloat16)
     return (
         time_query_grad,
         time_memory_grad,

time: 153 us -> 136 us (0.89)
  the two profiles are of different devices: /device:TPU:99 before, /device:TPU:97 now
where the time goes in v2:
time: 136 us; the launch traced here: 135 us
  starting transfers between devices  80 us (59%)
  waiting for transfers between devices  39.8 us (29%)
  Pallas kernels  9.21 us (7%)
  other arithmetic  3.51 us (3%)
    ppermute x3, waiting for transfers between devices, body(): lax.ppermute(sums[:, s].astype(jnp.bfloat16), ('high', 'low'), [(to, orig...  27.4 us
    ppermute x6, starting transfers between devices, across(): return lax.ppermute(array, 'track', [(i, i ^ bit) for i in range(tracks)])  24.9 us
    ppermute x3, starting transfers between devices, body(): held.append(lax.ppermute(memory, ('high', 'low'), places(s)))  16.7 us
    ppermute x5, starting transfers between devices, swapped(): return lax.ppermute(block, axis, [(0, 1), (1, 0)])  14.1 us
    all_to_all x1, starting transfers between devices, body(): lax.all_to_all(jnp.broadcast_to(held[None], (n_low, *held.shape)).reshape...  14 us
    ppermute x6, waiting for transfers between devices, across(): return lax.ppermute(array, 'track', [(i, i ^ bit) for i in range(tracks)])  6.5 us
    all_to_all x1, starting transfers between devices, body(): parts = lax.all_to_all(memory_grad, ('low', 'core'), 0, 0, tiled=True)  6.44 us
    pallas_call x1, Pallas kernels, body(): pl.pallas_call(functools.partial(grads_kernel, heads, head, scale), out_s...  4.33 us
  transfers between devices with their start and end apart: 19, of which 10 were waited for; matrix products, arithmetic and copies ran while one was open for 2% of the time, Pallas kernels for 4%

profile of v2, /device:TPU:97, one launch (start us, length us, event | category | flops | bytes accessed | tf_op | source)
XLA Modules:
  0.0 134.8 jit_solution(5651854460908107370)
XLA Ops:
  0.6 8.8 %collective-permute-start = (bf16[2,64,256]{2,1,0:T(8,128)(2,1)}, bf16[2,64,256]{2,1,0:T(8,128)(2,1)S(1)}, u32[]{:S(2)}, u32[]{:S(2)}) collective-permute-start(bf16[2,64,256]{2,1,0:T(8,128)(2,1)} %bitcast.73), channel_id=1, source_target_pairs={{0,16},{4,20},{8,24},{12,28},{16,32},{20,36},{24,40},{28,44},{32,4... | collective-permute-start | bytes 196616 | tf_op jit(solution)/shard_map/memory_high/ppermute | solution.py:223
  9.5 6.6 %collective-permute-start.3 = (bf16[2,64,256]{2,1,0:T(8,128)(2,1)}, bf16[2,64,256]{2,1,0:T(8,128)(2,1)S(1)}, u32[]{:S(2)}, u32[]{:S(2)}) collective-permute-start(bf16[2,64,256]{2,1,0:T(8,128)(2,1)} %bitcast.74), channel_id=1, source_target_pairs={{0,44},{4,40},{8,36},{12,32},{16,60},{20,56},{24,52},{28,48},{1,45... | collective-permute-start | bytes 196616 | tf_op jit(solution)/shard_map/memory_high/ppermute | solution.py:223
  16.0 1.3 collective-permute-start.4
  17.3 0.0 collective-permute-done
  17.3 0.3 collective-permute-done.3
  17.7 1.3 collective-permute-done.4
  19.0 0.9 pad_maximum_fusion.3
  19.9 1.1 broadcast_in_dim.4
  21.0 0.0 copy-start.3
  21.0 0.0 copy-start.4
  21.0 14.0 %all-to-all-start = ((bf16[8,4,64,256]{3,2,1,0:T(8,128)(2,1)}), bf16[8,4,64,256]{3,2,1,0:T(8,128)(2,1)S(1)}, u32[]{:S(2)}, u32[]{:S(2)}) async-start(bf16[8,4,64,256]{3,2,1,0:T(8,128)(2,1)} %bitcast.13), calls=%async_computation | async-start | bytes 2097152 | tf_op jit(solution)/shard_map/memory_low/all_to_all | solution.py:235
  35.0 0.0 copy-done.3
  35.0 0.0 copy-done.4
  35.0 0.0 copy-start.2
  35.1 2.3 %collective-permute-start.1 = (bf16[64,2048]{1,0:T(8,128)(2,1)S(1)}, bf16[64,2048]{1,0:T(8,128)(2,1)S(1)}, u32[]{:S(2)}, u32[]{:S(2)}) collective-permute-start(bf16[64,2048]{1,0:T(8,128)(2,1)S(1)} %get-tuple-element.31), channel_id=1, source_target_pairs={{0,1},{1,0},{2,3},{3,2},{4,5},{5,4},{6,7},{7,6},{8,9},{9,8},{10,11... | collective-permute-start | bytes 786440 | tf_op jit(solution)/shard_map/query_songs/ppermute | solution.py:30
  37.4 0.0 copy-done.2
  37.4 4.8 %collective-permute-start.6 = (bf16[1,128,256]{2,1,0:T(8,128)(2,1)S(1)}, bf16[1,128,256]{2,1,0:T(8,128)(2,1)S(1)}, u32[]{:S(2)}, u32[]{:S(2)}) collective-permute-start(bf16[1,128,256]{2,1,0:T(8,128)(2,1)S(1)} %bitcast.66), channel_id=1, source_target_pairs={{0,256},{64,320},{128,384},{192,448},{256,0},{320,64},{384,128},{4... | collective-permute-start | bytes 196616 | tf_op jit(solution)/shard_map/track_gather/ppermute | solution.py:242
  42.2 0.0 collective-permute-done.1
  42.3 2.3 %collective-permute-start.2 = (bf16[128,2048]{1,0:T(8,128)(2,1)S(1)}, bf16[128,2048]{1,0:T(8,128)(2,1)S(1)}, u32[]{:S(2)}, u32[]{:S(2)}) collective-permute-start(bf16[128,2048]{1,0:T(8,128)(2,1)S(1)} %pad_maximum_fusion.1.own), channel_id=1, source_target_pairs={{0,2},{2,0},{1,3},{3,1},{4,6},{6,4},{5,7},{7,5},{8,10},{10,8},{9,1... | collective-permute-start | bytes 1572872 | tf_op jit(solution)/shard_map/query_sides/ppermute | solution.py:30
  44.6 0.0 collective-permute-done.6
  44.6 4.7 %collective-permute-start.7 = (bf16[2,128,256]{2,1,0:T(8,128)(2,1)S(1)}, bf16[2,128,256]{2,1,0:T(8,128)(2,1)S(1)}, u32[]{:S(2)}, u32[]{:S(2)}) collective-permute-start(bf16[2,128,256]{2,1,0:T(8,128)(2,1)S(1)} %pad_maximum_fusion.5), channel_id=1, source_target_pairs={{0,128},{64,192},{128,0},{192,64},{256,384},{320,448},{384,256},{4... | collective-permute-start | bytes 393224 | tf_op jit(solution)/shard_map/track_gather/ppermute | solution.py:242
  49.3 3.0 %collective-permute-done.7 = bf16[2,128,256]{2,1,0:T(8,128)(2,1)S(1)} collective-permute-done((bf16[2,128,256]{2,1,0:T(8,128)(2,1)S(1)}, bf16[2,128,256]{2,1,0:T(8,128)(2,1)S(1)}, u32[]{:S(2)}, u32[]{:S(2)}) %collective-permute-start.7) | collective-permute-done | bytes 131104 | tf_op jit(solution)/shard_map/track_gather/ppermute | solution.py:242
  52.4 3.1 %collective-permute-start.8 = (bf16[4,128,256]{2,1,0:T(8,128)(2,1)S(1)}, bf16[4,128,256]{2,1,0:T(8,128)(2,1)S(1)}, u32[]{:S(2)}, u32[]{:S(2)}) collective-permute-start(bf16[4,128,256]{2,1,0:T(8,128)(2,1)S(1)} %pad_maximum_fusion.4), channel_id=1, source_target_pairs={{0,64},{64,0},{128,192},{192,128},{256,320},{320,256},{384,448},{4... | collective-permute-start | bytes 786440 | tf_op jit(solution)/shard_map/track_gather/ppermute | solution.py:242
  55.5 0.1 pad_add_fusion.info
  55.6 1.6 %collective-permute-done.2.other = bf16[128,2048]{1,0:T(8,128)(2,1)S(1)} collective-permute-done((bf16[128,2048]{1,0:T(8,128)(2,1)S(1)}, bf16[128,2048]{1,0:T(8,128)(2,1)S(1)}, u32[]{:S(2)}, u32[]{:S(2)}) %collective-permute-start.2) | collective-permute-done | bytes 524320 | tf_op jit(solution)/shard_map/query_sides/ppermute | solution.py:30
  57.2 1.7 %all-to-all-done.memory = bf16[8,4,64,256]{3,2,1,0:T(8,128)(2,1)S(1)} async-done(((bf16[8,4,64,256]{3,2,1,0:T(8,128)(2,1)}), bf16[8,4,64,256]{3,2,1,0:T(8,128)(2,1)S(1)}, u32[]{:S(2)}, u32[]{:S(2)}) %all-to-all-start) | async-done | bytes 1048608 | tf_op jit(solution)/shard_map/memory_low/all_to_all | solution.py:235
  58.9 2.4 %time_stats.1.mine = f32[3,8,256]{2,1,0:T(8,128)S(1)} custom-call(s32[4]{0:T(128)S(1)} %pad_add_fusion.info, bf16[128,2048]{1,0:T(8,128)(2,1)S(1)} %pad_maximum_fusion.1.own, bf16[128,2048]{1,0:T(8,128)(2,1)S(1)} %collective-permute-done.2.other, bf16[8,4,64,256]{3,2,1,0:T(8,128)(2,1)S(1)} %all-to-all-done.memory), custom_call_target="tpu_custom_call" | custom-call | tf_op jit(solution)/shard_map/time_stats/pallas_call | solution.py:249
  61.3 0.0 copy-start
  61.3 0.0 copy-start.1
  61.3 3.3 %collective-permute-start.5 = (f32[3,8,256]{2,1,0:T(8,128)S(1)}, f32[3,8,256]{2,1,0:T(8,128)S(1)}, u32[]{:S(2)}, u32[]{:S(2)}) collective-permute-start(f32[3,8,256]{2,1,0:T(8,128)S(1)} %time_stats.1.mine), channel_id=1, source_target_pairs={{0,2},{2,0},{1,3},{3,1},{4,6},{6,4},{5,7},{7,5},{8,10},{10,8},{9,1... | collective-permute-start | bytes 73736 | tf_op jit(solution)/shard_map/stats_sides/ppermute | solution.py:30
  64.7 0.0 collective-permute-done.8
  64.7 0.1 pad_maximum_fusion.2.memory
  64.7 0.0 copy-done
  64.8 0.0 copy-done.1
  64.8 2.5 %track_core.1 = (bf16[128,1024]{1,0:T(8,128)(2,1)}, bf16[8,128,256]{2,1,0:T(8,128)(2,1)S(1)}) custom-call(bf16[128,1024]{1,0:T(8,128)(2,1)S(1)} %bitcast.63, bf16[128,1024]{1,0:T(8,128)(2,1)S(1)} %bitcast.64, bf16[8,128,256]{2,1,0:T(8,128)(2,1)S(1)} %pad_maximum_fusion.2.memory), custom_call_target="tpu_custom_call" | custom-call | tf_op jit(solution)/shard_map/track_core/pallas_call | solution.py:261
  67.3 0.0 collective-permute-done.5.theirs
  67.3 4.3 %time_grads.1 = (f32[128,1024]{1,0:T(8,128)S(1)}, bf16[128,1024]{1,0:T(8,128)(2,1)S(1)}, bf16[8,4,64,256]{3,2,1,0:T(8,128)(2,1)}) custom-call(s32[4]{0:T(128)S(1)} %pad_add_fusion.info, bf16[128,2048]{1,0:T(8,128)(2,1)S(1)} %pad_maximum_fusion.1.own, bf16[128,2048]{1,0:T(8,128)(2,1)S(1)} %collective-permute-done.2.other, ...), custom_call_target="tpu_custom_call" | custom-call | tf_op jit(solution)/shard_map/time_grads/pallas_call | solution.py:273
  71.6 6.4 %all-to-all-start.1 = ((bf16[8,4,64,256]{3,2,1,0:T(8,128)(2,1)}), bf16[8,4,64,256]{3,2,1,0:T(8,128)(2,1)S(1)}, u32[]{:S(2)}, u32[]{:S(2)}) async-start(bf16[8,4,64,256]{3,2,1,0:T(8,128)(2,1)} %get-tuple-element.20), calls=%async_computation.1 | async-start | bytes 2097152 | tf_op jit(solution)/shard_map/memory_grad_low/all_to_all | solution.py:297
  78.1 3.1 %collective-permute-start.14 = (bf16[4,128,256]{2,1,0:T(8,128)(2,1)S(1)}, bf16[4,128,256]{2,1,0:T(8,128)(2,1)S(1)}, u32[]{:S(2)}, u32[]{:S(2)}) collective-permute-start(bf16[4,128,256]{2,1,0:T(8,128)(2,1)S(1)} %split.21), channel_id=1, source_target_pairs={{0,64},{64,0},{128,192},{192,128},{256,320},{320,256},{384,448},{4... | collective-permute-start | bytes 786440 | tf_op jit(solution)/shard_map/track_scatter/ppermute | solution.py:242
  81.2 2.8 %collective-permute-start.9 = (bf16[128,1024]{1,0:T(8,128)(2,1)S(1)}, bf16[128,1024]{1,0:T(8,128)(2,1)S(1)}, u32[]{:S(2)}, u32[]{:S(2)}) collective-permute-start(bf16[128,1024]{1,0:T(8,128)(2,1)S(1)} %get-tuple-element.19), channel_id=1, source_target_pairs={{0,2},{2,0},{1,3},{3,1},{4,6},{6,4},{5,7},{7,5},{8,10},{10,8},{9,1... | collective-permute-start | bytes 786440 | tf_op jit(solution)/shard_map/query_grad_sides/ppermute | solution.py:30
  84.0 3.4 %collective-permute-done.14 = bf16[4,128,256]{2,1,0:T(8,128)(2,1)S(1)} collective-permute-done((bf16[4,128,256]{2,1,0:T(8,128)(2,1)S(1)}, bf16[4,128,256]{2,1,0:T(8,128)(2,1)S(1)}, u32[]{:S(2)}, u32[]{:S(2)}) %collective-permute-start.14) | collective-permute-done | bytes 262176 | tf_op jit(solution)/shard_map/track_scatter/ppermute | solution.py:242
  87.5 0.1 convert_add_fusion
  87.6 4.7 %collective-permute-start.15 = (bf16[2,128,256]{2,1,0:T(8,128)(2,1)S(1)}, bf16[2,128,256]{2,1,0:T(8,128)(2,1)S(1)}, u32[]{:S(2)}, u32[]{:S(2)}) collective-permute-start(bf16[2,128,256]{2,1,0:T(8,128)(2,1)S(1)} %split.37), channel_id=1, source_target_pairs={{0,128},{64,192},{128,0},{192,64},{256,384},{320,448},{384,256},{4... | collective-permute-start | bytes 393224 | tf_op jit(solution)/shard_map/track_scatter/ppermute | solution.py:242
  92.2 0.0 collective-permute-done.9
  92.2 0.1 add_convert_fusion
  92.3 3.4 %collective-permute-start.10 = (bf16[64,1024]{1,0:T(8,128)(2,1)S(1)}, bf16[64,1024]{1,0:T(8,128)(2,1)S(1)}, u32[]{:S(2)}, u32[]{:S(2)}) collective-permute-start(bf16[64,1024]{1,0:T(8,128)(2,1)S(1)} %slice.28), channel_id=1, source_target_pairs={{0,1},{1,0},{2,3},{3,2},{4,5},{5,4},{6,7},{7,6},{8,9},{9,8},{10,11... | collective-permute-start | bytes 393224 | tf_op jit(solution)/shard_map/query_grad_songs/ppermute | solution.py:30
  95.7 0.0 collective-permute-done.15
  95.8 4.5 %collective-permute-start.16 = (bf16[1,128,256]{2,1,0:T(8,128)(2,1)S(1)}, bf16[1,128,256]{2,1,0:T(8,128)(2,1)S(1)}, u32[]{:S(2)}, u32[]{:S(2)}) collective-permute-start(bf16[1,128,256]{2,1,0:T(8,128)(2,1)S(1)} %split.38), channel_id=1, source_target_pairs={{0,256},{64,320},{128,384},{192,448},{256,0},{320,64},{384,128},{4... | collective-permute-start | bytes 196616 | tf_op jit(solution)/shard_map/track_scatter/ppermute | solution.py:242
  100.3 0.0 collective-permute-done.10
  100.3 0.7 maximum_bitcast_fusion
  101.1 0.9 all-to-all-done.1
  102.0 0.2 convert_reduce_fusion
  102.2 1.3 collective-permute-start.11
  103.5 1.3 collective-permute-start.12
  104.8 1.3 collective-permute-start.13
  106.1 0.0 collective-permute-done.16
  106.1 0.6 fusion
  106.7 4.5 %collective-permute-done.11 = bf16[2,64,256]{2,1,0:T(8,128)(2,1)S(1)} collective-permute-done((bf16[2,64,256]{2,1,0:T(8,128)(2,1)S(1)}, bf16[2,64,256]{2,1,0:T(8,128)(2,1)S(1)}, u32[]{:S(2)}, u32[]{:S(2)}) %collective-permute-start.11) | collective-permute-done | bytes 65568 | tf_op jit(solution)/shard_map/memory_grad_high/ppermute | solution.py:303
  111.2 17.4 %collective-permute-done.12 = bf16[2,64,256]{2,1,0:T(8,128)(2,1)S(1)} collective-permute-done((bf16[2,64,256]{2,1,0:T(8,128)(2,1)S(1)}, bf16[2,64,256]{2,1,0:T(8,128)(2,1)S(1)}, u32[]{:S(2)}, u32[]{:S(2)}) %collective-permute-start.12) | collective-permute-done | bytes 65568 | tf_op jit(solution)/shard_map/memory_grad_high/ppermute | solution.py:303
  128.7 5.5 %collective-permute-done.13 = bf16[2,64,256]{2,1,0:T(8,128)(2,1)S(1)} collective-permute-done((bf16[2,64,256]{2,1,0:T(8,128)(2,1)S(1)}, bf16[2,64,256]{2,1,0:T(8,128)(2,1)S(1)}, u32[]{:S(2)}, u32[]{:S(2)}) %collective-permute-start.13) | collective-permute-done | bytes 65568 | tf_op jit(solution)/shard_map/memory_grad_high/ppermute | solution.py:303
  134.1 0.7 fusion.5
  (14 shorter events, 0.3 us)
Async XLA Ops:
  0.6 16.7 %collective-permute-start = (bf16[2,64,256]{2,1,0:T(8,128)(2,1)}, bf16[2,64,256]{2,1,0:T(8,128)(2,1)S(1)}, u32[]{:S(2)}, u32[]{:S(2)}) collective-permute-start(bf16[2,64,256]{2,1,0:T(8,128)(2,1)} %bitcast.73), channel_id=1, source_target_pairs={{0,16},{4,20},{8,24},{12,28},{16,32},{20,36},{24,40},{28,44},{32,4... | collective-permute-start | bytes 196616 | tf_op jit(solution)/shard_map/memory_high/ppermute | solution.py:223
  9.5 8.2 %collective-permute-start.3 = (bf16[2,64,256]{2,1,0:T(8,128)(2,1)}, bf16[2,64,256]{2,1,0:T(8,128)(2,1)S(1)}, u32[]{:S(2)}, u32[]{:S(2)}) collective-permute-start(bf16[2,64,256]{2,1,0:T(8,128)(2,1)} %bitcast.74), channel_id=1, source_target_pairs={{0,44},{4,40},{8,36},{12,32},{16,60},{20,56},{24,52},{28,48},{1,45... | collective-permute-start | bytes 196616 | tf_op jit(solution)/shard_map/memory_high/ppermute | solution.py:223
  16.0 2.9 %collective-permute-start.4 = (bf16[2,64,256]{2,1,0:T(8,128)(2,1)}, bf16[2,64,256]{2,1,0:T(8,128)(2,1)S(1)}, u32[]{:S(2)}, u32[]{:S(2)}) collective-permute-start(bf16[2,64,256]{2,1,0:T(8,128)(2,1)} %bitcast.75), channel_id=1, source_target_pairs={{0,48},{4,52},{8,56},{12,60},{1,49},{5,53},{9,57},{13,61},{2,50},{... | collective-permute-start | bytes 196616 | tf_op jit(solution)/shard_map/memory_high/ppermute | solution.py:223
  21.0 14.0 %copy-start.3 = (bf16[2,64,1,1024]{3,1,2,0:T(8,128)(2,1)S(1)}, bf16[2,64,1,1024]{3,1,2,0:T(8,128)(2,1)}, u32[]{:S(2)}) copy-start(bf16[2,64,1,1024]{3,1,2,0:T(8,128)(2,1)} %param.8) | copy-start | bytes 786436
  21.0 14.0 %copy-start.4 = (bf16[2,64,1,1024]{3,1,2,0:T(8,128)(2,1)S(1)}, bf16[2,64,1,1024]{3,1,2,0:T(8,128)(2,1)}, u32[]{:S(2)}) copy-start(bf16[2,64,1,1024]{3,1,2,0:T(8,128)(2,1)} %param.6) | copy-start | bytes 786436
  21.0 37.9 %all-to-all-start = ((bf16[8,4,64,256]{3,2,1,0:T(8,128)(2,1)}), bf16[8,4,64,256]{3,2,1,0:T(8,128)(2,1)S(1)}, u32[]{:S(2)}, u32[]{:S(2)}) async-start(bf16[8,4,64,256]{3,2,1,0:T(8,128)(2,1)} %bitcast.13), calls=%async_computation | async-start | bytes 2097152 | tf_op jit(solution)/shard_map/memory_low/all_to_all | solution.py:235
  35.0 2.4 %copy-start.2 = (bf16[2,64,1,256]{3,1,2,0:T(8,128)(2,1)S(1)}, bf16[2,64,1,256]{3,1,2,0:T(8,128)(2,1)}, u32[]{:S(2)}) copy-start(bf16[2,64,1,256]{3,1,2,0:T(8,128)(2,1)} %param.10) | copy-start | bytes 196612
  35.1 7.1 %collective-permute-start.1 = (bf16[64,2048]{1,0:T(8,128)(2,1)S(1)}, bf16[64,2048]{1,0:T(8,128)(2,1)S(1)}, u32[]{:S(2)}, u32[]{:S(2)}) collective-permute-start(bf16[64,2048]{1,0:T(8,128)(2,1)S(1)} %get-tuple-element.31), channel_id=1, source_target_pairs={{0,1},{1,0},{2,3},{3,2},{4,5},{5,4},{6,7},{7,6},{8,9},{9,8},{10,11... | collective-permute-start | bytes 786440 | tf_op jit(solution)/shard_map/query_songs/ppermute | solution.py:30
  37.4 7.2 %collective-permute-start.6 = (bf16[1,128,256]{2,1,0:T(8,128)(2,1)S(1)}, bf16[1,128,256]{2,1,0:T(8,128)(2,1)S(1)}, u32[]{:S(2)}, u32[]{:S(2)}) collective-permute-start(bf16[1,128,256]{2,1,0:T(8,128)(2,1)S(1)} %bitcast.66), channel_id=1, source_target_pairs={{0,256},{64,320},{128,384},{192,448},{256,0},{320,64},{384,128},{4... | collective-permute-start | bytes 196616 | tf_op jit(solution)/shard_map/track_gather/ppermute | solution.py:242
  42.3 14.9 %collective-permute-start.2 = (bf16[128,2048]{1,0:T(8,128)(2,1)S(1)}, bf16[128,2048]{1,0:T(8,128)(2,1)S(1)}, u32[]{:S(2)}, u32[]{:S(2)}) collective-permute-start(bf16[128,2048]{1,0:T(8,128)(2,1)S(1)} %pad_maximum_fusion.1.own), channel_id=1, source_target_pairs={{0,2},{2,0},{1,3},{3,1},{4,6},{6,4},{5,7},{7,5},{8,10},{10,8},{9,1... | collective-permute-start | bytes 1572872 | tf_op jit(solution)/shard_map/query_sides/ppermute | solution.py:30
  44.6 7.7 %collective-permute-start.7 = (bf16[2,128,256]{2,1,0:T(8,128)(2,1)S(1)}, bf16[2,128,256]{2,1,0:T(8,128)(2,1)S(1)}, u32[]{:S(2)}, u32[]{:S(2)}) collective-permute-start(bf16[2,128,256]{2,1,0:T(8,128)(2,1)S(1)} %pad_maximum_fusion.5), channel_id=1, source_target_pairs={{0,128},{64,192},{128,0},{192,64},{256,384},{320,448},{384,256},{4... | collective-permute-start | bytes 393224 | tf_op jit(solution)/shard_map/track_gather/ppermute | solution.py:242
  52.4 12.3 %collective-permute-start.8 = (bf16[4,128,256]{2,1,0:T(8,128)(2,1)S(1)}, bf16[4,128,256]{2,1,0:T(8,128)(2,1)S(1)}, u32[]{:S(2)}, u32[]{:S(2)}) collective-permute-start(bf16[4,128,256]{2,1,0:T(8,128)(2,1)S(1)} %pad_maximum_fusion.4), channel_id=1, source_target_pairs={{0,64},{64,0},{128,192},{192,128},{256,320},{320,256},{384,448},{4... | collective-permute-start | bytes 786440 | tf_op jit(solution)/shard_map/track_gather/ppermute | solution.py:242
  61.3 3.4 %copy-start = (bf16[2,64,1,1024]{3,1,2,0:T(8,128)(2,1)S(1)}, bf16[2,64,1,1024]{3,1,2,0:T(8,128)(2,1)}, u32[]{:S(2)}) copy-start(bf16[2,64,1,1024]{3,1,2,0:T(8,128)(2,1)} %param.9) | copy-start | bytes 786436
  61.3 3.4 %copy-start.1 = (bf16[2,64,1,1024]{3,1,2,0:T(8,128)(2,1)S(1)}, bf16[2,64,1,1024]{3,1,2,0:T(8,128)(2,1)}, u32[]{:S(2)}) copy-start(bf16[2,64,1,1024]{3,1,2,0:T(8,128)(2,1)} %param.11) | copy-start | bytes 786436
  61.3 5.9 %collective-permute-start.5 = (f32[3,8,256]{2,1,0:T(8,128)S(1)}, f32[3,8,256]{2,1,0:T(8,128)S(1)}, u32[]{:S(2)}, u32[]{:S(2)}) collective-permute-start(f32[3,8,256]{2,1,0:T(8,128)S(1)} %time_stats.1.mine), channel_id=1, source_target_pairs={{0,2},{2,0},{1,3},{3,1},{4,6},{6,4},{5,7},{7,5},{8,10},{10,8},{9,1... | collective-permute-start | bytes 73736 | tf_op jit(solution)/shard_map/stats_sides/ppermute | solution.py:30
  71.6 30.4 %all-to-all-start.1 = ((bf16[8,4,64,256]{3,2,1,0:T(8,128)(2,1)}), bf16[8,4,64,256]{3,2,1,0:T(8,128)(2,1)S(1)}, u32[]{:S(2)}, u32[]{:S(2)}) async-start(bf16[8,4,64,256]{3,2,1,0:T(8,128)(2,1)} %get-tuple-element.20), calls=%async_computation.1 | async-start | bytes 2097152 | tf_op jit(solution)/shard_map/memory_grad_low/all_to_all | solution.py:297
  78.1 9.4 %collective-permute-start.14 = (bf16[4,128,256]{2,1,0:T(8,128)(2,1)S(1)}, bf16[4,128,256]{2,1,0:T(8,128)(2,1)S(1)}, u32[]{:S(2)}, u32[]{:S(2)}) collective-permute-start(bf16[4,128,256]{2,1,0:T(8,128)(2,1)S(1)} %split.21), channel_id=1, source_target_pairs={{0,64},{64,0},{128,192},{192,128},{256,320},{320,256},{384,448},{4... | collective-permute-start | bytes 786440 | tf_op jit(solution)/shard_map/track_scatter/ppermute | solution.py:242
  81.2 11.0 %collective-permute-start.9 = (bf16[128,1024]{1,0:T(8,128)(2,1)S(1)}, bf16[128,1024]{1,0:T(8,128)(2,1)S(1)}, u32[]{:S(2)}, u32[]{:S(2)}) collective-permute-start(bf16[128,1024]{1,0:T(8,128)(2,1)S(1)} %get-tuple-element.19), channel_id=1, source_target_pairs={{0,2},{2,0},{1,3},{3,1},{4,6},{6,4},{5,7},{7,5},{8,10},{10,8},{9,1... | collective-permute-start | bytes 786440 | tf_op jit(solution)/shard_map/query_grad_sides/ppermute | solution.py:30
  87.6 8.1 %collective-permute-start.15 = (bf16[2,128,256]{2,1,0:T(8,128)(2,1)S(1)}, bf16[2,128,256]{2,1,0:T(8,128)(2,1)S(1)}, u32[]{:S(2)}, u32[]{:S(2)}) collective-permute-start(bf16[2,128,256]{2,1,0:T(8,128)(2,1)S(1)} %split.37), channel_id=1, source_target_pairs={{0,128},{64,192},{128,0},{192,64},{256,384},{320,448},{384,256},{4... | collective-permute-start | bytes 393224 | tf_op jit(solution)/shard_map/track_scatter/ppermute | solution.py:242
  92.3 8.0 %collective-permute-start.10 = (bf16[64,1024]{1,0:T(8,128)(2,1)S(1)}, bf16[64,1024]{1,0:T(8,128)(2,1)S(1)}, u32[]{:S(2)}, u32[]{:S(2)}) collective-permute-start(bf16[64,1024]{1,0:T(8,128)(2,1)S(1)} %slice.28), channel_id=1, source_target_pairs={{0,1},{1,0},{2,3},{3,2},{4,5},{5,4},{6,7},{7,6},{8,9},{9,8},{10,11... | collective-permute-start | bytes 393224 | tf_op jit(solution)/shard_map/query_grad_songs/ppermute | solution.py:30
  95.8 10.3 %collective-permute-start.16 = (bf16[1,128,256]{2,1,0:T(8,128)(2,1)S(1)}, bf16[1,128,256]{2,1,0:T(8,128)(2,1)S(1)}, u32[]{:S(2)}, u32[]{:S(2)}) collective-permute-start(bf16[1,128,256]{2,1,0:T(8,128)(2,1)S(1)} %split.38), channel_id=1, source_target_pairs={{0,256},{64,320},{128,384},{192,448},{256,0},{320,64},{384,128},{4... | collective-permute-start | bytes 196616 | tf_op jit(solution)/shard_map/track_scatter/ppermute | solution.py:242
  102.2 9.1 %collective-permute-start.11 = (bf16[2,64,256]{2,1,0:T(8,128)(2,1)S(1)}, bf16[2,64,256]{2,1,0:T(8,128)(2,1)S(1)}, u32[]{:S(2)}, u32[]{:S(2)}) collective-permute-start(bf16[2,64,256]{2,1,0:T(8,128)(2,1)S(1)} %get-tuple-element.34), channel_id=1, source_target_pairs={{16,0},{20,4},{24,8},{28,12},{32,16},{36,20},{40,24},{44,28},{48,3... | collective-permute-start | bytes 196616 | tf_op jit(solution)/shard_map/memory_grad_high/ppermute | solution.py:303
  103.5 25.2 %collective-permute-start.12 = (bf16[2,64,256]{2,1,0:T(8,128)(2,1)S(1)}, bf16[2,64,256]{2,1,0:T(8,128)(2,1)S(1)}, u32[]{:S(2)}, u32[]{:S(2)}) collective-permute-start(bf16[2,64,256]{2,1,0:T(8,128)(2,1)S(1)} %get-tuple-element.36), channel_id=1, source_target_pairs={{44,0},{40,4},{36,8},{32,12},{60,16},{56,20},{52,24},{48,28},{45,1... | collective-permute-start | bytes 196616 | tf_op jit(solution)/shard_map/memory_grad_high/ppermute | solution.py:303
  104.8 29.4 %collective-permute-start.13 = (bf16[2,64,256]{2,1,0:T(8,128)(2,1)S(1)}, bf16[2,64,256]{2,1,0:T(8,128)(2,1)S(1)}, u32[]{:S(2)}, u32[]{:S(2)}) collective-permute-start(bf16[2,64,256]{2,1,0:T(8,128)(2,1)S(1)} %get-tuple-element.35), channel_id=1, source_target_pairs={{48,0},{52,4},{56,8},{60,12},{49,1},{53,5},{57,9},{61,13},{50,2},{... | collective-permute-start | bytes 196616 | tf_op jit(solution)/shard_map/memory_grad_high/ppermute | solution.py:303

commit v3 on v2

--- a/solution.py
+++ b/solution.py
@@ -59,9 +59,11 @@
     return jnp.concatenate([own[:, cut], other[:, cut]], axis=0)
 
 
-def stats_kernel(heads, head, factor, info, own, other, memory, out, mask, most, total, weighted):
+def stats_kernel(heads, head, factor, info, own, other, memory, out, mask, turned, most, total, weighted):
     groups, block = memory.shape[0] // 2, 2 * memory.shape[2]
     fill_mask(info, mask, block, groups)
+    for h in range(2 * heads):
+        turned[h] = head_rows(own, other, h, head).T
     most[...] = jnp.full(most.shape, FAR_BELOW, jnp.float32)
     total[...] = jnp.zeros(total.shape, jnp.float32)
     weighted[...] = jnp.zeros(weighted.shape, jnp.float32)
@@ -70,23 +72,26 @@
         keys = group_of(memory, index, head, 0)
         values = group_of(memory, index, head, 1)
         for h in range(heads):
-            scores = dot(keys, head_rows(own, other, h, head), NT)
-            products = dot(values, head_rows(own, other, heads + h, head), NT)
-            if masked:
-                scores = scores + mask[...]
-            rows = scores.shape[1]
-            scores = scores.reshape(-1, 8, rows)
-            products = products.reshape(-1, 8, rows)
-            raised = jnp.maximum(most[h], jnp.max(scores, axis=0))
-            fade = jnp.exp2((most[h] - raised) * factor)
-            weights = jnp.exp2((scores - raised[None]) * factor)
-            most[h] = raised
-            total[h] = total[h] * fade + jnp.sum(weights, axis=0)
-            weighted[h] = weighted[h] * fade + jnp.sum(weights * products, axis=0)
+            most_h, total_h, weighted_h = most[h], total[h], weighted[h]
+            for begin in range(0, keys.shape[0], block):
+                scores = dot(keys[begin : begin + block], turned[h], NN)
+                products = dot(values[begin : begin + block], turned[heads + h], NN)
+                if masked:
+                    scores = scores + mask[begin : begin + block]
+                rows = scores.shape[1]
+                scores = scores.reshape(-1, 8, rows)
+                products = products.reshape(-1, 8, rows)
+                raised = jnp.maximum(most_h, jnp.max(scores, axis=0))
+                fade = jnp.exp2((most_h - raised) * factor)
+                weights = jnp.exp2((scores - raised[None]) * factor)
+                most_h = raised
+                total_h = total_h * fade + jnp.sum(weights, axis=0)
+                weighted_h = weighted_h * fade + jnp.sum(weights * products, axis=0)
+            most[h], total[h], weighted[h] = most_h, total_h, weighted_h
 
     visit(0, True)
 
-    @pl.loop(1, info[0] + 1)
+    @pl.loop(memory.shape[1] - info[0], memory.shape[1])
     def _(index):
         visit(index, False)
 
@@ -146,7 +151,7 @@
 
     visit(0, True)
 
-    @pl.loop(1, info[0] + 1)
+    @pl.loop(memory.shape[1] - info[0], memory.shape[1])
     def _(index):
         visit(index, False)
 
@@ -218,11 +223,9 @@
 
     memory = time_memory[:, :, 0]
     with jax.named_scope("memory_high"):
-        held = [memory]
-        for s in range(1, n_high):
-            held.append(lax.ppermute(memory, ("high", "low"), places(s)))
-    near = held[1]
-    held = jnp.stack(held, axis=1)
+        steps = range(n_high - 1, 0, -1)
+        held = [memory] + [lax.ppermute(memory, ("high", "low"), places(s)) for s in steps]
+    near = held[-1]
     with jax.named_scope("query_songs"):
         packed = jnp.concatenate([time_query[:, :, 0], time_grad_out[:, :, 0]], axis=2)
         packed = after(packed, near)
@@ -232,9 +235,9 @@
     with jax.named_scope("query_sides"):
         other = swapped(own, "side")
     with jax.named_scope("memory_low"):
+        everyone = jnp.stack([jnp.broadcast_to(h[None], (n_low, *h.shape)) for h in held], axis=2)
         held = lax.all_to_all(
-            jnp.broadcast_to(held[None], (n_low, *held.shape)).reshape(-1, *held.shape[1:]),
-            ("low", "core"), 0, 0, tiled=True,
+            everyone.reshape(-1, *everyone.shape[2:]), ("low", "core"), 0, 0, tiled=True
         )
     bits = [1 << i for i in reversed(range((tracks - 1).bit_length()))]
 
@@ -251,7 +254,10 @@
         out_shape=jax.ShapeDtypeStruct((3, heads, rows), jnp.float32),
         in_specs=[SMEM] + [VMEM] * 3,
         out_specs=VMEM,
-        scratch_shapes=[pltpu.VMEM((n_low * block, rows), jnp.float32)]
+        scratch_shapes=[
+            pltpu.VMEM((n_low * block, rows), jnp.float32),
+            pltpu.VMEM((2 * heads, head, rows), jnp.bfloat16),
+        ]
         + [pltpu.VMEM((heads, 8, rows), jnp.float32)] * 3,
         compiler_params=PARAMS,
         name="time_stats",
@@ -299,9 +305,9 @@
         sums = jnp.sum(parts.astype(jnp.float32), axis=0)
     with jax.named_scope("memory_grad_high"):
         gathered = sums[:, 0]
-        for s in range(1, n_high):
+        for s in steps:
             back = lax.ppermute(
-                sums[:, s].astype(jnp.bfloat16),
+                sums[:, n_high - s].astype(jnp.bfloat16),
                 ("high", "low"),
                 [(to, origin) for origin, to in places(s)],
             )

time: 136 us -> 129 us (0.949)
  the two profiles are of different devices: /device:TPU:97 before, /device:TPU:129 now
where the time goes in v3:
time: 129 us; the launch traced here: 128 us
  starting transfers between devices  69.4 us (54%)
  waiting for transfers between devices  40 us (31%)
  Pallas kernels  13.1 us (10%)
  other arithmetic  3.78 us (3%)
    ppermute x6, starting transfers between devices, across(): return lax.ppermute(array, 'track', [(i, i ^ bit) for i in range(tracks)])  25.1 us
    ppermute x3, waiting for transfers between devices, body(): lax.ppermute(sums[:, n_high - s].astype(jnp.bfloat16), ('high', 'low'), [...  22.6 us
    ppermute x5, starting transfers between devices, swapped(): return lax.ppermute(block, axis, [(0, 1), (1, 0)])  13.5 us
    ppermute x3, starting transfers between devices, body(): lax.ppermute(memory, ('high', 'low'), places(s))  11.9 us
    all_to_all x1, starting transfers between devices, body(): lax.all_to_all(everyone.reshape(-1, *everyone.shape[2:]), ('low', 'core')...  8.02 us
    pallas_call x1, Pallas kernels, body(): pl.pallas_call(functools.partial(grads_kernel, heads, head, scale), out_s...  6.95 us
    ppermute x6, waiting for transfers between devices, across(): return lax.ppermute(array, 'track', [(i, i ^ bit) for i in range(tracks)])  6.47 us
    ppermute x3, starting transfers between devices, body(): lax.ppermute(sums[:, n_high - s].astype(jnp.bfloat16), ('high', 'low'), [...  6.34 us
  transfers between devices with their start and end apart: 19, of which 7 were waited for; matrix products, arithmetic and copies ran while one was open for 2% of the time, Pallas kernels for 5%

profile of v3, /device:TPU:129, one launch (start us, length us, event | category | flops | bytes accessed | tf_op | source)
XLA Modules:
  0.0 128.4 jit_solution(12611233749115163109)
XLA Ops:
  0.6 8.8 %collective-permute-start = (bf16[2,64,256]{2,1,0:T(8,128)(2,1)}, bf16[2,64,256]{2,1,0:T(8,128)(2,1)S(1)}, u32[]{:S(2)}, u32[]{:S(2)}) collective-permute-start(bf16[2,64,256]{2,1,0:T(8,128)(2,1)} %bitcast.68), channel_id=1, source_target_pairs={{0,16},{4,20},{8,24},{12,28},{16,32},{20,36},{24,40},{28,44},{32,4... | collective-permute-start | bytes 196616 | tf_op jit(solution)/shard_map/memory_high/ppermute | solution.py:227
  9.5 0.7 collective-permute-start.3
  10.1 2.4 %collective-permute-start.4 = (bf16[2,64,256]{2,1,0:T(8,128)(2,1)}, bf16[2,64,256]{2,1,0:T(8,128)(2,1)S(1)}, u32[]{:S(2)}, u32[]{:S(2)}) collective-permute-start(bf16[2,64,256]{2,1,0:T(8,128)(2,1)} %bitcast.70), channel_id=1, source_target_pairs={{0,44},{4,40},{8,36},{12,32},{16,60},{20,56},{24,52},{28,48},{1,45... | collective-permute-start | bytes 196616 | tf_op jit(solution)/shard_map/memory_high/ppermute | solution.py:227
  12.5 2.6 %collective-permute-done = bf16[2,64,256]{2,1,0:T(8,128)(2,1)S(1)} collective-permute-done((bf16[2,64,256]{2,1,0:T(8,128)(2,1)}, bf16[2,64,256]{2,1,0:T(8,128)(2,1)S(1)}, u32[]{:S(2)}, u32[]{:S(2)}) %collective-permute-start) | collective-permute-done | bytes 65568 | tf_op jit(solution)/shard_map/memory_high/ppermute | solution.py:227
  15.1 0.0 collective-permute-done.3
  15.1 0.0 collective-permute-done.4
  15.2 0.9 broadcast_in_dim.10
  16.1 1.1 pad_maximum_fusion
  17.2 0.0 copy-start.3
  17.2 0.0 copy-start.4
  17.2 8.0 %all-to-all-start = ((bf16[8,4,64,256]{3,2,1,0:T(8,128)(2,1)}), bf16[8,4,64,256]{3,2,1,0:T(8,128)(2,1)S(1)}, u32[]{:S(2)}, u32[]{:S(2)}) async-start(bf16[8,4,64,256]{3,2,1,0:T(8,128)(2,1)} %bitcast.9), calls=%async_computation | async-start | bytes 2097152 | tf_op jit(solution)/shard_map/memory_low/all_to_all | solution.py:239
  25.2 0.0 copy-done.3
  25.2 0.0 copy-done.4
  25.2 0.0 copy-start.2
  25.3 1.9 %collective-permute-start.1 = (bf16[64,2048]{1,0:T(8,128)(2,1)S(1)}, bf16[64,2048]{1,0:T(8,128)(2,1)S(1)}, u32[]{:S(2)}, u32[]{:S(2)}) collective-permute-start(bf16[64,2048]{1,0:T(8,128)(2,1)S(1)} %get-tuple-element.31), channel_id=1, source_target_pairs={{0,1},{1,0},{2,3},{3,2},{4,5},{5,4},{6,7},{7,6},{8,9},{9,8},{10,11... | collective-permute-start | bytes 786440 | tf_op jit(solution)/shard_map/query_songs/ppermute | solution.py:30
  27.3 0.0 copy-done.2
  27.3 4.8 %collective-permute-start.6 = (bf16[1,128,256]{2,1,0:T(8,128)(2,1)S(1)}, bf16[1,128,256]{2,1,0:T(8,128)(2,1)S(1)}, u32[]{:S(2)}, u32[]{:S(2)}) collective-permute-start(bf16[1,128,256]{2,1,0:T(8,128)(2,1)S(1)} %bitcast.62), channel_id=1, source_target_pairs={{0,256},{64,320},{128,384},{192,448},{256,0},{320,64},{384,128},{4... | collective-permute-start | bytes 196616 | tf_op jit(solution)/shard_map/track_gather/ppermute | solution.py:245
  32.1 0.0 collective-permute-done.1
  32.2 2.3 %collective-permute-start.2 = (bf16[128,2048]{1,0:T(8,128)(2,1)S(1)}, bf16[128,2048]{1,0:T(8,128)(2,1)S(1)}, u32[]{:S(2)}, u32[]{:S(2)}) collective-permute-start(bf16[128,2048]{1,0:T(8,128)(2,1)S(1)} %pad_maximum_fusion.2.own), channel_id=1, source_target_pairs={{0,2},{2,0},{1,3},{3,1},{4,6},{6,4},{5,7},{7,5},{8,10},{10,8},{9,1... | collective-permute-start | bytes 1572872 | tf_op jit(solution)/shard_map/query_sides/ppermute | solution.py:30
  34.5 0.0 collective-permute-done.6
  34.5 4.7 %collective-permute-start.7 = (bf16[2,128,256]{2,1,0:T(8,128)(2,1)S(1)}, bf16[2,128,256]{2,1,0:T(8,128)(2,1)S(1)}, u32[]{:S(2)}, u32[]{:S(2)}) collective-permute-start(bf16[2,128,256]{2,1,0:T(8,128)(2,1)S(1)} %pad_maximum_fusion.5), channel_id=1, source_target_pairs={{0,128},{64,192},{128,0},{192,64},{256,384},{320,448},{384,256},{4... | collective-permute-start | bytes 393224 | tf_op jit(solution)/shard_map/track_gather/ppermute | solution.py:245
  39.2 2.7 %collective-permute-done.7 = bf16[2,128,256]{2,1,0:T(8,128)(2,1)S(1)} collective-permute-done((bf16[2,128,256]{2,1,0:T(8,128)(2,1)S(1)}, bf16[2,128,256]{2,1,0:T(8,128)(2,1)S(1)}, u32[]{:S(2)}, u32[]{:S(2)}) %collective-permute-start.7) | collective-permute-done | bytes 131104 | tf_op jit(solution)/shard_map/track_gather/ppermute | solution.py:245
  41.9 3.3 %collective-permute-start.8 = (bf16[4,128,256]{2,1,0:T(8,128)(2,1)S(1)}, bf16[4,128,256]{2,1,0:T(8,128)(2,1)S(1)}, u32[]{:S(2)}, u32[]{:S(2)}) collective-permute-start(bf16[4,128,256]{2,1,0:T(8,128)(2,1)S(1)} %pad_maximum_fusion.4), channel_id=1, source_target_pairs={{0,64},{64,0},{128,192},{192,128},{256,320},{320,256},{384,448},{4... | collective-permute-start | bytes 786440 | tf_op jit(solution)/shard_map/track_gather/ppermute | solution.py:245
  45.2 0.1 pad_add_fusion.info
  45.3 1.5 %collective-permute-done.2.other = bf16[128,2048]{1,0:T(8,128)(2,1)S(1)} collective-permute-done((bf16[128,2048]{1,0:T(8,128)(2,1)S(1)}, bf16[128,2048]{1,0:T(8,128)(2,1)S(1)}, u32[]{:S(2)}, u32[]{:S(2)}) %collective-permute-start.2) | collective-permute-done | bytes 524320 | tf_op jit(solution)/shard_map/query_sides/ppermute | solution.py:30
  46.7 4.2 %all-to-all-done.memory = bf16[8,4,64,256]{3,2,1,0:T(8,128)(2,1)S(1)} async-done(((bf16[8,4,64,256]{3,2,1,0:T(8,128)(2,1)}), bf16[8,4,64,256]{3,2,1,0:T(8,128)(2,1)S(1)}, u32[]{:S(2)}, u32[]{:S(2)}) %all-to-all-start) | async-done | bytes 1048608 | tf_op jit(solution)/shard_map/memory_low/all_to_all | solution.py:239
  51.0 3.6 %time_stats.1.mine = f32[3,8,256]{2,1,0:T(8,128)S(1)} custom-call(s32[4]{0:T(128)S(1)} %pad_add_fusion.info, bf16[128,2048]{1,0:T(8,128)(2,1)S(1)} %pad_maximum_fusion.2.own, bf16[128,2048]{1,0:T(8,128)(2,1)S(1)} %collective-permute-done.2.other, bf16[8,4,64,256]{3,2,1,0:T(8,128)(2,1)S(1)} %all-to-all-done.memory), custom_call_target="tpu_custom_call" | custom-call | tf_op jit(solution)/shard_map/time_stats/pallas_call | solution.py:252
  54.6 0.0 copy-start
  54.6 0.0 copy-start.1
  54.6 3.3 %collective-permute-start.5 = (f32[3,8,256]{2,1,0:T(8,128)S(1)}, f32[3,8,256]{2,1,0:T(8,128)S(1)}, u32[]{:S(2)}, u32[]{:S(2)}) collective-permute-start(f32[3,8,256]{2,1,0:T(8,128)S(1)} %time_stats.1.mine), channel_id=1, source_target_pairs={{0,2},{2,0},{1,3},{3,1},{4,6},{6,4},{5,7},{7,5},{8,10},{10,8},{9,1... | collective-permute-start | bytes 73736 | tf_op jit(solution)/shard_map/stats_sides/ppermute | solution.py:30
  58.0 0.0 collective-permute-done.8
  58.0 0.1 pad_maximum_fusion.3.memory
  58.0 0.0 copy-done
  58.0 0.0 copy-done.1
  58.1 2.5 %track_core.1 = (bf16[128,1024]{1,0:T(8,128)(2,1)}, bf16[8,128,256]{2,1,0:T(8,128)(2,1)S(1)}) custom-call(bf16[128,1024]{1,0:T(8,128)(2,1)S(1)} %bitcast.59, bf16[128,1024]{1,0:T(8,128)(2,1)S(1)} %bitcast.60, bf16[8,128,256]{2,1,0:T(8,128)(2,1)S(1)} %pad_maximum_fusion.3.memory), custom_call_target="tpu_custom_call" | custom-call | tf_op jit(solution)/shard_map/track_core/pallas_call | solution.py:267
  60.6 0.0 collective-permute-done.5.theirs
  60.6 6.9 %time_grads.1 = (f32[128,1024]{1,0:T(8,128)S(1)}, bf16[128,1024]{1,0:T(8,128)(2,1)S(1)}, bf16[8,4,64,256]{3,2,1,0:T(8,128)(2,1)}) custom-call(s32[4]{0:T(128)S(1)} %pad_add_fusion.info, bf16[128,2048]{1,0:T(8,128)(2,1)S(1)} %pad_maximum_fusion.2.own, bf16[128,2048]{1,0:T(8,128)(2,1)S(1)} %collective-permute-done.2.other, ...), custom_call_target="tpu_custom_call" | custom-call | tf_op jit(solution)/shard_map/time_grads/pallas_call | solution.py:279
  67.5 4.6 %all-to-all-start.1 = ((bf16[8,4,64,256]{3,2,1,0:T(8,128)(2,1)}), bf16[8,4,64,256]{3,2,1,0:T(8,128)(2,1)S(1)}, u32[]{:S(2)}, u32[]{:S(2)}) async-start(bf16[8,4,64,256]{3,2,1,0:T(8,128)(2,1)} %get-tuple-element.20), calls=%async_computation.1 | async-start | bytes 2097152 | tf_op jit(solution)/shard_map/memory_grad_low/all_to_all | solution.py:303
  72.1 3.2 %collective-permute-start.14 = (bf16[4,128,256]{2,1,0:T(8,128)(2,1)S(1)}, bf16[4,128,256]{2,1,0:T(8,128)(2,1)S(1)}, u32[]{:S(2)}, u32[]{:S(2)}) collective-permute-start(bf16[4,128,256]{2,1,0:T(8,128)(2,1)S(1)} %split.21), channel_id=1, source_target_pairs={{0,64},{64,0},{128,192},{192,128},{256,320},{320,256},{384,448},{4... | collective-permute-start | bytes 786440 | tf_op jit(solution)/shard_map/track_scatter/ppermute | solution.py:245
  75.3 2.8 %collective-permute-start.9 = (bf16[128,1024]{1,0:T(8,128)(2,1)S(1)}, bf16[128,1024]{1,0:T(8,128)(2,1)S(1)}, u32[]{:S(2)}, u32[]{:S(2)}) collective-permute-start(bf16[128,1024]{1,0:T(8,128)(2,1)S(1)} %get-tuple-element.19), channel_id=1, source_target_pairs={{0,2},{2,0},{1,3},{3,1},{4,6},{6,4},{5,7},{7,5},{8,10},{10,8},{9,1... | collective-permute-start | bytes 786440 | tf_op jit(solution)/shard_map/query_grad_sides/ppermute | solution.py:30
  78.1 3.8 %collective-permute-done.14 = bf16[4,128,256]{2,1,0:T(8,128)(2,1)S(1)} collective-permute-done((bf16[4,128,256]{2,1,0:T(8,128)(2,1)S(1)}, bf16[4,128,256]{2,1,0:T(8,128)(2,1)S(1)}, u32[]{:S(2)}, u32[]{:S(2)}) %collective-permute-start.14) | collective-permute-done | bytes 262176 | tf_op jit(solution)/shard_map/track_scatter/ppermute | solution.py:245
  81.9 0.1 convert_add_fusion
  82.0 4.7 %collective-permute-start.15 = (bf16[2,128,256]{2,1,0:T(8,128)(2,1)S(1)}, bf16[2,128,256]{2,1,0:T(8,128)(2,1)S(1)}, u32[]{:S(2)}, u32[]{:S(2)}) collective-permute-start(bf16[2,128,256]{2,1,0:T(8,128)(2,1)S(1)} %split.37), channel_id=1, source_target_pairs={{0,128},{64,192},{128,0},{192,64},{256,384},{320,448},{384,256},{4... | collective-permute-start | bytes 393224 | tf_op jit(solution)/shard_map/track_scatter/ppermute | solution.py:245
  86.6 0.0 collective-permute-done.9
  86.7 0.1 add_convert_fusion
  86.7 3.1 %collective-permute-start.10 = (bf16[64,1024]{1,0:T(8,128)(2,1)S(1)}, bf16[64,1024]{1,0:T(8,128)(2,1)S(1)}, u32[]{:S(2)}, u32[]{:S(2)}) collective-permute-start(bf16[64,1024]{1,0:T(8,128)(2,1)S(1)} %slice.28), channel_id=1, source_target_pairs={{0,1},{1,0},{2,3},{3,2},{4,5},{5,4},{6,7},{7,6},{8,9},{9,8},{10,11... | collective-permute-start | bytes 393224 | tf_op jit(solution)/shard_map/query_grad_songs/ppermute | solution.py:30
  89.8 0.0 collective-permute-done.15
  89.9 4.5 %collective-permute-start.16 = (bf16[1,128,256]{2,1,0:T(8,128)(2,1)S(1)}, bf16[1,128,256]{2,1,0:T(8,128)(2,1)S(1)}, u32[]{:S(2)}, u32[]{:S(2)}) collective-permute-start(bf16[1,128,256]{2,1,0:T(8,128)(2,1)S(1)} %split.38), channel_id=1, source_target_pairs={{0,256},{64,320},{128,384},{192,448},{256,0},{320,64},{384,128},{4... | collective-permute-start | bytes 196616 | tf_op jit(solution)/shard_map/track_scatter/ppermute | solution.py:245
  94.4 0.0 collective-permute-done.10
  94.5 0.7 maximum_bitcast_fusion
  95.2 2.7 %all-to-all-done.1 = bf16[8,4,64,256]{3,2,1,0:T(8,128)(2,1)S(1)} async-done(((bf16[8,4,64,256]{3,2,1,0:T(8,128)(2,1)}), bf16[8,4,64,256]{3,2,1,0:T(8,128)(2,1)S(1)}, u32[]{:S(2)}, u32[]{:S(2)}) %all-to-all-start.1) | async-done | bytes 1048608 | tf_op jit(solution)/shard_map/memory_grad_low/all_to_all | solution.py:303
  97.9 0.2 convert_reduce_fusion
  98.1 0.7 collective-permute-start.11
  98.8 1.3 %collective-permute-start.12 = (bf16[2,64,256]{2,1,0:T(8,128)(2,1)S(1)}, bf16[2,64,256]{2,1,0:T(8,128)(2,1)S(1)}, u32[]{:S(2)}, u32[]{:S(2)}) collective-permute-start(bf16[2,64,256]{2,1,0:T(8,128)(2,1)S(1)} %get-tuple-element.36), channel_id=1, source_target_pairs={{44,0},{40,4},{36,8},{32,12},{60,16},{56,20},{52,24},{48,28},{45,1... | collective-permute-start | bytes 196616 | tf_op jit(solution)/shard_map/memory_grad_high/ppermute | solution.py:309
  100.1 4.4 %collective-permute-start.13 = (bf16[2,64,256]{2,1,0:T(8,128)(2,1)S(1)}, bf16[2,64,256]{2,1,0:T(8,128)(2,1)S(1)}, u32[]{:S(2)}, u32[]{:S(2)}) collective-permute-start(bf16[2,64,256]{2,1,0:T(8,128)(2,1)S(1)} %get-tuple-element.35), channel_id=1, source_target_pairs={{16,0},{20,4},{24,8},{28,12},{32,16},{36,20},{40,24},{44,28},{48,3... | collective-permute-start | bytes 196616 | tf_op jit(solution)/shard_map/memory_grad_high/ppermute | solution.py:309
  104.4 0.0 collective-permute-done.16
  104.5 0.6 fusion
  105.1 0.0 collective-permute-done.11
  105.1 22.6 %collective-permute-done.12 = bf16[2,64,256]{2,1,0:T(8,128)(2,1)S(1)} collective-permute-done((bf16[2,64,256]{2,1,0:T(8,128)(2,1)S(1)}, bf16[2,64,256]{2,1,0:T(8,128)(2,1)S(1)}, u32[]{:S(2)}, u32[]{:S(2)}) %collective-permute-start.12) | collective-permute-done | bytes 65568 | tf_op jit(solution)/shard_map/memory_grad_high/ppermute | solution.py:309
  127.7 0.0 collective-permute-done.13
  127.7 0.7 fusion.5
  (16 shorter events, 0.4 us)
Async XLA Ops:
  0.6 14.5 %collective-permute-start = (bf16[2,64,256]{2,1,0:T(8,128)(2,1)}, bf16[2,64,256]{2,1,0:T(8,128)(2,1)S(1)}, u32[]{:S(2)}, u32[]{:S(2)}) collective-permute-start(bf16[2,64,256]{2,1,0:T(8,128)(2,1)} %bitcast.68), channel_id=1, source_target_pairs={{0,16},{4,20},{8,24},{12,28},{16,32},{20,36},{24,40},{28,44},{32,4... | collective-permute-start | bytes 196616 | tf_op jit(solution)/shard_map/memory_high/ppermute | solution.py:227
  9.5 5.7 %collective-permute-start.3 = (bf16[2,64,256]{2,1,0:T(8,128)(2,1)}, bf16[2,64,256]{2,1,0:T(8,128)(2,1)S(1)}, u32[]{:S(2)}, u32[]{:S(2)}) collective-permute-start(bf16[2,64,256]{2,1,0:T(8,128)(2,1)} %bitcast.69), channel_id=1, source_target_pairs={{0,48},{4,52},{8,56},{12,60},{1,49},{5,53},{9,57},{13,61},{2,50},{... | collective-permute-start | bytes 196616 | tf_op jit(solution)/shard_map/memory_high/ppermute | solution.py:227
  10.1 5.0 %collective-permute-start.4 = (bf16[2,64,256]{2,1,0:T(8,128)(2,1)}, bf16[2,64,256]{2,1,0:T(8,128)(2,1)S(1)}, u32[]{:S(2)}, u32[]{:S(2)}) collective-permute-start(bf16[2,64,256]{2,1,0:T(8,128)(2,1)} %bitcast.70), channel_id=1, source_target_pairs={{0,44},{4,40},{8,36},{12,32},{16,60},{20,56},{24,52},{28,48},{1,45... | collective-permute-start | bytes 196616 | tf_op jit(solution)/shard_map/memory_high/ppermute | solution.py:227
  17.2 8.0 %copy-start.3 = (bf16[2,64,1,1024]{3,1,2,0:T(8,128)(2,1)S(1)}, bf16[2,64,1,1024]{3,1,2,0:T(8,128)(2,1)}, u32[]{:S(2)}) copy-start(bf16[2,64,1,1024]{3,1,2,0:T(8,128)(2,1)} %param.8) | copy-start | bytes 786436
  17.2 8.0 %copy-start.4 = (bf16[2,64,1,1024]{3,1,2,0:T(8,128)(2,1)S(1)}, bf16[2,64,1,1024]{3,1,2,0:T(8,128)(2,1)}, u32[]{:S(2)}) copy-start(bf16[2,64,1,1024]{3,1,2,0:T(8,128)(2,1)} %param.6) | copy-start | bytes 786436
  17.2 33.7 %all-to-all-start = ((bf16[8,4,64,256]{3,2,1,0:T(8,128)(2,1)}), bf16[8,4,64,256]{3,2,1,0:T(8,128)(2,1)S(1)}, u32[]{:S(2)}, u32[]{:S(2)}) async-start(bf16[8,4,64,256]{3,2,1,0:T(8,128)(2,1)} %bitcast.9), calls=%async_computation | async-start | bytes 2097152 | tf_op jit(solution)/shard_map/memory_low/all_to_all | solution.py:239
  25.2 2.0 %copy-start.2 = (bf16[2,64,1,256]{3,1,2,0:T(8,128)(2,1)S(1)}, bf16[2,64,1,256]{3,1,2,0:T(8,128)(2,1)}, u32[]{:S(2)}) copy-start(bf16[2,64,1,256]{3,1,2,0:T(8,128)(2,1)} %param.10) | copy-start | bytes 196612
  25.3 6.8 %collective-permute-start.1 = (bf16[64,2048]{1,0:T(8,128)(2,1)S(1)}, bf16[64,2048]{1,0:T(8,128)(2,1)S(1)}, u32[]{:S(2)}, u32[]{:S(2)}) collective-permute-start(bf16[64,2048]{1,0:T(8,128)(2,1)S(1)} %get-tuple-element.31), channel_id=1, source_target_pairs={{0,1},{1,0},{2,3},{3,2},{4,5},{5,4},{6,7},{7,6},{8,9},{9,8},{10,11... | collective-permute-start | bytes 786440 | tf_op jit(solution)/shard_map/query_songs/ppermute | solution.py:30
  27.3 7.2 %collective-permute-start.6 = (bf16[1,128,256]{2,1,0:T(8,128)(2,1)S(1)}, bf16[1,128,256]{2,1,0:T(8,128)(2,1)S(1)}, u32[]{:S(2)}, u32[]{:S(2)}) collective-permute-start(bf16[1,128,256]{2,1,0:T(8,128)(2,1)S(1)} %bitcast.62), channel_id=1, source_target_pairs={{0,256},{64,320},{128,384},{192,448},{256,0},{320,64},{384,128},{4... | collective-permute-start | bytes 196616 | tf_op jit(solution)/shard_map/track_gather/ppermute | solution.py:245
  32.2 14.6 %collective-permute-start.2 = (bf16[128,2048]{1,0:T(8,128)(2,1)S(1)}, bf16[128,2048]{1,0:T(8,128)(2,1)S(1)}, u32[]{:S(2)}, u32[]{:S(2)}) collective-permute-start(bf16[128,2048]{1,0:T(8,128)(2,1)S(1)} %pad_maximum_fusion.2.own), channel_id=1, source_target_pairs={{0,2},{2,0},{1,3},{3,1},{4,6},{6,4},{5,7},{7,5},{8,10},{10,8},{9,1... | collective-permute-start | bytes 1572872 | tf_op jit(solution)/shard_map/query_sides/ppermute | solution.py:30
  34.5 7.4 %collective-permute-start.7 = (bf16[2,128,256]{2,1,0:T(8,128)(2,1)S(1)}, bf16[2,128,256]{2,1,0:T(8,128)(2,1)S(1)}, u32[]{:S(2)}, u32[]{:S(2)}) collective-permute-start(bf16[2,128,256]{2,1,0:T(8,128)(2,1)S(1)} %pad_maximum_fusion.5), channel_id=1, source_target_pairs={{0,128},{64,192},{128,0},{192,64},{256,384},{320,448},{384,256},{4... | collective-permute-start | bytes 393224 | tf_op jit(solution)/shard_map/track_gather/ppermute | solution.py:245
  41.9 16.1 %collective-permute-start.8 = (bf16[4,128,256]{2,1,0:T(8,128)(2,1)S(1)}, bf16[4,128,256]{2,1,0:T(8,128)(2,1)S(1)}, u32[]{:S(2)}, u32[]{:S(2)}) collective-permute-start(bf16[4,128,256]{2,1,0:T(8,128)(2,1)S(1)} %pad_maximum_fusion.4), channel_id=1, source_target_pairs={{0,64},{64,0},{128,192},{192,128},{256,320},{320,256},{384,448},{4... | collective-permute-start | bytes 786440 | tf_op jit(solution)/shard_map/track_gather/ppermute | solution.py:245
  54.6 3.4 %copy-start = (bf16[2,64,1,1024]{3,1,2,0:T(8,128)(2,1)S(1)}, bf16[2,64,1,1024]{3,1,2,0:T(8,128)(2,1)}, u32[]{:S(2)}) copy-start(bf16[2,64,1,1024]{3,1,2,0:T(8,128)(2,1)} %param.9) | copy-start | bytes 786436
  54.6 3.4 %copy-start.1 = (bf16[2,64,1,1024]{3,1,2,0:T(8,128)(2,1)S(1)}, bf16[2,64,1,1024]{3,1,2,0:T(8,128)(2,1)}, u32[]{:S(2)}) copy-start(bf16[2,64,1,1024]{3,1,2,0:T(8,128)(2,1)} %param.11) | copy-start | bytes 786436
  54.6 5.9 %collective-permute-start.5 = (f32[3,8,256]{2,1,0:T(8,128)S(1)}, f32[3,8,256]{2,1,0:T(8,128)S(1)}, u32[]{:S(2)}, u32[]{:S(2)}) collective-permute-start(f32[3,8,256]{2,1,0:T(8,128)S(1)} %time_stats.1.mine), channel_id=1, source_target_pairs={{0,2},{2,0},{1,3},{3,1},{4,6},{6,4},{5,7},{7,5},{8,10},{10,8},{9,1... | collective-permute-start | bytes 73736 | tf_op jit(solution)/shard_map/stats_sides/ppermute | solution.py:30
  67.5 30.4 %all-to-all-start.1 = ((bf16[8,4,64,256]{3,2,1,0:T(8,128)(2,1)}), bf16[8,4,64,256]{3,2,1,0:T(8,128)(2,1)S(1)}, u32[]{:S(2)}, u32[]{:S(2)}) async-start(bf16[8,4,64,256]{3,2,1,0:T(8,128)(2,1)} %get-tuple-element.20), calls=%async_computation.1 | async-start | bytes 2097152 | tf_op jit(solution)/shard_map/memory_grad_low/all_to_all | solution.py:303
  72.1 9.8 %collective-permute-start.14 = (bf16[4,128,256]{2,1,0:T(8,128)(2,1)S(1)}, bf16[4,128,256]{2,1,0:T(8,128)(2,1)S(1)}, u32[]{:S(2)}, u32[]{:S(2)}) collective-permute-start(bf16[4,128,256]{2,1,0:T(8,128)(2,1)S(1)} %split.21), channel_id=1, source_target_pairs={{0,64},{64,0},{128,192},{192,128},{256,320},{320,256},{384,448},{4... | collective-permute-start | bytes 786440 | tf_op jit(solution)/shard_map/track_scatter/ppermute | solution.py:245
  75.3 11.4 %collective-permute-start.9 = (bf16[128,1024]{1,0:T(8,128)(2,1)S(1)}, bf16[128,1024]{1,0:T(8,128)(2,1)S(1)}, u32[]{:S(2)}, u32[]{:S(2)}) collective-permute-start(bf16[128,1024]{1,0:T(8,128)(2,1)S(1)} %get-tuple-element.19), channel_id=1, source_target_pairs={{0,2},{2,0},{1,3},{3,1},{4,6},{6,4},{5,7},{7,5},{8,10},{10,8},{9,1... | collective-permute-start | bytes 786440 | tf_op jit(solution)/shard_map/query_grad_sides/ppermute | solution.py:30
  82.0 7.8 %collective-permute-start.15 = (bf16[2,128,256]{2,1,0:T(8,128)(2,1)S(1)}, bf16[2,128,256]{2,1,0:T(8,128)(2,1)S(1)}, u32[]{:S(2)}, u32[]{:S(2)}) collective-permute-start(bf16[2,128,256]{2,1,0:T(8,128)(2,1)S(1)} %split.37), channel_id=1, source_target_pairs={{0,128},{64,192},{128,0},{192,64},{256,384},{320,448},{384,256},{4... | collective-permute-start | bytes 393224 | tf_op jit(solution)/shard_map/track_scatter/ppermute | solution.py:245
  86.7 7.7 %collective-permute-start.10 = (bf16[64,1024]{1,0:T(8,128)(2,1)S(1)}, bf16[64,1024]{1,0:T(8,128)(2,1)S(1)}, u32[]{:S(2)}, u32[]{:S(2)}) collective-permute-start(bf16[64,1024]{1,0:T(8,128)(2,1)S(1)} %slice.28), channel_id=1, source_target_pairs={{0,1},{1,0},{2,3},{3,2},{4,5},{5,4},{6,7},{7,6},{8,9},{9,8},{10,11... | collective-permute-start | bytes 393224 | tf_op jit(solution)/shard_map/query_grad_songs/ppermute | solution.py:30
  89.9 14.6 %collective-permute-start.16 = (bf16[1,128,256]{2,1,0:T(8,128)(2,1)S(1)}, bf16[1,128,256]{2,1,0:T(8,128)(2,1)S(1)}, u32[]{:S(2)}, u32[]{:S(2)}) collective-permute-start(bf16[1,128,256]{2,1,0:T(8,128)(2,1)S(1)} %split.38), channel_id=1, source_target_pairs={{0,256},{64,320},{128,384},{192,448},{256,0},{320,64},{384,128},{4... | collective-permute-start | bytes 196616 | tf_op jit(solution)/shard_map/track_scatter/ppermute | solution.py:245
  98.1 7.0 %collective-permute-start.11 = (bf16[2,64,256]{2,1,0:T(8,128)(2,1)S(1)}, bf16[2,64,256]{2,1,0:T(8,128)(2,1)S(1)}, u32[]{:S(2)}, u32[]{:S(2)}) collective-permute-start(bf16[2,64,256]{2,1,0:T(8,128)(2,1)S(1)} %get-tuple-element.34), channel_id=1, source_target_pairs={{48,0},{52,4},{56,8},{60,12},{49,1},{53,5},{57,9},{61,13},{50,2},{... | collective-permute-start | bytes 196616 | tf_op jit(solution)/shard_map/memory_grad_high/ppermute | solution.py:309
  98.8 29.0 %collective-permute-start.12 = (bf16[2,64,256]{2,1,0:T(8,128)(2,1)S(1)}, bf16[2,64,256]{2,1,0:T(8,128)(2,1)S(1)}, u32[]{:S(2)}, u32[]{:S(2)}) collective-permute-start(bf16[2,64,256]{2,1,0:T(8,128)(2,1)S(1)} %get-tuple-element.36), channel_id=1, source_target_pairs={{44,0},{40,4},{36,8},{32,12},{60,16},{56,20},{52,24},{48,28},{45,1... | collective-permute-start | bytes 196616 | tf_op jit(solution)/shard_map/memory_grad_high/ppermute | solution.py:309
  100.1 27.7 %collective-permute-start.13 = (bf16[2,64,256]{2,1,0:T(8,128)(2,1)S(1)}, bf16[2,64,256]{2,1,0:T(8,128)(2,1)S(1)}, u32[]{:S(2)}, u32[]{:S(2)}) collective-permute-start(bf16[2,64,256]{2,1,0:T(8,128)(2,1)S(1)} %get-tuple-element.35), channel_id=1, source_target_pairs={{16,0},{20,4},{24,8},{28,12},{32,16},{36,20},{40,24},{44,28},{48,3... | collective-permute-start | bytes 196616 | tf_op jit(solution)/shard_map/memory_grad_high/ppermute | solution.py:309

commit v4 on v3

--- a/solution.py
+++ b/solution.py
@@ -28,6 +28,14 @@
 
 def swapped(block, axis):
     return lax.ppermute(block, axis, [(0, 1), (1, 0)])
+
+
+def half_on(group, place, places):
+    return places - 1 - place
+
+
+def half_back(group, place, places):
+    return half_on(group, place, places) if group == 0 else (place - 1) % places
 
 
 def fill_mask(info, mask, block, groups):
@@ -145,8 +153,11 @@
         key_grad = (dot(slopes_half[...], queries[...], NN) * scale).astype(jnp.bfloat16)
         for g in range(2 * groups):
             cut = slice(g * half, (g + 1) * half)
-            memory_grad[g, index, :, :head] = key_grad[cut]
-            memory_grad[g, index, :, head:] = value_grad[cut]
+            moved = jnp.logical_and(2 * index == memory.shape[1], info[0] == memory.shape[1] - 1)
+            leaves = 2 * half_back(1, half_on(1, g // 2, groups), groups) + g % 2
+            to = jnp.where(moved, leaves, g)
+            memory_grad[to, index, :, :head] = key_grad[cut]
+            memory_grad[to, index, :, head:] = value_grad[cut]
         query_grad[...] += dot(keys, slopes_half[...], TN)
 
     visit(0, True)
@@ -213,18 +224,18 @@
     def of_song(array, index):
         return lax.dynamic_index_in_dim(array, index, 0, keepdims=False)
 
-    def places(step):
+    def places(step, half_ring):
         pairs = []
         for i in range(n_high - step):
             for j in range(n_low):
-                to = n_low - 1 - j if 2 * step == n_high else j
+                to = half_ring(i, j, n_low) if 2 * step == n_high else j
                 pairs.append((i * n_low + j, (i + step) * n_low + to))
         return pairs
 
     memory = time_memory[:, :, 0]
     with jax.named_scope("memory_high"):
         steps = range(n_high - 1, 0, -1)
-        held = [memory] + [lax.ppermute(memory, ("high", "low"), places(s)) for s in steps]
+        held = [memory] + [lax.ppermute(memory, ("high", "low"), places(s, half_on)) for s in steps]
     near = held[-1]
     with jax.named_scope("query_songs"):
         packed = jnp.concatenate([time_query[:, :, 0], time_grad_out[:, :, 0]], axis=2)
@@ -305,13 +316,13 @@
         sums = jnp.sum(parts.astype(jnp.float32), axis=0)
     with jax.named_scope("memory_grad_high"):
         gathered = sums[:, 0]
-        for s in steps:
-            back = lax.ppermute(
+        for s in (3, 2, 1):
+            came = lax.ppermute(
                 sums[:, n_high - s].astype(jnp.bfloat16),
                 ("high", "low"),
-                [(to, origin) for origin, to in places(s)],
+                [(to, origin) for origin, to in places(s, half_back)],
             )
-            gathered = gathered + back.astype(jnp.float32)
+            gathered = gathered + came.astype(jnp.float32)
         time_memory_grad = gathered.astype(jnp.bfloat16).reshape(time_memory.shape)
 
     def to_songs(array):

time: 129 us -> 128 us (level)
  the two profiles are of different devices: /device:TPU:129 before, /device:TPU:102 now
where the time goes in v4:
time: 128 us
  starting transfers between devices  70.8 us (55%)
  waiting for transfers between devices  41.7 us (33%)
  Pallas kernels  9.17 us (7%)
  other arithmetic  3.78 us (3%)
    ppermute x3, waiting for transfers between devices, body(): lax.ppermute(sums[:, n_high - s].astype(jnp.bfloat16), ('high', 'low'), [...  23.7 us
    ppermute x6, starting transfers between devices, across(): return lax.ppermute(array, 'track', [(i, i ^ bit) for i in range(tracks)])  22 us
    ppermute x3, starting transfers between devices, body(): lax.ppermute(memory, ('high', 'low'), places(s, half_on))  16.6 us
    ppermute x5, starting transfers between devices, swapped(): return lax.ppermute(block, axis, [(0, 1), (1, 0)])  13.3 us
    ppermute x6, waiting for transfers between devices, across(): return lax.ppermute(array, 'track', [(i, i ^ bit) for i in range(tracks)])  12.7 us
    all_to_all x1, starting transfers between devices, body(): lax.all_to_all(everyone.reshape(-1, *everyone.shape[2:]), ('low', 'core')...  8.95 us
    all_to_all x1, starting transfers between devices, body(): parts = lax.all_to_all(memory_grad, ('low', 'core'), 0, 0, tiled=True)  6.08 us
    pallas_call x1, Pallas kernels, body(): pl.pallas_call(functools.partial(grads_kernel, heads, head, scale), out_s...  4.33 us
  transfers between devices with their start and end apart: 19, of which 8 were waited for; matrix products, arithmetic and copies ran while one was open for 2% of the time, Pallas kernels for 4%

profile of v4, /device:TPU:102, one launch (start us, length us, event | category | flops | bytes accessed | tf_op | source)
XLA Modules:
  0.0 127.6 jit_solution(4067553128413484991)
XLA Ops:
  0.6 9.1 %collective-permute-start = (bf16[2,64,256]{2,1,0:T(8,128)(2,1)}, bf16[2,64,256]{2,1,0:T(8,128)(2,1)S(1)}, u32[]{:S(2)}, u32[]{:S(2)}) collective-permute-start(bf16[2,64,256]{2,1,0:T(8,128)(2,1)} %bitcast.68), channel_id=1, source_target_pairs={{0,16},{4,20},{8,24},{12,28},{16,32},{20,36},{24,40},{28,44},{32,4... | collective-permute-start | bytes 196616 | tf_op jit(solution)/shard_map/memory_high/ppermute | solution.py:238
  9.7 2.2 %collective-permute-start.3 = (bf16[2,64,256]{2,1,0:T(8,128)(2,1)}, bf16[2,64,256]{2,1,0:T(8,128)(2,1)S(1)}, u32[]{:S(2)}, u32[]{:S(2)}) collective-permute-start(bf16[2,64,256]{2,1,0:T(8,128)(2,1)} %bitcast.69), channel_id=1, source_target_pairs={{0,48},{4,52},{8,56},{12,60},{1,49},{5,53},{9,57},{13,61},{2,50},{... | collective-permute-start | bytes 196616 | tf_op jit(solution)/shard_map/memory_high/ppermute | solution.py:238
  12.0 5.3 %collective-permute-start.4 = (bf16[2,64,256]{2,1,0:T(8,128)(2,1)}, bf16[2,64,256]{2,1,0:T(8,128)(2,1)S(1)}, u32[]{:S(2)}, u32[]{:S(2)}) collective-permute-start(bf16[2,64,256]{2,1,0:T(8,128)(2,1)} %bitcast.70), channel_id=1, source_target_pairs={{0,44},{4,40},{8,36},{12,32},{16,60},{20,56},{24,52},{28,48},{1,45... | collective-permute-start | bytes 196616 | tf_op jit(solution)/shard_map/memory_high/ppermute | solution.py:238
  17.3 0.0 collective-permute-done
  17.3 0.0 collective-permute-done.3
  17.3 2.7 %collective-permute-done.4 = bf16[2,64,256]{2,1,0:T(8,128)(2,1)S(1)} collective-permute-done((bf16[2,64,256]{2,1,0:T(8,128)(2,1)}, bf16[2,64,256]{2,1,0:T(8,128)(2,1)S(1)}, u32[]{:S(2)}, u32[]{:S(2)}) %collective-permute-start.4) | collective-permute-done | bytes 65568 | tf_op jit(solution)/shard_map/memory_high/ppermute | solution.py:238
  20.1 0.9 broadcast_in_dim.10
  21.0 1.1 pad_maximum_fusion
  22.1 0.0 copy-start.3
  22.1 0.0 copy-start.4
  22.1 8.9 %all-to-all-start = ((bf16[8,4,64,256]{3,2,1,0:T(8,128)(2,1)}), bf16[8,4,64,256]{3,2,1,0:T(8,128)(2,1)S(1)}, u32[]{:S(2)}, u32[]{:S(2)}) async-start(bf16[8,4,64,256]{3,2,1,0:T(8,128)(2,1)} %bitcast.9), calls=%async_computation | async-start | bytes 2097152 | tf_op jit(solution)/shard_map/memory_low/all_to_all | solution.py:250
  31.1 0.0 copy-done.3
  31.1 0.0 copy-done.4
  31.1 0.0 copy-start.2
  31.2 2.1 %collective-permute-start.1 = (bf16[64,2048]{1,0:T(8,128)(2,1)S(1)}, bf16[64,2048]{1,0:T(8,128)(2,1)S(1)}, u32[]{:S(2)}, u32[]{:S(2)}) collective-permute-start(bf16[64,2048]{1,0:T(8,128)(2,1)S(1)} %get-tuple-element.31), channel_id=1, source_target_pairs={{0,1},{1,0},{2,3},{3,2},{4,5},{5,4},{6,7},{7,6},{8,9},{9,8},{10,11... | collective-permute-start | bytes 786440 | tf_op jit(solution)/shard_map/query_songs/ppermute | solution.py:30
  33.2 0.0 copy-done.2
  33.3 5.1 %collective-permute-start.6 = (bf16[1,128,256]{2,1,0:T(8,128)(2,1)S(1)}, bf16[1,128,256]{2,1,0:T(8,128)(2,1)S(1)}, u32[]{:S(2)}, u32[]{:S(2)}) collective-permute-start(bf16[1,128,256]{2,1,0:T(8,128)(2,1)S(1)} %bitcast.62), channel_id=1, source_target_pairs={{0,256},{64,320},{128,384},{192,448},{256,0},{320,64},{384,128},{4... | collective-permute-start | bytes 196616 | tf_op jit(solution)/shard_map/track_gather/ppermute | solution.py:256
  38.4 0.0 collective-permute-done.1
  38.4 2.6 %collective-permute-start.2 = (bf16[128,2048]{1,0:T(8,128)(2,1)S(1)}, bf16[128,2048]{1,0:T(8,128)(2,1)S(1)}, u32[]{:S(2)}, u32[]{:S(2)}) collective-permute-start(bf16[128,2048]{1,0:T(8,128)(2,1)S(1)} %pad_maximum_fusion.2.own), channel_id=1, source_target_pairs={{0,2},{2,0},{1,3},{3,1},{4,6},{6,4},{5,7},{7,5},{8,10},{10,8},{9,1... | collective-permute-start | bytes 1572872 | tf_op jit(solution)/shard_map/query_sides/ppermute | solution.py:30
  41.0 0.0 collective-permute-done.6
  41.1 3.3 %collective-permute-start.7 = (bf16[2,128,256]{2,1,0:T(8,128)(2,1)S(1)}, bf16[2,128,256]{2,1,0:T(8,128)(2,1)S(1)}, u32[]{:S(2)}, u32[]{:S(2)}) collective-permute-start(bf16[2,128,256]{2,1,0:T(8,128)(2,1)S(1)} %pad_maximum_fusion.5), channel_id=1, source_target_pairs={{0,128},{64,192},{128,0},{192,64},{256,384},{320,448},{384,256},{4... | collective-permute-start | bytes 393224 | tf_op jit(solution)/shard_map/track_gather/ppermute | solution.py:256
  44.4 5.3 %collective-permute-done.7 = bf16[2,128,256]{2,1,0:T(8,128)(2,1)S(1)} collective-permute-done((bf16[2,128,256]{2,1,0:T(8,128)(2,1)S(1)}, bf16[2,128,256]{2,1,0:T(8,128)(2,1)S(1)}, u32[]{:S(2)}, u32[]{:S(2)}) %collective-permute-start.7) | collective-permute-done | bytes 131104 | tf_op jit(solution)/shard_map/track_gather/ppermute | solution.py:256
  49.7 2.7 %collective-permute-start.8 = (bf16[4,128,256]{2,1,0:T(8,128)(2,1)S(1)}, bf16[4,128,256]{2,1,0:T(8,128)(2,1)S(1)}, u32[]{:S(2)}, u32[]{:S(2)}) collective-permute-start(bf16[4,128,256]{2,1,0:T(8,128)(2,1)S(1)} %pad_maximum_fusion.4), channel_id=1, source_target_pairs={{0,64},{64,0},{128,192},{192,128},{256,320},{320,256},{384,448},{4... | collective-permute-start | bytes 786440 | tf_op jit(solution)/shard_map/track_gather/ppermute | solution.py:256
  52.4 0.1 pad_add_fusion.info
  52.5 1.7 %collective-permute-done.2.other = bf16[128,2048]{1,0:T(8,128)(2,1)S(1)} collective-permute-done((bf16[128,2048]{1,0:T(8,128)(2,1)S(1)}, bf16[128,2048]{1,0:T(8,128)(2,1)S(1)}, u32[]{:S(2)}, u32[]{:S(2)}) %collective-permute-start.2) | collective-permute-done | bytes 524320 | tf_op jit(solution)/shard_map/query_sides/ppermute | solution.py:30
  54.2 0.8 all-to-all-done.memory
  55.1 2.3 %time_stats.1.mine = f32[3,8,256]{2,1,0:T(8,128)S(1)} custom-call(s32[4]{0:T(128)S(1)} %pad_add_fusion.info, bf16[128,2048]{1,0:T(8,128)(2,1)S(1)} %pad_maximum_fusion.2.own, bf16[128,2048]{1,0:T(8,128)(2,1)S(1)} %collective-permute-done.2.other, bf16[8,4,64,256]{3,2,1,0:T(8,128)(2,1)S(1)} %all-to-all-done.memory), custom_call_target="tpu_custom_call" | custom-call | tf_op jit(solution)/shard_map/time_stats/pallas_call | solution.py:263
  57.4 0.0 copy-start
  57.4 0.0 copy-start.1
  57.4 3.6 %collective-permute-start.5 = (f32[3,8,256]{2,1,0:T(8,128)S(1)}, f32[3,8,256]{2,1,0:T(8,128)S(1)}, u32[]{:S(2)}, u32[]{:S(2)}) collective-permute-start(f32[3,8,256]{2,1,0:T(8,128)S(1)} %time_stats.1.mine), channel_id=1, source_target_pairs={{0,2},{2,0},{1,3},{3,1},{4,6},{6,4},{5,7},{7,5},{8,10},{10,8},{9,1... | collective-permute-start | bytes 73736 | tf_op jit(solution)/shard_map/stats_sides/ppermute | solution.py:30
  61.0 0.0 collective-permute-done.8
  61.1 0.1 pad_maximum_fusion.3.memory
  61.1 0.0 copy-done
  61.1 0.0 copy-done.1
  61.1 2.5 %track_core.1 = (bf16[128,1024]{1,0:T(8,128)(2,1)}, bf16[8,128,256]{2,1,0:T(8,128)(2,1)S(1)}) custom-call(bf16[128,1024]{1,0:T(8,128)(2,1)S(1)} %bitcast.59, bf16[128,1024]{1,0:T(8,128)(2,1)S(1)} %bitcast.60, bf16[8,128,256]{2,1,0:T(8,128)(2,1)S(1)} %pad_maximum_fusion.3.memory), custom_call_target="tpu_custom_call" | custom-call | tf_op jit(solution)/shard_map/track_core/pallas_call | solution.py:278
  63.6 0.0 collective-permute-done.5.theirs
  63.6 4.3 %time_grads.1 = (f32[128,1024]{1,0:T(8,128)S(1)}, bf16[128,1024]{1,0:T(8,128)(2,1)S(1)}, bf16[8,4,64,256]{3,2,1,0:T(8,128)(2,1)}) custom-call(s32[4]{0:T(128)S(1)} %pad_add_fusion.info, bf16[128,2048]{1,0:T(8,128)(2,1)S(1)} %pad_maximum_fusion.2.own, bf16[128,2048]{1,0:T(8,128)(2,1)S(1)} %collective-permute-done.2.other, ...), custom_call_target="tpu_custom_call" | custom-call | tf_op jit(solution)/shard_map/time_grads/pallas_call | solution.py:290
  68.0 6.1 %all-to-all-start.1 = ((bf16[8,4,64,256]{3,2,1,0:T(8,128)(2,1)}), bf16[8,4,64,256]{3,2,1,0:T(8,128)(2,1)S(1)}, u32[]{:S(2)}, u32[]{:S(2)}) async-start(bf16[8,4,64,256]{3,2,1,0:T(8,128)(2,1)} %get-tuple-element.20), calls=%async_computation.1 | async-start | bytes 2097152 | tf_op jit(solution)/shard_map/memory_grad_low/all_to_all | solution.py:314
  74.1 2.7 %collective-permute-start.14 = (bf16[4,128,256]{2,1,0:T(8,128)(2,1)S(1)}, bf16[4,128,256]{2,1,0:T(8,128)(2,1)S(1)}, u32[]{:S(2)}, u32[]{:S(2)}) collective-permute-start(bf16[4,128,256]{2,1,0:T(8,128)(2,1)S(1)} %split.21), channel_id=1, source_target_pairs={{0,64},{64,0},{128,192},{192,128},{256,320},{320,256},{384,448},{4... | collective-permute-start | bytes 786440 | tf_op jit(solution)/shard_map/track_scatter/ppermute | solution.py:256
  76.8 3.1 %collective-permute-start.9 = (bf16[128,1024]{1,0:T(8,128)(2,1)S(1)}, bf16[128,1024]{1,0:T(8,128)(2,1)S(1)}, u32[]{:S(2)}, u32[]{:S(2)}) collective-permute-start(bf16[128,1024]{1,0:T(8,128)(2,1)S(1)} %get-tuple-element.19), channel_id=1, source_target_pairs={{0,2},{2,0},{1,3},{3,1},{4,6},{6,4},{5,7},{7,5},{8,10},{10,8},{9,1... | collective-permute-start | bytes 786440 | tf_op jit(solution)/shard_map/query_grad_sides/ppermute | solution.py:30
  79.9 4.4 %collective-permute-done.14 = bf16[4,128,256]{2,1,0:T(8,128)(2,1)S(1)} collective-permute-done((bf16[4,128,256]{2,1,0:T(8,128)(2,1)S(1)}, bf16[4,128,256]{2,1,0:T(8,128)(2,1)S(1)}, u32[]{:S(2)}, u32[]{:S(2)}) %collective-permute-start.14) | collective-permute-done | bytes 262176 | tf_op jit(solution)/shard_map/track_scatter/ppermute | solution.py:256
  84.3 0.1 convert_add_fusion
  84.4 3.3 %collective-permute-start.15 = (bf16[2,128,256]{2,1,0:T(8,128)(2,1)S(1)}, bf16[2,128,256]{2,1,0:T(8,128)(2,1)S(1)}, u32[]{:S(2)}, u32[]{:S(2)}) collective-permute-start(bf16[2,128,256]{2,1,0:T(8,128)(2,1)S(1)} %split.37), channel_id=1, source_target_pairs={{0,128},{64,192},{128,0},{192,64},{256,384},{320,448},{384,256},{4... | collective-permute-start | bytes 393224 | tf_op jit(solution)/shard_map/track_scatter/ppermute | solution.py:256
  87.7 0.0 collective-permute-done.9
  87.7 0.1 add_convert_fusion
  87.8 1.9 %collective-permute-start.10 = (bf16[64,1024]{1,0:T(8,128)(2,1)S(1)}, bf16[64,1024]{1,0:T(8,128)(2,1)S(1)}, u32[]{:S(2)}, u32[]{:S(2)}) collective-permute-start(bf16[64,1024]{1,0:T(8,128)(2,1)S(1)} %slice.28), channel_id=1, source_target_pairs={{0,1},{1,0},{2,3},{3,2},{4,5},{5,4},{6,7},{7,6},{8,9},{9,8},{10,11... | collective-permute-start | bytes 393224 | tf_op jit(solution)/shard_map/query_grad_songs/ppermute | solution.py:30
  89.7 3.0 %collective-permute-done.15 = bf16[2,128,256]{2,1,0:T(8,128)(2,1)S(1)} collective-permute-done((bf16[2,128,256]{2,1,0:T(8,128)(2,1)S(1)}, bf16[2,128,256]{2,1,0:T(8,128)(2,1)S(1)}, u32[]{:S(2)}, u32[]{:S(2)}) %collective-permute-start.15) | collective-permute-done | bytes 131104 | tf_op jit(solution)/shard_map/track_scatter/ppermute | solution.py:256
  92.8 4.8 %collective-permute-start.16 = (bf16[1,128,256]{2,1,0:T(8,128)(2,1)S(1)}, bf16[1,128,256]{2,1,0:T(8,128)(2,1)S(1)}, u32[]{:S(2)}, u32[]{:S(2)}) collective-permute-start(bf16[1,128,256]{2,1,0:T(8,128)(2,1)S(1)} %split.38), channel_id=1, source_target_pairs={{0,256},{64,320},{128,384},{192,448},{256,0},{320,64},{384,128},{4... | collective-permute-start | bytes 196616 | tf_op jit(solution)/shard_map/track_scatter/ppermute | solution.py:256
  97.6 0.0 collective-permute-done.10
  97.7 0.7 maximum_bitcast_fusion
  98.4 0.0 all-to-all-done.1
  98.4 0.2 convert_reduce_fusion
  98.6 1.3 %collective-permute-start.11 = (bf16[2,64,256]{2,1,0:T(8,128)(2,1)S(1)}, bf16[2,64,256]{2,1,0:T(8,128)(2,1)S(1)}, u32[]{:S(2)}, u32[]{:S(2)}) collective-permute-start(bf16[2,64,256]{2,1,0:T(8,128)(2,1)S(1)} %get-tuple-element.34), channel_id=1, source_target_pairs={{48,0},{52,4},{56,8},{60,12},{49,1},{53,5},{57,9},{61,13},{50,2},{... | collective-permute-start | bytes 196616 | tf_op jit(solution)/shard_map/memory_grad_high/ppermute | solution.py:320
  99.9 1.3 %collective-permute-start.12 = (bf16[2,64,256]{2,1,0:T(8,128)(2,1)S(1)}, bf16[2,64,256]{2,1,0:T(8,128)(2,1)S(1)}, u32[]{:S(2)}, u32[]{:S(2)}) collective-permute-start(bf16[2,64,256]{2,1,0:T(8,128)(2,1)S(1)} %get-tuple-element.36), channel_id=1, source_target_pairs={{44,0},{40,4},{36,8},{32,12},{60,16},{48,20},{52,24},{56,28},{45,1... | collective-permute-start | bytes 196616 | tf_op jit(solution)/shard_map/memory_grad_high/ppermute | solution.py:320
  101.2 1.3 %collective-permute-start.13 = (bf16[2,64,256]{2,1,0:T(8,128)(2,1)S(1)}, bf16[2,64,256]{2,1,0:T(8,128)(2,1)S(1)}, u32[]{:S(2)}, u32[]{:S(2)}) collective-permute-start(bf16[2,64,256]{2,1,0:T(8,128)(2,1)S(1)} %get-tuple-element.35), channel_id=1, source_target_pairs={{16,0},{20,4},{24,8},{28,12},{32,16},{36,20},{40,24},{44,28},{48,3... | collective-permute-start | bytes 196616 | tf_op jit(solution)/shard_map/memory_grad_high/ppermute | solution.py:320
  102.5 0.0 collective-permute-done.16
  102.5 0.6 fusion
  103.2 21.9 %collective-permute-done.11 = bf16[2,64,256]{2,1,0:T(8,128)(2,1)S(1)} collective-permute-done((bf16[2,64,256]{2,1,0:T(8,128)(2,1)S(1)}, bf16[2,64,256]{2,1,0:T(8,128)(2,1)S(1)}, u32[]{:S(2)}, u32[]{:S(2)}) %collective-permute-start.11) | collective-permute-done | bytes 65568 | tf_op jit(solution)/shard_map/memory_grad_high/ppermute | solution.py:320
  125.0 1.9 %collective-permute-done.12 = bf16[2,64,256]{2,1,0:T(8,128)(2,1)S(1)} collective-permute-done((bf16[2,64,256]{2,1,0:T(8,128)(2,1)S(1)}, bf16[2,64,256]{2,1,0:T(8,128)(2,1)S(1)}, u32[]{:S(2)}, u32[]{:S(2)}) %collective-permute-start.12) | collective-permute-done | bytes 65568 | tf_op jit(solution)/shard_map/memory_grad_high/ppermute | solution.py:320
  126.9 0.0 collective-permute-done.13
  126.9 0.7 fusion.5
  (16 shorter events, 0.4 us)
Async XLA Ops:
  0.6 16.6 %collective-permute-start = (bf16[2,64,256]{2,1,0:T(8,128)(2,1)}, bf16[2,64,256]{2,1,0:T(8,128)(2,1)S(1)}, u32[]{:S(2)}, u32[]{:S(2)}) collective-permute-start(bf16[2,64,256]{2,1,0:T(8,128)(2,1)} %bitcast.68), channel_id=1, source_target_pairs={{0,16},{4,20},{8,24},{12,28},{16,32},{20,36},{24,40},{28,44},{32,4... | collective-permute-start | bytes 196616 | tf_op jit(solution)/shard_map/memory_high/ppermute | solution.py:238
  9.7 7.6 %collective-permute-start.3 = (bf16[2,64,256]{2,1,0:T(8,128)(2,1)}, bf16[2,64,256]{2,1,0:T(8,128)(2,1)S(1)}, u32[]{:S(2)}, u32[]{:S(2)}) collective-permute-start(bf16[2,64,256]{2,1,0:T(8,128)(2,1)} %bitcast.69), channel_id=1, source_target_pairs={{0,48},{4,52},{8,56},{12,60},{1,49},{5,53},{9,57},{13,61},{2,50},{... | collective-permute-start | bytes 196616 | tf_op jit(solution)/shard_map/memory_high/ppermute | solution.py:238
  12.0 8.0 %collective-permute-start.4 = (bf16[2,64,256]{2,1,0:T(8,128)(2,1)}, bf16[2,64,256]{2,1,0:T(8,128)(2,1)S(1)}, u32[]{:S(2)}, u32[]{:S(2)}) collective-permute-start(bf16[2,64,256]{2,1,0:T(8,128)(2,1)} %bitcast.70), channel_id=1, source_target_pairs={{0,44},{4,40},{8,36},{12,32},{16,60},{20,56},{24,52},{28,48},{1,45... | collective-permute-start | bytes 196616 | tf_op jit(solution)/shard_map/memory_high/ppermute | solution.py:238
  22.1 9.0 %copy-start.3 = (bf16[2,64,1,1024]{3,1,2,0:T(8,128)(2,1)S(1)}, bf16[2,64,1,1024]{3,1,2,0:T(8,128)(2,1)}, u32[]{:S(2)}) copy-start(bf16[2,64,1,1024]{3,1,2,0:T(8,128)(2,1)} %param.8) | copy-start | bytes 786436
  22.1 9.0 %copy-start.4 = (bf16[2,64,1,1024]{3,1,2,0:T(8,128)(2,1)S(1)}, bf16[2,64,1,1024]{3,1,2,0:T(8,128)(2,1)}, u32[]{:S(2)}) copy-start(bf16[2,64,1,1024]{3,1,2,0:T(8,128)(2,1)} %param.6) | copy-start | bytes 786436
  22.1 32.9 %all-to-all-start = ((bf16[8,4,64,256]{3,2,1,0:T(8,128)(2,1)}), bf16[8,4,64,256]{3,2,1,0:T(8,128)(2,1)S(1)}, u32[]{:S(2)}, u32[]{:S(2)}) async-start(bf16[8,4,64,256]{3,2,1,0:T(8,128)(2,1)} %bitcast.9), calls=%async_computation | async-start | bytes 2097152 | tf_op jit(solution)/shard_map/memory_low/all_to_all | solution.py:250
  31.1 2.2 %copy-start.2 = (bf16[2,64,1,256]{3,1,2,0:T(8,128)(2,1)S(1)}, bf16[2,64,1,256]{3,1,2,0:T(8,128)(2,1)}, u32[]{:S(2)}) copy-start(bf16[2,64,1,256]{3,1,2,0:T(8,128)(2,1)} %param.10) | copy-start | bytes 196612
  31.2 7.2 %collective-permute-start.1 = (bf16[64,2048]{1,0:T(8,128)(2,1)S(1)}, bf16[64,2048]{1,0:T(8,128)(2,1)S(1)}, u32[]{:S(2)}, u32[]{:S(2)}) collective-permute-start(bf16[64,2048]{1,0:T(8,128)(2,1)S(1)} %get-tuple-element.31), channel_id=1, source_target_pairs={{0,1},{1,0},{2,3},{3,2},{4,5},{5,4},{6,7},{7,6},{8,9},{9,8},{10,11... | collective-permute-start | bytes 786440 | tf_op jit(solution)/shard_map/query_songs/ppermute | solution.py:30
  33.3 7.8 %collective-permute-start.6 = (bf16[1,128,256]{2,1,0:T(8,128)(2,1)S(1)}, bf16[1,128,256]{2,1,0:T(8,128)(2,1)S(1)}, u32[]{:S(2)}, u32[]{:S(2)}) collective-permute-start(bf16[1,128,256]{2,1,0:T(8,128)(2,1)S(1)} %bitcast.62), channel_id=1, source_target_pairs={{0,256},{64,320},{128,384},{192,448},{256,0},{320,64},{384,128},{4... | collective-permute-start | bytes 196616 | tf_op jit(solution)/shard_map/track_gather/ppermute | solution.py:256
  38.4 15.8 %collective-permute-start.2 = (bf16[128,2048]{1,0:T(8,128)(2,1)S(1)}, bf16[128,2048]{1,0:T(8,128)(2,1)S(1)}, u32[]{:S(2)}, u32[]{:S(2)}) collective-permute-start(bf16[128,2048]{1,0:T(8,128)(2,1)S(1)} %pad_maximum_fusion.2.own), channel_id=1, source_target_pairs={{0,2},{2,0},{1,3},{3,1},{4,6},{6,4},{5,7},{7,5},{8,10},{10,8},{9,1... | collective-permute-start | bytes 1572872 | tf_op jit(solution)/shard_map/query_sides/ppermute | solution.py:30
  41.1 8.6 %collective-permute-start.7 = (bf16[2,128,256]{2,1,0:T(8,128)(2,1)S(1)}, bf16[2,128,256]{2,1,0:T(8,128)(2,1)S(1)}, u32[]{:S(2)}, u32[]{:S(2)}) collective-permute-start(bf16[2,128,256]{2,1,0:T(8,128)(2,1)S(1)} %pad_maximum_fusion.5), channel_id=1, source_target_pairs={{0,128},{64,192},{128,0},{192,64},{256,384},{320,448},{384,256},{4... | collective-permute-start | bytes 393224 | tf_op jit(solution)/shard_map/track_gather/ppermute | solution.py:256
  49.7 11.4 %collective-permute-start.8 = (bf16[4,128,256]{2,1,0:T(8,128)(2,1)S(1)}, bf16[4,128,256]{2,1,0:T(8,128)(2,1)S(1)}, u32[]{:S(2)}, u32[]{:S(2)}) collective-permute-start(bf16[4,128,256]{2,1,0:T(8,128)(2,1)S(1)} %pad_maximum_fusion.4), channel_id=1, source_target_pairs={{0,64},{64,0},{128,192},{192,128},{256,320},{320,256},{384,448},{4... | collective-permute-start | bytes 786440 | tf_op jit(solution)/shard_map/track_gather/ppermute | solution.py:256
  57.4 3.7 %copy-start = (bf16[2,64,1,1024]{3,1,2,0:T(8,128)(2,1)S(1)}, bf16[2,64,1,1024]{3,1,2,0:T(8,128)(2,1)}, u32[]{:S(2)}) copy-start(bf16[2,64,1,1024]{3,1,2,0:T(8,128)(2,1)} %param.9) | copy-start | bytes 786436
  57.4 3.7 %copy-start.1 = (bf16[2,64,1,1024]{3,1,2,0:T(8,128)(2,1)S(1)}, bf16[2,64,1,1024]{3,1,2,0:T(8,128)(2,1)}, u32[]{:S(2)}) copy-start(bf16[2,64,1,1024]{3,1,2,0:T(8,128)(2,1)} %param.11) | copy-start | bytes 786436
  57.4 6.2 %collective-permute-start.5 = (f32[3,8,256]{2,1,0:T(8,128)S(1)}, f32[3,8,256]{2,1,0:T(8,128)S(1)}, u32[]{:S(2)}, u32[]{:S(2)}) collective-permute-start(f32[3,8,256]{2,1,0:T(8,128)S(1)} %time_stats.1.mine), channel_id=1, source_target_pairs={{0,2},{2,0},{1,3},{3,1},{4,6},{6,4},{5,7},{7,5},{8,10},{10,8},{9,1... | collective-permute-start | bytes 73736 | tf_op jit(solution)/shard_map/stats_sides/ppermute | solution.py:30
  68.0 30.4 %all-to-all-start.1 = ((bf16[8,4,64,256]{3,2,1,0:T(8,128)(2,1)}), bf16[8,4,64,256]{3,2,1,0:T(8,128)(2,1)S(1)}, u32[]{:S(2)}, u32[]{:S(2)}) async-start(bf16[8,4,64,256]{3,2,1,0:T(8,128)(2,1)} %get-tuple-element.20), calls=%async_computation.1 | async-start | bytes 2097152 | tf_op jit(solution)/shard_map/memory_grad_low/all_to_all | solution.py:314
  74.1 10.3 %collective-permute-start.14 = (bf16[4,128,256]{2,1,0:T(8,128)(2,1)S(1)}, bf16[4,128,256]{2,1,0:T(8,128)(2,1)S(1)}, u32[]{:S(2)}, u32[]{:S(2)}) collective-permute-start(bf16[4,128,256]{2,1,0:T(8,128)(2,1)S(1)} %split.21), channel_id=1, source_target_pairs={{0,64},{64,0},{128,192},{192,128},{256,320},{320,256},{384,448},{4... | collective-permute-start | bytes 786440 | tf_op jit(solution)/shard_map/track_scatter/ppermute | solution.py:256
  76.8 10.9 %collective-permute-start.9 = (bf16[128,1024]{1,0:T(8,128)(2,1)S(1)}, bf16[128,1024]{1,0:T(8,128)(2,1)S(1)}, u32[]{:S(2)}, u32[]{:S(2)}) collective-permute-start(bf16[128,1024]{1,0:T(8,128)(2,1)S(1)} %get-tuple-element.19), channel_id=1, source_target_pairs={{0,2},{2,0},{1,3},{3,1},{4,6},{6,4},{5,7},{7,5},{8,10},{10,8},{9,1... | collective-permute-start | bytes 786440 | tf_op jit(solution)/shard_map/query_grad_sides/ppermute | solution.py:30
  84.4 8.4 %collective-permute-start.15 = (bf16[2,128,256]{2,1,0:T(8,128)(2,1)S(1)}, bf16[2,128,256]{2,1,0:T(8,128)(2,1)S(1)}, u32[]{:S(2)}, u32[]{:S(2)}) collective-permute-start(bf16[2,128,256]{2,1,0:T(8,128)(2,1)S(1)} %split.37), channel_id=1, source_target_pairs={{0,128},{64,192},{128,0},{192,64},{256,384},{320,448},{384,256},{4... | collective-permute-start | bytes 393224 | tf_op jit(solution)/shard_map/track_scatter/ppermute | solution.py:256
  87.8 9.8 %collective-permute-start.10 = (bf16[64,1024]{1,0:T(8,128)(2,1)S(1)}, bf16[64,1024]{1,0:T(8,128)(2,1)S(1)}, u32[]{:S(2)}, u32[]{:S(2)}) collective-permute-start(bf16[64,1024]{1,0:T(8,128)(2,1)S(1)} %slice.28), channel_id=1, source_target_pairs={{0,1},{1,0},{2,3},{3,2},{4,5},{5,4},{6,7},{7,6},{8,9},{9,8},{10,11... | collective-permute-start | bytes 393224 | tf_op jit(solution)/shard_map/query_grad_songs/ppermute | solution.py:30
  92.8 9.7 %collective-permute-start.16 = (bf16[1,128,256]{2,1,0:T(8,128)(2,1)S(1)}, bf16[1,128,256]{2,1,0:T(8,128)(2,1)S(1)}, u32[]{:S(2)}, u32[]{:S(2)}) collective-permute-start(bf16[1,128,256]{2,1,0:T(8,128)(2,1)S(1)} %split.38), channel_id=1, source_target_pairs={{0,256},{64,320},{128,384},{192,448},{256,0},{320,64},{384,128},{4... | collective-permute-start | bytes 196616 | tf_op jit(solution)/shard_map/track_scatter/ppermute | solution.py:256
  98.6 26.4 %collective-permute-start.11 = (bf16[2,64,256]{2,1,0:T(8,128)(2,1)S(1)}, bf16[2,64,256]{2,1,0:T(8,128)(2,1)S(1)}, u32[]{:S(2)}, u32[]{:S(2)}) collective-permute-start(bf16[2,64,256]{2,1,0:T(8,128)(2,1)S(1)} %get-tuple-element.34), channel_id=1, source_target_pairs={{48,0},{52,4},{56,8},{60,12},{49,1},{53,5},{57,9},{61,13},{50,2},{... | collective-permute-start | bytes 196616 | tf_op jit(solution)/shard_map/memory_grad_high/ppermute | solution.py:320
  99.9 27.0 %collective-permute-start.12 = (bf16[2,64,256]{2,1,0:T(8,128)(2,1)S(1)}, bf16[2,64,256]{2,1,0:T(8,128)(2,1)S(1)}, u32[]{:S(2)}, u32[]{:S(2)}) collective-permute-start(bf16[2,64,256]{2,1,0:T(8,128)(2,1)S(1)} %get-tuple-element.36), channel_id=1, source_target_pairs={{44,0},{40,4},{36,8},{32,12},{60,16},{48,20},{52,24},{56,28},{45,1... | collective-permute-start | bytes 196616 | tf_op jit(solution)/shard_map/memory_grad_high/ppermute | solution.py:320
  101.2 25.7 %collective-permute-start.13 = (bf16[2,64,256]{2,1,0:T(8,128)(2,1)S(1)}, bf16[2,64,256]{2,1,0:T(8,128)(2,1)S(1)}, u32[]{:S(2)}, u32[]{:S(2)}) collective-permute-start(bf16[2,64,256]{2,1,0:T(8,128)(2,1)S(1)} %get-tuple-element.35), channel_id=1, source_target_pairs={{16,0},{20,4},{24,8},{28,12},{32,16},{36,20},{40,24},{44,28},{48,3... | collective-permute-start | bytes 196616 | tf_op jit(solution)/shard_map/memory_grad_high/ppermute | solution.py:320

commit v5 on v4

--- a/solution.py
+++ b/solution.py
@@ -239,7 +239,7 @@
     near = held[-1]
     with jax.named_scope("query_songs"):
         packed = jnp.concatenate([time_query[:, :, 0], time_grad_out[:, :, 0]], axis=2)
-        packed = after(packed, near)
+        packed = after(packed, held[1])
         own = jnp.concatenate(
             [of_song(packed, core), swapped(of_song(packed, 1 - core), "core")], axis=0
         )

time: 128 us -> 127 us (level)
  the two profiles are of different devices: /device:TPU:102 before, /device:TPU:129 now
where the time goes in v5:
time: 127 us
  starting transfers between devices  68.9 us (54%)
  waiting for transfers between devices  38.8 us (31%)
  Pallas kernels  13.1 us (10%)
  other arithmetic  3.78 us (3%)
    ppermute x6, starting transfers between devices, across(): return lax.ppermute(array, 'track', [(i, i ^ bit) for i in range(tracks)])  25.1 us
    ppermute x3, waiting for transfers between devices, body(): lax.ppermute(sums[:, n_high - s].astype(jnp.bfloat16), ('high', 'low'), [...  21.6 us
    ppermute x5, starting transfers between devices, swapped(): return lax.ppermute(block, axis, [(0, 1), (1, 0)])  13.5 us
    ppermute x3, starting transfers between devices, body(): lax.ppermute(memory, ('high', 'low'), places(s, half_on))  11.9 us
    all_to_all x1, starting transfers between devices, body(): lax.all_to_all(everyone.reshape(-1, *everyone.shape[2:]), ('low', 'core')...  8.82 us
    pallas_call x1, Pallas kernels, body(): pl.pallas_call(functools.partial(grads_kernel, heads, head, scale), out_s...  6.94 us
    ppermute x6, waiting for transfers between devices, across(): return lax.ppermute(array, 'track', [(i, i ^ bit) for i in range(tracks)])  6.45 us
    ppermute x3, starting transfers between devices, body(): lax.ppermute(sums[:, n_high - s].astype(jnp.bfloat16), ('high', 'low'), [...  5.07 us
  transfers between devices with their start and end apart: 19, of which 7 were waited for; matrix products, arithmetic and copies ran while one was open for 2% of the time, Pallas kernels for 5%

profile of v5, /device:TPU:129, one launch (start us, length us, event | category | flops | bytes accessed | tf_op | source)
XLA Modules:
  0.0 126.7 jit_solution(55695415409175231)
XLA Ops:
  0.6 0.7 collective-permute-start
  1.3 8.8 %collective-permute-start.4 = (bf16[2,64,256]{2,1,0:T(8,128)(2,1)}, bf16[2,64,256]{2,1,0:T(8,128)(2,1)S(1)}, u32[]{:S(2)}, u32[]{:S(2)}) collective-permute-start(bf16[2,64,256]{2,1,0:T(8,128)(2,1)} %bitcast.69), channel_id=1, source_target_pairs={{0,16},{4,20},{8,24},{12,28},{16,32},{20,36},{24,40},{28,44},{32,4... | collective-permute-start | bytes 196616 | tf_op jit(solution)/shard_map/memory_high/ppermute | solution.py:238
  10.1 2.4 %collective-permute-start.3 = (bf16[2,64,256]{2,1,0:T(8,128)(2,1)}, bf16[2,64,256]{2,1,0:T(8,128)(2,1)S(1)}, u32[]{:S(2)}, u32[]{:S(2)}) collective-permute-start(bf16[2,64,256]{2,1,0:T(8,128)(2,1)} %bitcast.70), channel_id=1, source_target_pairs={{0,44},{4,40},{8,36},{12,32},{16,60},{20,56},{24,52},{28,48},{1,45... | collective-permute-start | bytes 196616 | tf_op jit(solution)/shard_map/memory_high/ppermute | solution.py:238
  12.5 0.0 collective-permute-done
  12.6 2.4 %collective-permute-done.4 = bf16[2,64,256]{2,1,0:T(8,128)(2,1)S(1)} collective-permute-done((bf16[2,64,256]{2,1,0:T(8,128)(2,1)}, bf16[2,64,256]{2,1,0:T(8,128)(2,1)S(1)}, u32[]{:S(2)}, u32[]{:S(2)}) %collective-permute-start.4) | collective-permute-done | bytes 65568 | tf_op jit(solution)/shard_map/memory_high/ppermute | solution.py:238
  15.0 0.0 collective-permute-done.3
  15.1 0.9 broadcast_in_dim.10
  15.9 1.1 pad_maximum_fusion
  17.1 0.0 copy-start.3
  17.1 0.0 copy-start.4
  17.1 8.8 %all-to-all-start = ((bf16[8,4,64,256]{3,2,1,0:T(8,128)(2,1)}), bf16[8,4,64,256]{3,2,1,0:T(8,128)(2,1)S(1)}, u32[]{:S(2)}, u32[]{:S(2)}) async-start(bf16[8,4,64,256]{3,2,1,0:T(8,128)(2,1)} %bitcast.9), calls=%async_computation | async-start | bytes 2097152 | tf_op jit(solution)/shard_map/memory_low/all_to_all | solution.py:250
  25.9 0.0 copy-done.3
  25.9 0.0 copy-done.4
  25.9 0.0 copy-start.2
  26.0 1.9 %collective-permute-start.1 = (bf16[64,2048]{1,0:T(8,128)(2,1)S(1)}, bf16[64,2048]{1,0:T(8,128)(2,1)S(1)}, u32[]{:S(2)}, u32[]{:S(2)}) collective-permute-start(bf16[64,2048]{1,0:T(8,128)(2,1)S(1)} %get-tuple-element.31), channel_id=1, source_target_pairs={{0,1},{1,0},{2,3},{3,2},{4,5},{5,4},{6,7},{7,6},{8,9},{9,8},{10,11... | collective-permute-start | bytes 786440 | tf_op jit(solution)/shard_map/query_songs/ppermute | solution.py:30
  27.9 0.0 copy-done.2
  28.0 4.8 %collective-permute-start.6 = (bf16[1,128,256]{2,1,0:T(8,128)(2,1)S(1)}, bf16[1,128,256]{2,1,0:T(8,128)(2,1)S(1)}, u32[]{:S(2)}, u32[]{:S(2)}) collective-permute-start(bf16[1,128,256]{2,1,0:T(8,128)(2,1)S(1)} %bitcast.62), channel_id=1, source_target_pairs={{0,256},{64,320},{128,384},{192,448},{256,0},{320,64},{384,128},{4... | collective-permute-start | bytes 196616 | tf_op jit(solution)/shard_map/track_gather/ppermute | solution.py:256
  32.8 0.0 collective-permute-done.1
  32.8 2.3 %collective-permute-start.2 = (bf16[128,2048]{1,0:T(8,128)(2,1)S(1)}, bf16[128,2048]{1,0:T(8,128)(2,1)S(1)}, u32[]{:S(2)}, u32[]{:S(2)}) collective-permute-start(bf16[128,2048]{1,0:T(8,128)(2,1)S(1)} %pad_maximum_fusion.2.own), channel_id=1, source_target_pairs={{0,2},{2,0},{1,3},{3,1},{4,6},{6,4},{5,7},{7,5},{8,10},{10,8},{9,1... | collective-permute-start | bytes 1572872 | tf_op jit(solution)/shard_map/query_sides/ppermute | solution.py:30
  35.2 0.0 collective-permute-done.6
  35.2 4.7 %collective-permute-start.7 = (bf16[2,128,256]{2,1,0:T(8,128)(2,1)S(1)}, bf16[2,128,256]{2,1,0:T(8,128)(2,1)S(1)}, u32[]{:S(2)}, u32[]{:S(2)}) collective-permute-start(bf16[2,128,256]{2,1,0:T(8,128)(2,1)S(1)} %pad_maximum_fusion.5), channel_id=1, source_target_pairs={{0,128},{64,192},{128,0},{192,64},{256,384},{320,448},{384,256},{4... | collective-permute-start | bytes 393224 | tf_op jit(solution)/shard_map/track_gather/ppermute | solution.py:256
  39.9 2.7 %collective-permute-done.7 = bf16[2,128,256]{2,1,0:T(8,128)(2,1)S(1)} collective-permute-done((bf16[2,128,256]{2,1,0:T(8,128)(2,1)S(1)}, bf16[2,128,256]{2,1,0:T(8,128)(2,1)S(1)}, u32[]{:S(2)}, u32[]{:S(2)}) %collective-permute-start.7) | collective-permute-done | bytes 131104 | tf_op jit(solution)/shard_map/track_gather/ppermute | solution.py:256
  42.6 3.3 %collective-permute-start.8 = (bf16[4,128,256]{2,1,0:T(8,128)(2,1)S(1)}, bf16[4,128,256]{2,1,0:T(8,128)(2,1)S(1)}, u32[]{:S(2)}, u32[]{:S(2)}) collective-permute-start(bf16[4,128,256]{2,1,0:T(8,128)(2,1)S(1)} %pad_maximum_fusion.4), channel_id=1, source_target_pairs={{0,64},{64,0},{128,192},{192,128},{256,320},{320,256},{384,448},{4... | collective-permute-start | bytes 786440 | tf_op jit(solution)/shard_map/track_gather/ppermute | solution.py:256
  45.9 0.1 pad_add_fusion.info
  45.9 1.5 %collective-permute-done.2.other = bf16[128,2048]{1,0:T(8,128)(2,1)S(1)} collective-permute-done((bf16[128,2048]{1,0:T(8,128)(2,1)S(1)}, bf16[128,2048]{1,0:T(8,128)(2,1)S(1)}, u32[]{:S(2)}, u32[]{:S(2)}) %collective-permute-start.2) | collective-permute-done | bytes 524320 | tf_op jit(solution)/shard_map/query_sides/ppermute | solution.py:30
  47.4 4.2 %all-to-all-done.memory = bf16[8,4,64,256]{3,2,1,0:T(8,128)(2,1)S(1)} async-done(((bf16[8,4,64,256]{3,2,1,0:T(8,128)(2,1)}), bf16[8,4,64,256]{3,2,1,0:T(8,128)(2,1)S(1)}, u32[]{:S(2)}, u32[]{:S(2)}) %all-to-all-start) | async-done | bytes 1048608 | tf_op jit(solution)/shard_map/memory_low/all_to_all | solution.py:250
  51.6 3.6 %time_stats.1.mine = f32[3,8,256]{2,1,0:T(8,128)S(1)} custom-call(s32[4]{0:T(128)S(1)} %pad_add_fusion.info, bf16[128,2048]{1,0:T(8,128)(2,1)S(1)} %pad_maximum_fusion.2.own, bf16[128,2048]{1,0:T(8,128)(2,1)S(1)} %collective-permute-done.2.other, bf16[8,4,64,256]{3,2,1,0:T(8,128)(2,1)S(1)} %all-to-all-done.memory), custom_call_target="tpu_custom_call" | custom-call | tf_op jit(solution)/shard_map/time_stats/pallas_call | solution.py:263
  55.3 0.0 copy-start
  55.3 0.0 copy-start.1
  55.3 3.4 %collective-permute-start.5 = (f32[3,8,256]{2,1,0:T(8,128)S(1)}, f32[3,8,256]{2,1,0:T(8,128)S(1)}, u32[]{:S(2)}, u32[]{:S(2)}) collective-permute-start(f32[3,8,256]{2,1,0:T(8,128)S(1)} %time_stats.1.mine), channel_id=1, source_target_pairs={{0,2},{2,0},{1,3},{3,1},{4,6},{6,4},{5,7},{7,5},{8,10},{10,8},{9,1... | collective-permute-start | bytes 73736 | tf_op jit(solution)/shard_map/stats_sides/ppermute | solution.py:30
  58.7 0.0 collective-permute-done.8
  58.7 0.1 pad_maximum_fusion.3.memory
  58.7 0.0 copy-done
  58.7 0.0 copy-done.1
  58.7 2.5 %track_core.1 = (bf16[128,1024]{1,0:T(8,128)(2,1)}, bf16[8,128,256]{2,1,0:T(8,128)(2,1)S(1)}) custom-call(bf16[128,1024]{1,0:T(8,128)(2,1)S(1)} %bitcast.59, bf16[128,1024]{1,0:T(8,128)(2,1)S(1)} %bitcast.60, bf16[8,128,256]{2,1,0:T(8,128)(2,1)S(1)} %pad_maximum_fusion.3.memory), custom_call_target="tpu_custom_call" | custom-call | tf_op jit(solution)/shard_map/track_core/pallas_call | solution.py:278
  61.2 0.0 collective-permute-done.5.theirs
  61.2 6.9 %time_grads.1 = (f32[128,1024]{1,0:T(8,128)S(1)}, bf16[128,1024]{1,0:T(8,128)(2,1)S(1)}, bf16[8,4,64,256]{3,2,1,0:T(8,128)(2,1)}) custom-call(s32[4]{0:T(128)S(1)} %pad_add_fusion.info, bf16[128,2048]{1,0:T(8,128)(2,1)S(1)} %pad_maximum_fusion.2.own, bf16[128,2048]{1,0:T(8,128)(2,1)S(1)} %collective-permute-done.2.other, ...), custom_call_target="tpu_custom_call" | custom-call | tf_op jit(solution)/shard_map/time_grads/pallas_call | solution.py:290
  68.2 4.6 %all-to-all-start.1 = ((bf16[8,4,64,256]{3,2,1,0:T(8,128)(2,1)}), bf16[8,4,64,256]{3,2,1,0:T(8,128)(2,1)S(1)}, u32[]{:S(2)}, u32[]{:S(2)}) async-start(bf16[8,4,64,256]{3,2,1,0:T(8,128)(2,1)} %get-tuple-element.20), calls=%async_computation.1 | async-start | bytes 2097152 | tf_op jit(solution)/shard_map/memory_grad_low/all_to_all | solution.py:314
  72.8 3.2 %collective-permute-start.14 = (bf16[4,128,256]{2,1,0:T(8,128)(2,1)S(1)}, bf16[4,128,256]{2,1,0:T(8,128)(2,1)S(1)}, u32[]{:S(2)}, u32[]{:S(2)}) collective-permute-start(bf16[4,128,256]{2,1,0:T(8,128)(2,1)S(1)} %split.21), channel_id=1, source_target_pairs={{0,64},{64,0},{128,192},{192,128},{256,320},{320,256},{384,448},{4... | collective-permute-start | bytes 786440 | tf_op jit(solution)/shard_map/track_scatter/ppermute | solution.py:256
  76.0 2.8 %collective-permute-start.9 = (bf16[128,1024]{1,0:T(8,128)(2,1)S(1)}, bf16[128,1024]{1,0:T(8,128)(2,1)S(1)}, u32[]{:S(2)}, u32[]{:S(2)}) collective-permute-start(bf16[128,1024]{1,0:T(8,128)(2,1)S(1)} %get-tuple-element.19), channel_id=1, source_target_pairs={{0,2},{2,0},{1,3},{3,1},{4,6},{6,4},{5,7},{7,5},{8,10},{10,8},{9,1... | collective-permute-start | bytes 786440 | tf_op jit(solution)/shard_map/query_grad_sides/ppermute | solution.py:30
  78.8 3.7 %collective-permute-done.14 = bf16[4,128,256]{2,1,0:T(8,128)(2,1)S(1)} collective-permute-done((bf16[4,128,256]{2,1,0:T(8,128)(2,1)S(1)}, bf16[4,128,256]{2,1,0:T(8,128)(2,1)S(1)}, u32[]{:S(2)}, u32[]{:S(2)}) %collective-permute-start.14) | collective-permute-done | bytes 262176 | tf_op jit(solution)/shard_map/track_scatter/ppermute | solution.py:256
  82.6 0.1 convert_add_fusion
  82.7 4.7 %collective-permute-start.15 = (bf16[2,128,256]{2,1,0:T(8,128)(2,1)S(1)}, bf16[2,128,256]{2,1,0:T(8,128)(2,1)S(1)}, u32[]{:S(2)}, u32[]{:S(2)}) collective-permute-start(bf16[2,128,256]{2,1,0:T(8,128)(2,1)S(1)} %split.37), channel_id=1, source_target_pairs={{0,128},{64,192},{128,0},{192,64},{256,384},{320,448},{384,256},{4... | collective-permute-start | bytes 393224 | tf_op jit(solution)/shard_map/track_scatter/ppermute | solution.py:256
  87.3 0.0 collective-permute-done.9
  87.3 0.1 add_convert_fusion
  87.4 3.1 %collective-permute-start.10 = (bf16[64,1024]{1,0:T(8,128)(2,1)S(1)}, bf16[64,1024]{1,0:T(8,128)(2,1)S(1)}, u32[]{:S(2)}, u32[]{:S(2)}) collective-permute-start(bf16[64,1024]{1,0:T(8,128)(2,1)S(1)} %slice.28), channel_id=1, source_target_pairs={{0,1},{1,0},{2,3},{3,2},{4,5},{5,4},{6,7},{7,6},{8,9},{9,8},{10,11... | collective-permute-start | bytes 393224 | tf_op jit(solution)/shard_map/query_grad_songs/ppermute | solution.py:30
  90.5 0.0 collective-permute-done.15
  90.5 4.5 %collective-permute-start.16 = (bf16[1,128,256]{2,1,0:T(8,128)(2,1)S(1)}, bf16[1,128,256]{2,1,0:T(8,128)(2,1)S(1)}, u32[]{:S(2)}, u32[]{:S(2)}) collective-permute-start(bf16[1,128,256]{2,1,0:T(8,128)(2,1)S(1)} %split.38), channel_id=1, source_target_pairs={{0,256},{64,320},{128,384},{192,448},{256,0},{320,64},{384,128},{4... | collective-permute-start | bytes 196616 | tf_op jit(solution)/shard_map/track_scatter/ppermute | solution.py:256
  95.1 0.0 collective-permute-done.10
  95.1 0.7 maximum_bitcast_fusion
  95.9 2.7 %all-to-all-done.1 = bf16[8,4,64,256]{3,2,1,0:T(8,128)(2,1)S(1)} async-done(((bf16[8,4,64,256]{3,2,1,0:T(8,128)(2,1)}), bf16[8,4,64,256]{3,2,1,0:T(8,128)(2,1)S(1)}, u32[]{:S(2)}, u32[]{:S(2)}) %all-to-all-start.1) | async-done | bytes 1048608 | tf_op jit(solution)/shard_map/memory_grad_low/all_to_all | solution.py:314
  98.5 0.2 convert_reduce_fusion
  98.8 0.7 collective-permute-start.11
  99.4 1.3 %collective-permute-start.12 = (bf16[2,64,256]{2,1,0:T(8,128)(2,1)S(1)}, bf16[2,64,256]{2,1,0:T(8,128)(2,1)S(1)}, u32[]{:S(2)}, u32[]{:S(2)}) collective-permute-start(bf16[2,64,256]{2,1,0:T(8,128)(2,1)S(1)} %get-tuple-element.36), channel_id=1, source_target_pairs={{44,0},{40,4},{36,8},{32,12},{60,16},{48,20},{52,24},{56,28},{45,1... | collective-permute-start | bytes 196616 | tf_op jit(solution)/shard_map/memory_grad_high/ppermute | solution.py:320
  100.7 3.1 %collective-permute-start.13 = (bf16[2,64,256]{2,1,0:T(8,128)(2,1)S(1)}, bf16[2,64,256]{2,1,0:T(8,128)(2,1)S(1)}, u32[]{:S(2)}, u32[]{:S(2)}) collective-permute-start(bf16[2,64,256]{2,1,0:T(8,128)(2,1)S(1)} %get-tuple-element.35), channel_id=1, source_target_pairs={{16,0},{20,4},{24,8},{28,12},{32,16},{36,20},{40,24},{44,28},{48,3... | collective-permute-start | bytes 196616 | tf_op jit(solution)/shard_map/memory_grad_high/ppermute | solution.py:320
  103.8 0.0 collective-permute-done.16
  103.8 0.6 fusion
  104.5 0.0 collective-permute-done.11
  104.5 21.6 %collective-permute-done.12 = bf16[2,64,256]{2,1,0:T(8,128)(2,1)S(1)} collective-permute-done((bf16[2,64,256]{2,1,0:T(8,128)(2,1)S(1)}, bf16[2,64,256]{2,1,0:T(8,128)(2,1)S(1)}, u32[]{:S(2)}, u32[]{:S(2)}) %collective-permute-start.12) | collective-permute-done | bytes 65568 | tf_op jit(solution)/shard_map/memory_grad_high/ppermute | solution.py:320
  126.1 0.0 collective-permute-done.13
  126.1 0.7 fusion.5
  (16 shorter events, 0.4 us)
Async XLA Ops:
  0.6 11.9 %collective-permute-start = (bf16[2,64,256]{2,1,0:T(8,128)(2,1)}, bf16[2,64,256]{2,1,0:T(8,128)(2,1)S(1)}, u32[]{:S(2)}, u32[]{:S(2)}) collective-permute-start(bf16[2,64,256]{2,1,0:T(8,128)(2,1)} %bitcast.68), channel_id=1, source_target_pairs={{0,48},{4,52},{8,56},{12,60},{1,49},{5,53},{9,57},{13,61},{2,50},{... | collective-permute-start | bytes 196616 | tf_op jit(solution)/shard_map/memory_high/ppermute | solution.py:238
  1.3 13.7 %collective-permute-start.4 = (bf16[2,64,256]{2,1,0:T(8,128)(2,1)}, bf16[2,64,256]{2,1,0:T(8,128)(2,1)S(1)}, u32[]{:S(2)}, u32[]{:S(2)}) collective-permute-start(bf16[2,64,256]{2,1,0:T(8,128)(2,1)} %bitcast.69), channel_id=1, source_target_pairs={{0,16},{4,20},{8,24},{12,28},{16,32},{20,36},{24,40},{28,44},{32,4... | collective-permute-start | bytes 196616 | tf_op jit(solution)/shard_map/memory_high/ppermute | solution.py:238
  10.1 4.9 %collective-permute-start.3 = (bf16[2,64,256]{2,1,0:T(8,128)(2,1)}, bf16[2,64,256]{2,1,0:T(8,128)(2,1)S(1)}, u32[]{:S(2)}, u32[]{:S(2)}) collective-permute-start(bf16[2,64,256]{2,1,0:T(8,128)(2,1)} %bitcast.70), channel_id=1, source_target_pairs={{0,44},{4,40},{8,36},{12,32},{16,60},{20,56},{24,52},{28,48},{1,45... | collective-permute-start | bytes 196616 | tf_op jit(solution)/shard_map/memory_high/ppermute | solution.py:238
  17.1 8.8 %copy-start.3 = (bf16[2,64,1,1024]{3,1,2,0:T(8,128)(2,1)S(1)}, bf16[2,64,1,1024]{3,1,2,0:T(8,128)(2,1)}, u32[]{:S(2)}) copy-start(bf16[2,64,1,1024]{3,1,2,0:T(8,128)(2,1)} %param.8) | copy-start | bytes 786436
  17.1 8.8 %copy-start.4 = (bf16[2,64,1,1024]{3,1,2,0:T(8,128)(2,1)S(1)}, bf16[2,64,1,1024]{3,1,2,0:T(8,128)(2,1)}, u32[]{:S(2)}) copy-start(bf16[2,64,1,1024]{3,1,2,0:T(8,128)(2,1)} %param.6) | copy-start | bytes 786436
  17.1 34.5 %all-to-all-start = ((bf16[8,4,64,256]{3,2,1,0:T(8,128)(2,1)}), bf16[8,4,64,256]{3,2,1,0:T(8,128)(2,1)S(1)}, u32[]{:S(2)}, u32[]{:S(2)}) async-start(bf16[8,4,64,256]{3,2,1,0:T(8,128)(2,1)} %bitcast.9), calls=%async_computation | async-start | bytes 2097152 | tf_op jit(solution)/shard_map/memory_low/all_to_all | solution.py:250
  25.9 2.0 %copy-start.2 = (bf16[2,64,1,256]{3,1,2,0:T(8,128)(2,1)S(1)}, bf16[2,64,1,256]{3,1,2,0:T(8,128)(2,1)}, u32[]{:S(2)}) copy-start(bf16[2,64,1,256]{3,1,2,0:T(8,128)(2,1)} %param.10) | copy-start | bytes 196612
  26.0 6.8 %collective-permute-start.1 = (bf16[64,2048]{1,0:T(8,128)(2,1)S(1)}, bf16[64,2048]{1,0:T(8,128)(2,1)S(1)}, u32[]{:S(2)}, u32[]{:S(2)}) collective-permute-start(bf16[64,2048]{1,0:T(8,128)(2,1)S(1)} %get-tuple-element.31), channel_id=1, source_target_pairs={{0,1},{1,0},{2,3},{3,2},{4,5},{5,4},{6,7},{7,6},{8,9},{9,8},{10,11... | collective-permute-start | bytes 786440 | tf_op jit(solution)/shard_map/query_songs/ppermute | solution.py:30
  28.0 7.2 %collective-permute-start.6 = (bf16[1,128,256]{2,1,0:T(8,128)(2,1)S(1)}, bf16[1,128,256]{2,1,0:T(8,128)(2,1)S(1)}, u32[]{:S(2)}, u32[]{:S(2)}) collective-permute-start(bf16[1,128,256]{2,1,0:T(8,128)(2,1)S(1)} %bitcast.62), channel_id=1, source_target_pairs={{0,256},{64,320},{128,384},{192,448},{256,0},{320,64},{384,128},{4... | collective-permute-start | bytes 196616 | tf_op jit(solution)/shard_map/track_gather/ppermute | solution.py:256
  32.8 14.6 %collective-permute-start.2 = (bf16[128,2048]{1,0:T(8,128)(2,1)S(1)}, bf16[128,2048]{1,0:T(8,128)(2,1)S(1)}, u32[]{:S(2)}, u32[]{:S(2)}) collective-permute-start(bf16[128,2048]{1,0:T(8,128)(2,1)S(1)} %pad_maximum_fusion.2.own), channel_id=1, source_target_pairs={{0,2},{2,0},{1,3},{3,1},{4,6},{6,4},{5,7},{7,5},{8,10},{10,8},{9,1... | collective-permute-start | bytes 1572872 | tf_op jit(solution)/shard_map/query_sides/ppermute | solution.py:30
  35.2 7.4 %collective-permute-start.7 = (bf16[2,128,256]{2,1,0:T(8,128)(2,1)S(1)}, bf16[2,128,256]{2,1,0:T(8,128)(2,1)S(1)}, u32[]{:S(2)}, u32[]{:S(2)}) collective-permute-start(bf16[2,128,256]{2,1,0:T(8,128)(2,1)S(1)} %pad_maximum_fusion.5), channel_id=1, source_target_pairs={{0,128},{64,192},{128,0},{192,64},{256,384},{320,448},{384,256},{4... | collective-permute-start | bytes 393224 | tf_op jit(solution)/shard_map/track_gather/ppermute | solution.py:256
  42.6 16.1 %collective-permute-start.8 = (bf16[4,128,256]{2,1,0:T(8,128)(2,1)S(1)}, bf16[4,128,256]{2,1,0:T(8,128)(2,1)S(1)}, u32[]{:S(2)}, u32[]{:S(2)}) collective-permute-start(bf16[4,128,256]{2,1,0:T(8,128)(2,1)S(1)} %pad_maximum_fusion.4), channel_id=1, source_target_pairs={{0,64},{64,0},{128,192},{192,128},{256,320},{320,256},{384,448},{4... | collective-permute-start | bytes 786440 | tf_op jit(solution)/shard_map/track_gather/ppermute | solution.py:256
  55.3 3.5 %copy-start = (bf16[2,64,1,1024]{3,1,2,0:T(8,128)(2,1)S(1)}, bf16[2,64,1,1024]{3,1,2,0:T(8,128)(2,1)}, u32[]{:S(2)}) copy-start(bf16[2,64,1,1024]{3,1,2,0:T(8,128)(2,1)} %param.9) | copy-start | bytes 786436
  55.3 3.5 %copy-start.1 = (bf16[2,64,1,1024]{3,1,2,0:T(8,128)(2,1)S(1)}, bf16[2,64,1,1024]{3,1,2,0:T(8,128)(2,1)}, u32[]{:S(2)}) copy-start(bf16[2,64,1,1024]{3,1,2,0:T(8,128)(2,1)} %param.11) | copy-start | bytes 786436
  55.3 6.0 %collective-permute-start.5 = (f32[3,8,256]{2,1,0:T(8,128)S(1)}, f32[3,8,256]{2,1,0:T(8,128)S(1)}, u32[]{:S(2)}, u32[]{:S(2)}) collective-permute-start(f32[3,8,256]{2,1,0:T(8,128)S(1)} %time_stats.1.mine), channel_id=1, source_target_pairs={{0,2},{2,0},{1,3},{3,1},{4,6},{6,4},{5,7},{7,5},{8,10},{10,8},{9,1... | collective-permute-start | bytes 73736 | tf_op jit(solution)/shard_map/stats_sides/ppermute | solution.py:30
  68.2 30.3 %all-to-all-start.1 = ((bf16[8,4,64,256]{3,2,1,0:T(8,128)(2,1)}), bf16[8,4,64,256]{3,2,1,0:T(8,128)(2,1)S(1)}, u32[]{:S(2)}, u32[]{:S(2)}) async-start(bf16[8,4,64,256]{3,2,1,0:T(8,128)(2,1)} %get-tuple-element.20), calls=%async_computation.1 | async-start | bytes 2097152 | tf_op jit(solution)/shard_map/memory_grad_low/all_to_all | solution.py:314
  72.8 9.8 %collective-permute-start.14 = (bf16[4,128,256]{2,1,0:T(8,128)(2,1)S(1)}, bf16[4,128,256]{2,1,0:T(8,128)(2,1)S(1)}, u32[]{:S(2)}, u32[]{:S(2)}) collective-permute-start(bf16[4,128,256]{2,1,0:T(8,128)(2,1)S(1)} %split.21), channel_id=1, source_target_pairs={{0,64},{64,0},{128,192},{192,128},{256,320},{320,256},{384,448},{4... | collective-permute-start | bytes 786440 | tf_op jit(solution)/shard_map/track_scatter/ppermute | solution.py:256
  76.0 11.4 %collective-permute-start.9 = (bf16[128,1024]{1,0:T(8,128)(2,1)S(1)}, bf16[128,1024]{1,0:T(8,128)(2,1)S(1)}, u32[]{:S(2)}, u32[]{:S(2)}) collective-permute-start(bf16[128,1024]{1,0:T(8,128)(2,1)S(1)} %get-tuple-element.19), channel_id=1, source_target_pairs={{0,2},{2,0},{1,3},{3,1},{4,6},{6,4},{5,7},{7,5},{8,10},{10,8},{9,1... | collective-permute-start | bytes 786440 | tf_op jit(solution)/shard_map/query_grad_sides/ppermute | solution.py:30
  82.7 7.8 %collective-permute-start.15 = (bf16[2,128,256]{2,1,0:T(8,128)(2,1)S(1)}, bf16[2,128,256]{2,1,0:T(8,128)(2,1)S(1)}, u32[]{:S(2)}, u32[]{:S(2)}) collective-permute-start(bf16[2,128,256]{2,1,0:T(8,128)(2,1)S(1)} %split.37), channel_id=1, source_target_pairs={{0,128},{64,192},{128,0},{192,64},{256,384},{320,448},{384,256},{4... | collective-permute-start | bytes 393224 | tf_op jit(solution)/shard_map/track_scatter/ppermute | solution.py:256
  87.4 7.7 %collective-permute-start.10 = (bf16[64,1024]{1,0:T(8,128)(2,1)S(1)}, bf16[64,1024]{1,0:T(8,128)(2,1)S(1)}, u32[]{:S(2)}, u32[]{:S(2)}) collective-permute-start(bf16[64,1024]{1,0:T(8,128)(2,1)S(1)} %slice.28), channel_id=1, source_target_pairs={{0,1},{1,0},{2,3},{3,2},{4,5},{5,4},{6,7},{7,6},{8,9},{9,8},{10,11... | collective-permute-start | bytes 393224 | tf_op jit(solution)/shard_map/query_grad_songs/ppermute | solution.py:30
  90.5 13.3 %collective-permute-start.16 = (bf16[1,128,256]{2,1,0:T(8,128)(2,1)S(1)}, bf16[1,128,256]{2,1,0:T(8,128)(2,1)S(1)}, u32[]{:S(2)}, u32[]{:S(2)}) collective-permute-start(bf16[1,128,256]{2,1,0:T(8,128)(2,1)S(1)} %split.38), channel_id=1, source_target_pairs={{0,256},{64,320},{128,384},{192,448},{256,0},{320,64},{384,128},{4... | collective-permute-start | bytes 196616 | tf_op jit(solution)/shard_map/track_scatter/ppermute | solution.py:256
  98.8 5.7 %collective-permute-start.11 = (bf16[2,64,256]{2,1,0:T(8,128)(2,1)S(1)}, bf16[2,64,256]{2,1,0:T(8,128)(2,1)S(1)}, u32[]{:S(2)}, u32[]{:S(2)}) collective-permute-start(bf16[2,64,256]{2,1,0:T(8,128)(2,1)S(1)} %get-tuple-element.34), channel_id=1, source_target_pairs={{48,0},{52,4},{56,8},{60,12},{49,1},{53,5},{57,9},{61,13},{50,2},{... | collective-permute-start | bytes 196616 | tf_op jit(solution)/shard_map/memory_grad_high/ppermute | solution.py:320
  99.4 26.6 %collective-permute-start.12 = (bf16[2,64,256]{2,1,0:T(8,128)(2,1)S(1)}, bf16[2,64,256]{2,1,0:T(8,128)(2,1)S(1)}, u32[]{:S(2)}, u32[]{:S(2)}) collective-permute-start(bf16[2,64,256]{2,1,0:T(8,128)(2,1)S(1)} %get-tuple-element.36), channel_id=1, source_target_pairs={{44,0},{40,4},{36,8},{32,12},{60,16},{48,20},{52,24},{56,28},{45,1... | collective-permute-start | bytes 196616 | tf_op jit(solution)/shard_map/memory_grad_high/ppermute | solution.py:320
  100.7 25.3 %collective-permute-start.13 = (bf16[2,64,256]{2,1,0:T(8,128)(2,1)S(1)}, bf16[2,64,256]{2,1,0:T(8,128)(2,1)S(1)}, u32[]{:S(2)}, u32[]{:S(2)}) collective-permute-start(bf16[2,64,256]{2,1,0:T(8,128)(2,1)S(1)} %get-tuple-element.35), channel_id=1, source_target_pairs={{16,0},{20,4},{24,8},{28,12},{32,16},{36,20},{40,24},{44,28},{48,3... | collective-permute-start | bytes 196616 | tf_op jit(solution)/shard_map/memory_grad_high/ppermute | solution.py:320

commit v6 on v5

--- a/solution.py
+++ b/solution.py
@@ -141,14 +141,16 @@
         values = group_of(memory, index, head, 1)
         for h in range(heads):
             cut = slice(h * rows, (h + 1) * rows)
-            scores = dot(keys, queries[cut], NT)
-            products = dot(values, grads[cut], NT)
-            if masked:
-                scores = scores + mask[...]
-            weights = jnp.exp2(scores * factor - shift[h : h + 1])
-            slopes = weights * (products - delta[h : h + 1])
-            weights_half[:, cut] = weights.astype(jnp.bfloat16)
-            slopes_half[:, cut] = slopes.astype(jnp.bfloat16)
+            for begin in range(0, keys.shape[0], rows):
+                part = slice(begin, begin + rows)
+                scores = dot(keys[part], queries[cut], NT)
+                products = dot(values[part], grads[cut], NT)
+                if masked:
+                    scores = scores + mask[part]
+                weights = jnp.exp2(scores * factor - shift[h : h + 1])
+                slopes = weights * (products - delta[h : h + 1])
+                weights_half[part, cut] = weights.astype(jnp.bfloat16)
+                slopes_half[part, cut] = slopes.astype(jnp.bfloat16)
         value_grad = dot(weights_half[...], grads[...], NN).astype(jnp.bfloat16)
         key_grad = (dot(slopes_half[...], queries[...], NN) * scale).astype(jnp.bfloat16)
         for g in range(2 * groups):

time: 127 us -> 127 us (level)
  no operation moved by 1% of the time
where the time goes in v6:
time: 127 us
  starting transfers between devices  68.9 us (54%)
  waiting for transfers between devices  38.8 us (31%)
  Pallas kernels  13 us (10%)
  other arithmetic  3.78 us (3%)
    ppermute x6, starting transfers between devices, across(): return lax.ppermute(array, 'track', [(i, i ^ bit) for i in range(tracks)])  25.1 us
    ppermute x3, waiting for transfers between devices, body(): lax.ppermute(sums[:, n_high - s].astype(jnp.bfloat16), ('high', 'low'), [...  21.6 us
    ppermute x5, starting transfers between devices, swapped(): return lax.ppermute(block, axis, [(0, 1), (1, 0)])  13.5 us
    ppermute x3, starting transfers between devices, body(): lax.ppermute(memory, ('high', 'low'), places(s, half_on))  11.9 us
    all_to_all x1, starting transfers between devices, body(): lax.all_to_all(everyone.reshape(-1, *everyone.shape[2:]), ('low', 'core')...  8.82 us
    pallas_call x1, Pallas kernels, body(): pl.pallas_call(functools.partial(grads_kernel, heads, head, scale), out_s...  6.9 us
    ppermute x6, waiting for transfers between devices, across(): return lax.ppermute(array, 'track', [(i, i ^ bit) for i in range(tracks)])  6.45 us
    ppermute x3, starting transfers between devices, body(): lax.ppermute(sums[:, n_high - s].astype(jnp.bfloat16), ('high', 'low'), [...  5.07 us
  transfers between devices with their start and end apart: 19, of which 7 were waited for; matrix products, arithmetic and copies ran while one was open for 2% of the time, Pallas kernels for 5%

profile of v6, /device:TPU:129, one launch (start us, length us, event | category | flops | bytes accessed | tf_op | source)
XLA Modules:
  0.0 126.7 jit_solution(6570428734579026294)
XLA Ops:
  0.6 0.7 collective-permute-start
  1.3 8.8 %collective-permute-start.4 = (bf16[2,64,256]{2,1,0:T(8,128)(2,1)}, bf16[2,64,256]{2,1,0:T(8,128)(2,1)S(1)}, u32[]{:S(2)}, u32[]{:S(2)}) collective-permute-start(bf16[2,64,256]{2,1,0:T(8,128)(2,1)} %bitcast.69), channel_id=1, source_target_pairs={{0,16},{4,20},{8,24},{12,28},{16,32},{20,36},{24,40},{28,44},{32,4... | collective-permute-start | bytes 196616 | tf_op jit(solution)/shard_map/memory_high/ppermute | solution.py:240
  10.1 2.4 %collective-permute-start.3 = (bf16[2,64,256]{2,1,0:T(8,128)(2,1)}, bf16[2,64,256]{2,1,0:T(8,128)(2,1)S(1)}, u32[]{:S(2)}, u32[]{:S(2)}) collective-permute-start(bf16[2,64,256]{2,1,0:T(8,128)(2,1)} %bitcast.70), channel_id=1, source_target_pairs={{0,44},{4,40},{8,36},{12,32},{16,60},{20,56},{24,52},{28,48},{1,45... | collective-permute-start | bytes 196616 | tf_op jit(solution)/shard_map/memory_high/ppermute | solution.py:240
  12.5 0.0 collective-permute-done
  12.6 2.4 %collective-permute-done.4 = bf16[2,64,256]{2,1,0:T(8,128)(2,1)S(1)} collective-permute-done((bf16[2,64,256]{2,1,0:T(8,128)(2,1)}, bf16[2,64,256]{2,1,0:T(8,128)(2,1)S(1)}, u32[]{:S(2)}, u32[]{:S(2)}) %collective-permute-start.4) | collective-permute-done | bytes 65568 | tf_op jit(solution)/shard_map/memory_high/ppermute | solution.py:240
  15.0 0.0 collective-permute-done.3
  15.1 0.9 broadcast_in_dim.10
  15.9 1.1 pad_maximum_fusion
  17.1 0.0 copy-start.3
  17.1 0.0 copy-start.4
  17.1 8.8 %all-to-all-start = ((bf16[8,4,64,256]{3,2,1,0:T(8,128)(2,1)}), bf16[8,4,64,256]{3,2,1,0:T(8,128)(2,1)S(1)}, u32[]{:S(2)}, u32[]{:S(2)}) async-start(bf16[8,4,64,256]{3,2,1,0:T(8,128)(2,1)} %bitcast.9), calls=%async_computation | async-start | bytes 2097152 | tf_op jit(solution)/shard_map/memory_low/all_to_all | solution.py:252
  25.9 0.0 copy-done.3
  25.9 0.0 copy-done.4
  25.9 0.0 copy-start.2
  26.0 1.9 %collective-permute-start.1 = (bf16[64,2048]{1,0:T(8,128)(2,1)S(1)}, bf16[64,2048]{1,0:T(8,128)(2,1)S(1)}, u32[]{:S(2)}, u32[]{:S(2)}) collective-permute-start(bf16[64,2048]{1,0:T(8,128)(2,1)S(1)} %get-tuple-element.31), channel_id=1, source_target_pairs={{0,1},{1,0},{2,3},{3,2},{4,5},{5,4},{6,7},{7,6},{8,9},{9,8},{10,11... | collective-permute-start | bytes 786440 | tf_op jit(solution)/shard_map/query_songs/ppermute | solution.py:30
  27.9 0.0 copy-done.2
  28.0 4.8 %collective-permute-start.6 = (bf16[1,128,256]{2,1,0:T(8,128)(2,1)S(1)}, bf16[1,128,256]{2,1,0:T(8,128)(2,1)S(1)}, u32[]{:S(2)}, u32[]{:S(2)}) collective-permute-start(bf16[1,128,256]{2,1,0:T(8,128)(2,1)S(1)} %bitcast.62), channel_id=1, source_target_pairs={{0,256},{64,320},{128,384},{192,448},{256,0},{320,64},{384,128},{4... | collective-permute-start | bytes 196616 | tf_op jit(solution)/shard_map/track_gather/ppermute | solution.py:258
  32.8 0.0 collective-permute-done.1
  32.8 2.3 %collective-permute-start.2 = (bf16[128,2048]{1,0:T(8,128)(2,1)S(1)}, bf16[128,2048]{1,0:T(8,128)(2,1)S(1)}, u32[]{:S(2)}, u32[]{:S(2)}) collective-permute-start(bf16[128,2048]{1,0:T(8,128)(2,1)S(1)} %pad_maximum_fusion.2.own), channel_id=1, source_target_pairs={{0,2},{2,0},{1,3},{3,1},{4,6},{6,4},{5,7},{7,5},{8,10},{10,8},{9,1... | collective-permute-start | bytes 1572872 | tf_op jit(solution)/shard_map/query_sides/ppermute | solution.py:30
  35.2 0.0 collective-permute-done.6
  35.2 4.7 %collective-permute-start.7 = (bf16[2,128,256]{2,1,0:T(8,128)(2,1)S(1)}, bf16[2,128,256]{2,1,0:T(8,128)(2,1)S(1)}, u32[]{:S(2)}, u32[]{:S(2)}) collective-permute-start(bf16[2,128,256]{2,1,0:T(8,128)(2,1)S(1)} %pad_maximum_fusion.5), channel_id=1, source_target_pairs={{0,128},{64,192},{128,0},{192,64},{256,384},{320,448},{384,256},{4... | collective-permute-start | bytes 393224 | tf_op jit(solution)/shard_map/track_gather/ppermute | solution.py:258
  39.9 2.7 %collective-permute-done.7 = bf16[2,128,256]{2,1,0:T(8,128)(2,1)S(1)} collective-permute-done((bf16[2,128,256]{2,1,0:T(8,128)(2,1)S(1)}, bf16[2,128,256]{2,1,0:T(8,128)(2,1)S(1)}, u32[]{:S(2)}, u32[]{:S(2)}) %collective-permute-start.7) | collective-permute-done | bytes 131104 | tf_op jit(solution)/shard_map/track_gather/ppermute | solution.py:258
  42.6 3.3 %collective-permute-start.8 = (bf16[4,128,256]{2,1,0:T(8,128)(2,1)S(1)}, bf16[4,128,256]{2,1,0:T(8,128)(2,1)S(1)}, u32[]{:S(2)}, u32[]{:S(2)}) collective-permute-start(bf16[4,128,256]{2,1,0:T(8,128)(2,1)S(1)} %pad_maximum_fusion.4), channel_id=1, source_target_pairs={{0,64},{64,0},{128,192},{192,128},{256,320},{320,256},{384,448},{4... | collective-permute-start | bytes 786440 | tf_op jit(solution)/shard_map/track_gather/ppermute | solution.py:258
  45.9 0.1 pad_add_fusion.info
  45.9 1.5 %collective-permute-done.2.other = bf16[128,2048]{1,0:T(8,128)(2,1)S(1)} collective-permute-done((bf16[128,2048]{1,0:T(8,128)(2,1)S(1)}, bf16[128,2048]{1,0:T(8,128)(2,1)S(1)}, u32[]{:S(2)}, u32[]{:S(2)}) %collective-permute-start.2) | collective-permute-done | bytes 524320 | tf_op jit(solution)/shard_map/query_sides/ppermute | solution.py:30
  47.4 4.2 %all-to-all-done.memory = bf16[8,4,64,256]{3,2,1,0:T(8,128)(2,1)S(1)} async-done(((bf16[8,4,64,256]{3,2,1,0:T(8,128)(2,1)}), bf16[8,4,64,256]{3,2,1,0:T(8,128)(2,1)S(1)}, u32[]{:S(2)}, u32[]{:S(2)}) %all-to-all-start) | async-done | bytes 1048608 | tf_op jit(solution)/shard_map/memory_low/all_to_all | solution.py:252
  51.6 3.6 %time_stats.1.mine = f32[3,8,256]{2,1,0:T(8,128)S(1)} custom-call(s32[4]{0:T(128)S(1)} %pad_add_fusion.info, bf16[128,2048]{1,0:T(8,128)(2,1)S(1)} %pad_maximum_fusion.2.own, bf16[128,2048]{1,0:T(8,128)(2,1)S(1)} %collective-permute-done.2.other, bf16[8,4,64,256]{3,2,1,0:T(8,128)(2,1)S(1)} %all-to-all-done.memory), custom_call_target="tpu_custom_call" | custom-call | tf_op jit(solution)/shard_map/time_stats/pallas_call | solution.py:265
  55.3 0.0 copy-start
  55.3 0.0 copy-start.1
  55.3 3.4 %collective-permute-start.5 = (f32[3,8,256]{2,1,0:T(8,128)S(1)}, f32[3,8,256]{2,1,0:T(8,128)S(1)}, u32[]{:S(2)}, u32[]{:S(2)}) collective-permute-start(f32[3,8,256]{2,1,0:T(8,128)S(1)} %time_stats.1.mine), channel_id=1, source_target_pairs={{0,2},{2,0},{1,3},{3,1},{4,6},{6,4},{5,7},{7,5},{8,10},{10,8},{9,1... | collective-permute-start | bytes 73736 | tf_op jit(solution)/shard_map/stats_sides/ppermute | solution.py:30
  58.7 0.0 collective-permute-done.8
  58.7 0.1 pad_maximum_fusion.3.memory
  58.7 0.0 copy-done
  58.7 0.0 copy-done.1
  58.7 2.5 %track_core.1 = (bf16[128,1024]{1,0:T(8,128)(2,1)}, bf16[8,128,256]{2,1,0:T(8,128)(2,1)S(1)}) custom-call(bf16[128,1024]{1,0:T(8,128)(2,1)S(1)} %bitcast.59, bf16[128,1024]{1,0:T(8,128)(2,1)S(1)} %bitcast.60, bf16[8,128,256]{2,1,0:T(8,128)(2,1)S(1)} %pad_maximum_fusion.3.memory), custom_call_target="tpu_custom_call" | custom-call | tf_op jit(solution)/shard_map/track_core/pallas_call | solution.py:280
  61.2 0.0 collective-permute-done.5.theirs
  61.2 6.9 %time_grads.1 = (f32[128,1024]{1,0:T(8,128)S(1)}, bf16[128,1024]{1,0:T(8,128)(2,1)S(1)}, bf16[8,4,64,256]{3,2,1,0:T(8,128)(2,1)}) custom-call(s32[4]{0:T(128)S(1)} %pad_add_fusion.info, bf16[128,2048]{1,0:T(8,128)(2,1)S(1)} %pad_maximum_fusion.2.own, bf16[128,2048]{1,0:T(8,128)(2,1)S(1)} %collective-permute-done.2.other, ...), custom_call_target="tpu_custom_call" | custom-call | tf_op jit(solution)/shard_map/time_grads/pallas_call | solution.py:292
  68.1 4.6 %all-to-all-start.1 = ((bf16[8,4,64,256]{3,2,1,0:T(8,128)(2,1)}), bf16[8,4,64,256]{3,2,1,0:T(8,128)(2,1)S(1)}, u32[]{:S(2)}, u32[]{:S(2)}) async-start(bf16[8,4,64,256]{3,2,1,0:T(8,128)(2,1)} %get-tuple-element.20), calls=%async_computation.1 | async-start | bytes 2097152 | tf_op jit(solution)/shard_map/memory_grad_low/all_to_all | solution.py:316
  72.8 3.2 %collective-permute-start.14 = (bf16[4,128,256]{2,1,0:T(8,128)(2,1)S(1)}, bf16[4,128,256]{2,1,0:T(8,128)(2,1)S(1)}, u32[]{:S(2)}, u32[]{:S(2)}) collective-permute-start(bf16[4,128,256]{2,1,0:T(8,128)(2,1)S(1)} %split.21), channel_id=1, source_target_pairs={{0,64},{64,0},{128,192},{192,128},{256,320},{320,256},{384,448},{4... | collective-permute-start | bytes 786440 | tf_op jit(solution)/shard_map/track_scatter/ppermute | solution.py:258
  75.9 2.8 %collective-permute-start.9 = (bf16[128,1024]{1,0:T(8,128)(2,1)S(1)}, bf16[128,1024]{1,0:T(8,128)(2,1)S(1)}, u32[]{:S(2)}, u32[]{:S(2)}) collective-permute-start(bf16[128,1024]{1,0:T(8,128)(2,1)S(1)} %get-tuple-element.19), channel_id=1, source_target_pairs={{0,2},{2,0},{1,3},{3,1},{4,6},{6,4},{5,7},{7,5},{8,10},{10,8},{9,1... | collective-permute-start | bytes 786440 | tf_op jit(solution)/shard_map/query_grad_sides/ppermute | solution.py:30
  78.8 3.7 %collective-permute-done.14 = bf16[4,128,256]{2,1,0:T(8,128)(2,1)S(1)} collective-permute-done((bf16[4,128,256]{2,1,0:T(8,128)(2,1)S(1)}, bf16[4,128,256]{2,1,0:T(8,128)(2,1)S(1)}, u32[]{:S(2)}, u32[]{:S(2)}) %collective-permute-start.14) | collective-permute-done | bytes 262176 | tf_op jit(solution)/shard_map/track_scatter/ppermute | solution.py:258
  82.5 0.1 convert_add_fusion
  82.6 4.7 %collective-permute-start.15 = (bf16[2,128,256]{2,1,0:T(8,128)(2,1)S(1)}, bf16[2,128,256]{2,1,0:T(8,128)(2,1)S(1)}, u32[]{:S(2)}, u32[]{:S(2)}) collective-permute-start(bf16[2,128,256]{2,1,0:T(8,128)(2,1)S(1)} %split.37), channel_id=1, source_target_pairs={{0,128},{64,192},{128,0},{192,64},{256,384},{320,448},{384,256},{4... | collective-permute-start | bytes 393224 | tf_op jit(solution)/shard_map/track_scatter/ppermute | solution.py:258
  87.3 0.0 collective-permute-done.9
  87.3 0.1 add_convert_fusion
  87.4 3.1 %collective-permute-start.10 = (bf16[64,1024]{1,0:T(8,128)(2,1)S(1)}, bf16[64,1024]{1,0:T(8,128)(2,1)S(1)}, u32[]{:S(2)}, u32[]{:S(2)}) collective-permute-start(bf16[64,1024]{1,0:T(8,128)(2,1)S(1)} %slice.28), channel_id=1, source_target_pairs={{0,1},{1,0},{2,3},{3,2},{4,5},{5,4},{6,7},{7,6},{8,9},{9,8},{10,11... | collective-permute-start | bytes 393224 | tf_op jit(solution)/shard_map/query_grad_songs/ppermute | solution.py:30
  90.4 0.0 collective-permute-done.15
  90.5 4.5 %collective-permute-start.16 = (bf16[1,128,256]{2,1,0:T(8,128)(2,1)S(1)}, bf16[1,128,256]{2,1,0:T(8,128)(2,1)S(1)}, u32[]{:S(2)}, u32[]{:S(2)}) collective-permute-start(bf16[1,128,256]{2,1,0:T(8,128)(2,1)S(1)} %split.38), channel_id=1, source_target_pairs={{0,256},{64,320},{128,384},{192,448},{256,0},{320,64},{384,128},{4... | collective-permute-start | bytes 196616 | tf_op jit(solution)/shard_map/track_scatter/ppermute | solution.py:258
  95.0 0.0 collective-permute-done.10
  95.1 0.7 maximum_bitcast_fusion
  95.8 2.7 %all-to-all-done.1 = bf16[8,4,64,256]{3,2,1,0:T(8,128)(2,1)S(1)} async-done(((bf16[8,4,64,256]{3,2,1,0:T(8,128)(2,1)}), bf16[8,4,64,256]{3,2,1,0:T(8,128)(2,1)S(1)}, u32[]{:S(2)}, u32[]{:S(2)}) %all-to-all-start.1) | async-done | bytes 1048608 | tf_op jit(solution)/shard_map/memory_grad_low/all_to_all | solution.py:316
  98.5 0.2 convert_reduce_fusion
  98.7 0.7 collective-permute-start.11
  99.4 1.3 %collective-permute-start.12 = (bf16[2,64,256]{2,1,0:T(8,128)(2,1)S(1)}, bf16[2,64,256]{2,1,0:T(8,128)(2,1)S(1)}, u32[]{:S(2)}, u32[]{:S(2)}) collective-permute-start(bf16[2,64,256]{2,1,0:T(8,128)(2,1)S(1)} %get-tuple-element.36), channel_id=1, source_target_pairs={{44,0},{40,4},{36,8},{32,12},{60,16},{48,20},{52,24},{56,28},{45,1... | collective-permute-start | bytes 196616 | tf_op jit(solution)/shard_map/memory_grad_high/ppermute | solution.py:322
  100.7 3.1 %collective-permute-start.13 = (bf16[2,64,256]{2,1,0:T(8,128)(2,1)S(1)}, bf16[2,64,256]{2,1,0:T(8,128)(2,1)S(1)}, u32[]{:S(2)}, u32[]{:S(2)}) collective-permute-start(bf16[2,64,256]{2,1,0:T(8,128)(2,1)S(1)} %get-tuple-element.35), channel_id=1, source_target_pairs={{16,0},{20,4},{24,8},{28,12},{32,16},{36,20},{40,24},{44,28},{48,3... | collective-permute-start | bytes 196616 | tf_op jit(solution)/shard_map/memory_grad_high/ppermute | solution.py:322
  103.8 0.0 collective-permute-done.16
  103.8 0.6 fusion
  104.5 0.0 collective-permute-done.11
  104.5 21.5 %collective-permute-done.12 = bf16[2,64,256]{2,1,0:T(8,128)(2,1)S(1)} collective-permute-done((bf16[2,64,256]{2,1,0:T(8,128)(2,1)S(1)}, bf16[2,64,256]{2,1,0:T(8,128)(2,1)S(1)}, u32[]{:S(2)}, u32[]{:S(2)}) %collective-permute-start.12) | collective-permute-done | bytes 65568 | tf_op jit(solution)/shard_map/memory_grad_high/ppermute | solution.py:322
  126.0 0.0 collective-permute-done.13
  126.0 0.7 fusion.5
  (16 shorter events, 0.4 us)
Async XLA Ops:
  0.6 11.9 %collective-permute-start = (bf16[2,64,256]{2,1,0:T(8,128)(2,1)}, bf16[2,64,256]{2,1,0:T(8,128)(2,1)S(1)}, u32[]{:S(2)}, u32[]{:S(2)}) collective-permute-start(bf16[2,64,256]{2,1,0:T(8,128)(2,1)} %bitcast.68), channel_id=1, source_target_pairs={{0,48},{4,52},{8,56},{12,60},{1,49},{5,53},{9,57},{13,61},{2,50},{... | collective-permute-start | bytes 196616 | tf_op jit(solution)/shard_map/memory_high/ppermute | solution.py:240
  1.3 13.7 %collective-permute-start.4 = (bf16[2,64,256]{2,1,0:T(8,128)(2,1)}, bf16[2,64,256]{2,1,0:T(8,128)(2,1)S(1)}, u32[]{:S(2)}, u32[]{:S(2)}) collective-permute-start(bf16[2,64,256]{2,1,0:T(8,128)(2,1)} %bitcast.69), channel_id=1, source_target_pairs={{0,16},{4,20},{8,24},{12,28},{16,32},{20,36},{24,40},{28,44},{32,4... | collective-permute-start | bytes 196616 | tf_op jit(solution)/shard_map/memory_high/ppermute | solution.py:240
  10.1 4.9 %collective-permute-start.3 = (bf16[2,64,256]{2,1,0:T(8,128)(2,1)}, bf16[2,64,256]{2,1,0:T(8,128)(2,1)S(1)}, u32[]{:S(2)}, u32[]{:S(2)}) collective-permute-start(bf16[2,64,256]{2,1,0:T(8,128)(2,1)} %bitcast.70), channel_id=1, source_target_pairs={{0,44},{4,40},{8,36},{12,32},{16,60},{20,56},{24,52},{28,48},{1,45... | collective-permute-start | bytes 196616 | tf_op jit(solution)/shard_map/memory_high/ppermute | solution.py:240
  17.1 8.8 %copy-start.3 = (bf16[2,64,1,1024]{3,1,2,0:T(8,128)(2,1)S(1)}, bf16[2,64,1,1024]{3,1,2,0:T(8,128)(2,1)}, u32[]{:S(2)}) copy-start(bf16[2,64,1,1024]{3,1,2,0:T(8,128)(2,1)} %param.8) | copy-start | bytes 786436
  17.1 8.8 %copy-start.4 = (bf16[2,64,1,1024]{3,1,2,0:T(8,128)(2,1)S(1)}, bf16[2,64,1,1024]{3,1,2,0:T(8,128)(2,1)}, u32[]{:S(2)}) copy-start(bf16[2,64,1,1024]{3,1,2,0:T(8,128)(2,1)} %param.6) | copy-start | bytes 786436
  17.1 34.5 %all-to-all-start = ((bf16[8,4,64,256]{3,2,1,0:T(8,128)(2,1)}), bf16[8,4,64,256]{3,2,1,0:T(8,128)(2,1)S(1)}, u32[]{:S(2)}, u32[]{:S(2)}) async-start(bf16[8,4,64,256]{3,2,1,0:T(8,128)(2,1)} %bitcast.9), calls=%async_computation | async-start | bytes 2097152 | tf_op jit(solution)/shard_map/memory_low/all_to_all | solution.py:252
  25.9 2.0 %copy-start.2 = (bf16[2,64,1,256]{3,1,2,0:T(8,128)(2,1)S(1)}, bf16[2,64,1,256]{3,1,2,0:T(8,128)(2,1)}, u32[]{:S(2)}) copy-start(bf16[2,64,1,256]{3,1,2,0:T(8,128)(2,1)} %param.10) | copy-start | bytes 196612
  26.0 6.8 %collective-permute-start.1 = (bf16[64,2048]{1,0:T(8,128)(2,1)S(1)}, bf16[64,2048]{1,0:T(8,128)(2,1)S(1)}, u32[]{:S(2)}, u32[]{:S(2)}) collective-permute-start(bf16[64,2048]{1,0:T(8,128)(2,1)S(1)} %get-tuple-element.31), channel_id=1, source_target_pairs={{0,1},{1,0},{2,3},{3,2},{4,5},{5,4},{6,7},{7,6},{8,9},{9,8},{10,11... | collective-permute-start | bytes 786440 | tf_op jit(solution)/shard_map/query_songs/ppermute | solution.py:30
  28.0 7.2 %collective-permute-start.6 = (bf16[1,128,256]{2,1,0:T(8,128)(2,1)S(1)}, bf16[1,128,256]{2,1,0:T(8,128)(2,1)S(1)}, u32[]{:S(2)}, u32[]{:S(2)}) collective-permute-start(bf16[1,128,256]{2,1,0:T(8,128)(2,1)S(1)} %bitcast.62), channel_id=1, source_target_pairs={{0,256},{64,320},{128,384},{192,448},{256,0},{320,64},{384,128},{4... | collective-permute-start | bytes 196616 | tf_op jit(solution)/shard_map/track_gather/ppermute | solution.py:258
  32.8 14.6 %collective-permute-start.2 = (bf16[128,2048]{1,0:T(8,128)(2,1)S(1)}, bf16[128,2048]{1,0:T(8,128)(2,1)S(1)}, u32[]{:S(2)}, u32[]{:S(2)}) collective-permute-start(bf16[128,2048]{1,0:T(8,128)(2,1)S(1)} %pad_maximum_fusion.2.own), channel_id=1, source_target_pairs={{0,2},{2,0},{1,3},{3,1},{4,6},{6,4},{5,7},{7,5},{8,10},{10,8},{9,1... | collective-permute-start | bytes 1572872 | tf_op jit(solution)/shard_map/query_sides/ppermute | solution.py:30
  35.2 7.4 %collective-permute-start.7 = (bf16[2,128,256]{2,1,0:T(8,128)(2,1)S(1)}, bf16[2,128,256]{2,1,0:T(8,128)(2,1)S(1)}, u32[]{:S(2)}, u32[]{:S(2)}) collective-permute-start(bf16[2,128,256]{2,1,0:T(8,128)(2,1)S(1)} %pad_maximum_fusion.5), channel_id=1, source_target_pairs={{0,128},{64,192},{128,0},{192,64},{256,384},{320,448},{384,256},{4... | collective-permute-start | bytes 393224 | tf_op jit(solution)/shard_map/track_gather/ppermute | solution.py:258
  42.6 16.1 %collective-permute-start.8 = (bf16[4,128,256]{2,1,0:T(8,128)(2,1)S(1)}, bf16[4,128,256]{2,1,0:T(8,128)(2,1)S(1)}, u32[]{:S(2)}, u32[]{:S(2)}) collective-permute-start(bf16[4,128,256]{2,1,0:T(8,128)(2,1)S(1)} %pad_maximum_fusion.4), channel_id=1, source_target_pairs={{0,64},{64,0},{128,192},{192,128},{256,320},{320,256},{384,448},{4... | collective-permute-start | bytes 786440 | tf_op jit(solution)/shard_map/track_gather/ppermute | solution.py:258
  55.3 3.5 %copy-start = (bf16[2,64,1,1024]{3,1,2,0:T(8,128)(2,1)S(1)}, bf16[2,64,1,1024]{3,1,2,0:T(8,128)(2,1)}, u32[]{:S(2)}) copy-start(bf16[2,64,1,1024]{3,1,2,0:T(8,128)(2,1)} %param.9) | copy-start | bytes 786436
  55.3 3.5 %copy-start.1 = (bf16[2,64,1,1024]{3,1,2,0:T(8,128)(2,1)S(1)}, bf16[2,64,1,1024]{3,1,2,0:T(8,128)(2,1)}, u32[]{:S(2)}) copy-start(bf16[2,64,1,1024]{3,1,2,0:T(8,128)(2,1)} %param.11) | copy-start | bytes 786436
  55.3 6.0 %collective-permute-start.5 = (f32[3,8,256]{2,1,0:T(8,128)S(1)}, f32[3,8,256]{2,1,0:T(8,128)S(1)}, u32[]{:S(2)}, u32[]{:S(2)}) collective-permute-start(f32[3,8,256]{2,1,0:T(8,128)S(1)} %time_stats.1.mine), channel_id=1, source_target_pairs={{0,2},{2,0},{1,3},{3,1},{4,6},{6,4},{5,7},{7,5},{8,10},{10,8},{9,1... | collective-permute-start | bytes 73736 | tf_op jit(solution)/shard_map/stats_sides/ppermute | solution.py:30
  68.1 30.3 %all-to-all-start.1 = ((bf16[8,4,64,256]{3,2,1,0:T(8,128)(2,1)}), bf16[8,4,64,256]{3,2,1,0:T(8,128)(2,1)S(1)}, u32[]{:S(2)}, u32[]{:S(2)}) async-start(bf16[8,4,64,256]{3,2,1,0:T(8,128)(2,1)} %get-tuple-element.20), calls=%async_computation.1 | async-start | bytes 2097152 | tf_op jit(solution)/shard_map/memory_grad_low/all_to_all | solution.py:316
  72.8 9.8 %collective-permute-start.14 = (bf16[4,128,256]{2,1,0:T(8,128)(2,1)S(1)}, bf16[4,128,256]{2,1,0:T(8,128)(2,1)S(1)}, u32[]{:S(2)}, u32[]{:S(2)}) collective-permute-start(bf16[4,128,256]{2,1,0:T(8,128)(2,1)S(1)} %split.21), channel_id=1, source_target_pairs={{0,64},{64,0},{128,192},{192,128},{256,320},{320,256},{384,448},{4... | collective-permute-start | bytes 786440 | tf_op jit(solution)/shard_map/track_scatter/ppermute | solution.py:258
  75.9 11.4 %collective-permute-start.9 = (bf16[128,1024]{1,0:T(8,128)(2,1)S(1)}, bf16[128,1024]{1,0:T(8,128)(2,1)S(1)}, u32[]{:S(2)}, u32[]{:S(2)}) collective-permute-start(bf16[128,1024]{1,0:T(8,128)(2,1)S(1)} %get-tuple-element.19), channel_id=1, source_target_pairs={{0,2},{2,0},{1,3},{3,1},{4,6},{6,4},{5,7},{7,5},{8,10},{10,8},{9,1... | collective-permute-start | bytes 786440 | tf_op jit(solution)/shard_map/query_grad_sides/ppermute | solution.py:30
  82.6 7.8 %collective-permute-start.15 = (bf16[2,128,256]{2,1,0:T(8,128)(2,1)S(1)}, bf16[2,128,256]{2,1,0:T(8,128)(2,1)S(1)}, u32[]{:S(2)}, u32[]{:S(2)}) collective-permute-start(bf16[2,128,256]{2,1,0:T(8,128)(2,1)S(1)} %split.37), channel_id=1, source_target_pairs={{0,128},{64,192},{128,0},{192,64},{256,384},{320,448},{384,256},{4... | collective-permute-start | bytes 393224 | tf_op jit(solution)/shard_map/track_scatter/ppermute | solution.py:258
  87.4 7.7 %collective-permute-start.10 = (bf16[64,1024]{1,0:T(8,128)(2,1)S(1)}, bf16[64,1024]{1,0:T(8,128)(2,1)S(1)}, u32[]{:S(2)}, u32[]{:S(2)}) collective-permute-start(bf16[64,1024]{1,0:T(8,128)(2,1)S(1)} %slice.28), channel_id=1, source_target_pairs={{0,1},{1,0},{2,3},{3,2},{4,5},{5,4},{6,7},{7,6},{8,9},{9,8},{10,11... | collective-permute-start | bytes 393224 | tf_op jit(solution)/shard_map/query_grad_songs/ppermute | solution.py:30
  90.5 13.3 %collective-permute-start.16 = (bf16[1,128,256]{2,1,0:T(8,128)(2,1)S(1)}, bf16[1,128,256]{2,1,0:T(8,128)(2,1)S(1)}, u32[]{:S(2)}, u32[]{:S(2)}) collective-permute-start(bf16[1,128,256]{2,1,0:T(8,128)(2,1)S(1)} %split.38), channel_id=1, source_target_pairs={{0,256},{64,320},{128,384},{192,448},{256,0},{320,64},{384,128},{4... | collective-permute-start | bytes 196616 | tf_op jit(solution)/shard_map/track_scatter/ppermute | solution.py:258
  98.7 5.8 %collective-permute-start.11 = (bf16[2,64,256]{2,1,0:T(8,128)(2,1)S(1)}, bf16[2,64,256]{2,1,0:T(8,128)(2,1)S(1)}, u32[]{:S(2)}, u32[]{:S(2)}) collective-permute-start(bf16[2,64,256]{2,1,0:T(8,128)(2,1)S(1)} %get-tuple-element.34), channel_id=1, source_target_pairs={{48,0},{52,4},{56,8},{60,12},{49,1},{53,5},{57,9},{61,13},{50,2},{... | collective-permute-start | bytes 196616 | tf_op jit(solution)/shard_map/memory_grad_high/ppermute | solution.py:322
  99.4 26.6 %collective-permute-start.12 = (bf16[2,64,256]{2,1,0:T(8,128)(2,1)S(1)}, bf16[2,64,256]{2,1,0:T(8,128)(2,1)S(1)}, u32[]{:S(2)}, u32[]{:S(2)}) collective-permute-start(bf16[2,64,256]{2,1,0:T(8,128)(2,1)S(1)} %get-tuple-element.36), channel_id=1, source_target_pairs={{44,0},{40,4},{36,8},{32,12},{60,16},{48,20},{52,24},{56,28},{45,1... | collective-permute-start | bytes 196616 | tf_op jit(solution)/shard_map/memory_grad_high/ppermute | solution.py:322
  100.7 25.3 %collective-permute-start.13 = (bf16[2,64,256]{2,1,0:T(8,128)(2,1)S(1)}, bf16[2,64,256]{2,1,0:T(8,128)(2,1)S(1)}, u32[]{:S(2)}, u32[]{:S(2)}) collective-permute-start(bf16[2,64,256]{2,1,0:T(8,128)(2,1)S(1)} %get-tuple-element.35), channel_id=1, source_target_pairs={{16,0},{20,4},{24,8},{28,12},{32,16},{36,20},{40,24},{44,28},{48,3... | collective-permute-start | bytes 196616 | tf_op jit(solution)/shard_map/memory_grad_high/ppermute | solution.py:322
